TPU v7x, 32 devices: a whole 2x2x4 slice. The times are simulated.
32 devices in a mesh: dp: 8 (over y, x, core), ctx: 4 (over z).
Axes of the slice: x: 2, y: 2, z: 4, core: 2. Of those that a mesh axis runs over, the one named last changes fastest.
Arguments:
- tokens: bfloat16 [64, 512, 1024], P('dp', 'ctx'), may hold values from -6 to 6
- lengths: int32 [64], P('dp'), may hold values from 128 to 512, as said below
- cotangent: bfloat16 [64, 512, 1024], P('dp', 'ctx'), may hold values from -6 to 6
- weight_query: bfloat16 [1024, 1024], P('dp', 'ctx'), may hold values from -0.1875 to 0.1875
- weight_key: bfloat16 [1024, 1024], P('dp', 'ctx'), may hold values from -0.1875 to 0.1875
- weight_value: bfloat16 [1024, 1024], P('dp', 'ctx'), may hold values from -0.1875 to 0.1875
- weight_out: bfloat16 [1024, 1024], P('dp', 'ctx'), may hold values from -0.75 to 0.75
- weight_inner: bfloat16 [1024, 4096], P('dp', 'ctx'), may hold values from -0.1875 to 0.1875
- weight_outer: bfloat16 [4096, 1024], P('dp', 'ctx'), may hold values from -0.09375 to 0.09375
- bias_query: float32 [1024], replicated, may hold values from -3 to 3
- bias_value: float32 [1024], replicated, may hold values from -3 to 3
- bias_out: float32 [1024], replicated, may hold values from -3 to 3
- bias_inner: float32 [4096], replicated, may hold values from -3 to 3
- bias_outer: float32 [1024], replicated, may hold values from -3 to 3
- gain_attn: float32 [1024], replicated, may hold values from 0.25 to 1.75
- shift_attn: float32 [1024], replicated, may hold values from -3 to 3
- gain_ffn: float32 [1024], replicated, may hold values from 0.25 to 1.75
- shift_ffn: float32 [1024], replicated, may hold values from -3 to 3
Outputs:
- mixed: bfloat16 [64, 512, 1024], P('dp', 'ctx')
- grad_tokens: float32 [64, 512, 1024], P('dp', 'ctx')
- grad_weight_query: float32 [1024, 1024], P('dp', 'ctx')
- grad_weight_key: float32 [1024, 1024], P('dp', 'ctx')
- grad_weight_value: float32 [1024, 1024], P('dp', 'ctx')
- grad_weight_out: float32 [1024, 1024], P('dp', 'ctx')
- grad_weight_inner: float32 [1024, 4096], P('dp', 'ctx')
- grad_weight_outer: float32 [4096, 1024], P('dp', 'ctx')
- grad_bias_query: float32 [1024], replicated
- grad_bias_value: float32 [1024], replicated
- grad_bias_out: float32 [1024], replicated
- grad_bias_inner: float32 [4096], replicated
- grad_bias_outer: float32 [1024], replicated
- grad_gain_attn: float32 [1024], replicated
- grad_shift_attn: float32 [1024], replicated
- grad_gain_ffn: float32 [1024], replicated
- grad_shift_ffn: float32 [1024], replicated
Inputs may be any that keep to these rules, and one draw needn't show every extreme that they name: `lengths`: valid slots of each sequence; among the 8 sequences of each index of dp, one has all 512 slots valid.
All inputs are finite; a program needn't handle non-finite values.
Results may differ from a plain program's by a relative error of at most 0.012.
Values may be sent and summed in bfloat16 or wider, within the bound.
No kernel may reach another device: no remote copies, remote signals or barrier semaphores. Data moves between devices by JAX's collectives and lax.ppermute only.
A program may use at most 256 MiB of HBM per device.

v0:
```python
import jax
import jax.numpy as jnp
from jax import lax
from jax.sharding import PartitionSpec as P

HEADS = 16
HEAD_DIM = 64
MICRO = 2


epsilon = 1e-05
masked_score = -1000000000.0
score_scale = 0.125


def layer_norm(summed, norm_gain, norm_shift):
    centred = summed - jnp.mean(summed, axis=-1, keepdims=True)
    spread = jnp.mean(centred * centred, axis=-1, keepdims=True)
    return centred * lax.rsqrt(spread + epsilon) * norm_gain + norm_shift


def gelu_exact(inner):
    return jax.nn.gelu(inner, approximate=False)


def fetch_weights(w_query, w_key, w_value, w_out, w_inner, w_outer):
    widened = (
        lax.all_gather(w_query, "ctx", axis=1, tiled=True),
        lax.all_gather(w_key, "ctx", axis=1, tiled=True),
        lax.all_gather(w_value, "ctx", axis=1, tiled=True),
        lax.all_gather(w_out, "ctx", axis=1, tiled=True),
        lax.all_gather(w_inner, "ctx", axis=1, tiled=True),
        lax.all_gather(w_outer, "ctx", axis=1, tiled=True),
    )
    return (
        lax.all_gather(widened[0], "dp", axis=0, tiled=True),
        lax.all_gather(widened[1], "dp", axis=0, tiled=True),
        lax.all_gather(widened[2], "dp", axis=0, tiled=True),
        lax.all_gather(widened[3], "dp", axis=0, tiled=True),
        lax.all_gather(widened[4], "dp", axis=0, tiled=True),
        lax.all_gather(widened[5], "dp", axis=0, tiled=True),
    )


def masked_scores(query_heads, key_heads, key_valid):
    scores = (
        jnp.einsum("schd,slhd->shcl", query_heads, key_heads, preferred_element_type=jnp.float32)
        * score_scale
    )
    return jnp.where(key_valid, scores, masked_score)


def forward_local(weights, vectors, block, seq_lengths):
    w_query, w_key, w_value, w_out, w_inner, w_outer = weights
    b_query, b_value, b_out, b_inner, b_outer, gain_one, shift_one, gain_two, shift_two = vectors
    seq_count, slot_count, width = block.shape
    in_rows = block.reshape(seq_count * slot_count, width)
    query_low = (jnp.dot(in_rows, w_query, preferred_element_type=jnp.float32) + b_query).astype(
        jnp.bfloat16
    )
    key_low = jnp.dot(in_rows, w_key, preferred_element_type=jnp.float32).astype(jnp.bfloat16)
    value_low = (jnp.dot(in_rows, w_value, preferred_element_type=jnp.float32) + b_value).astype(
        jnp.bfloat16
    )
    key_local = key_low.reshape(seq_count, slot_count, width)
    value_local = value_low.reshape(seq_count, slot_count, width)
    key_full, value_full = (
        lax.all_gather(key_local, "ctx", axis=1, tiled=True),
        lax.all_gather(value_local, "ctx", axis=1, tiled=True),
    )
    key_count = key_full.shape[1]
    query_heads = query_low.reshape(seq_count, slot_count, HEADS, HEAD_DIM)
    key_heads = key_full.reshape(seq_count, key_count, HEADS, HEAD_DIM)
    value_heads = value_full.reshape(seq_count, key_count, HEADS, HEAD_DIM)
    key_valid = (jnp.arange(key_count)[None, :] < seq_lengths[:, None])[:, None, None, :]
    scores = masked_scores(query_heads, key_heads, key_valid)
    top_score = jnp.max(scores, axis=-1, keepdims=True)
    log_total = top_score + jnp.log(jnp.sum(jnp.exp(scores - top_score), axis=-1, keepdims=True))
    probs_low = jnp.exp(scores - log_total).astype(jnp.bfloat16)
    heads_out = jnp.einsum(
        "shcl,slhd->schd", probs_low, value_heads, preferred_element_type=jnp.float32
    )
    heads_low = heads_out.reshape(seq_count * slot_count, width).astype(jnp.bfloat16)
    attended = jnp.dot(heads_low, w_out, preferred_element_type=jnp.float32) + b_out
    summed_one = in_rows.astype(jnp.float32) + attended
    hidden_one = layer_norm(summed_one, gain_one, shift_one)
    hidden_low = hidden_one.astype(jnp.bfloat16)
    inner = jnp.dot(hidden_low, w_inner, preferred_element_type=jnp.float32) + b_inner
    active_low = gelu_exact(inner).astype(jnp.bfloat16)
    outer = jnp.dot(active_low, w_outer, preferred_element_type=jnp.float32) + b_outer
    summed_two = hidden_one + outer
    output = layer_norm(summed_two, gain_two, shift_two)
    kept = (
        in_rows,
        query_heads,
        key_heads,
        value_heads,
        key_valid,
        log_total,
        heads_low,
        summed_one,
        hidden_low,
        inner,
        active_low,
        summed_two,
    )
    return (output, kept)


def backward_local(weights, vectors, kept, grad_out):
    w_query, w_key, w_value, w_out, w_inner, w_outer = weights
    b_query, b_value, b_out, b_inner, b_outer, gain_one, shift_one, gain_two, shift_two = vectors
    (
        in_rows,
        query_heads,
        key_heads,
        value_heads,
        key_valid,
        log_total,
        heads_low,
        summed_one,
        hidden_low,
        inner,
        active_low,
        summed_two,
    ) = kept
    seq_count, slot_count = (query_heads.shape[0], query_heads.shape[1])
    key_count = key_heads.shape[1]
    row_count, width = in_rows.shape
    unused_two, pull_two = jax.vjp(layer_norm, summed_two, gain_two, shift_two)
    grad_sum_two, grad_gain_two, grad_shift_two = pull_two(grad_out)
    outer_low = grad_sum_two.astype(jnp.bfloat16)
    grad_b_outer = jnp.sum(outer_low.astype(jnp.float32), axis=0)
    grad_w_outer = jnp.einsum(
        "nf,nd->fd", active_low, outer_low, preferred_element_type=jnp.float32
    )
    grad_active = jnp.einsum("nd,fd->nf", outer_low, w_outer, preferred_element_type=jnp.float32)
    unused_gelu, pull_gelu = jax.vjp(gelu_exact, inner)
    inner_low = pull_gelu(grad_active)[0].astype(jnp.bfloat16)
    grad_b_inner = jnp.sum(inner_low.astype(jnp.float32), axis=0)
    grad_w_inner = jnp.einsum(
        "nd,nf->df", hidden_low, inner_low, preferred_element_type=jnp.float32
    )
    grad_hidden = (
        jnp.einsum("nf,df->nd", inner_low, w_inner, preferred_element_type=jnp.float32)
        + grad_sum_two
    )
    unused_one, pull_one = jax.vjp(layer_norm, summed_one, gain_one, shift_one)
    grad_sum_one, grad_gain_one, grad_shift_one = pull_one(grad_hidden)
    attend_low = grad_sum_one.astype(jnp.bfloat16)
    grad_b_out = jnp.sum(attend_low.astype(jnp.float32), axis=0)
    grad_w_out = jnp.einsum("nd,ne->de", heads_low, attend_low, preferred_element_type=jnp.float32)
    grad_heads = jnp.einsum("ne,de->nd", attend_low, w_out, preferred_element_type=jnp.float32)
    grad_heads = grad_heads.astype(jnp.bfloat16).reshape(seq_count, slot_count, HEADS, HEAD_DIM)
    scores = masked_scores(query_heads, key_heads, key_valid)
    probs = jnp.exp(scores - log_total)
    probs_low = probs.astype(jnp.bfloat16)
    grad_probs = jnp.einsum(
        "schd,slhd->shcl", grad_heads, value_heads, preferred_element_type=jnp.float32
    )
    inner_sum = jnp.sum(probs * grad_probs, axis=-1, keepdims=True)
    score_low = (probs * (grad_probs - inner_sum)).astype(jnp.bfloat16)
    query_grad = (
        jnp.einsum("shcl,slhd->schd", score_low, key_heads, preferred_element_type=jnp.float32)
        * score_scale
    )
    query_grad_low = query_grad.astype(jnp.bfloat16).reshape(row_count, width)
    key_part = (
        jnp.einsum("shcl,schd->slhd", score_low, query_heads, preferred_element_type=jnp.float32)
        * score_scale
    )
    value_part = jnp.einsum(
        "shcl,schd->slhd", probs_low, grad_heads, preferred_element_type=jnp.float32
    )
    key_part = key_part.reshape(seq_count, key_count, width)
    value_part = value_part.reshape(seq_count, key_count, width)
    key_sum, value_sum = (
        lax.psum_scatter(key_part, "ctx", scatter_dimension=1, tiled=True),
        lax.psum_scatter(value_part, "ctx", scatter_dimension=1, tiled=True),
    )
    key_grad_low = key_sum.reshape(row_count, width).astype(jnp.bfloat16)
    value_grad_low = value_sum.reshape(row_count, width).astype(jnp.bfloat16)
    grad_w_query = jnp.einsum(
        "nd,ne->de", in_rows, query_grad_low, preferred_element_type=jnp.float32
    )
    grad_w_key = jnp.einsum("nd,ne->de", in_rows, key_grad_low, preferred_element_type=jnp.float32)
    grad_w_value = jnp.einsum(
        "nd,ne->de", in_rows, value_grad_low, preferred_element_type=jnp.float32
    )
    grad_b_query = jnp.sum(query_grad_low.astype(jnp.float32), axis=0)
    grad_b_value = jnp.sum(value_grad_low.astype(jnp.float32), axis=0)
    grad_rows = grad_sum_one + jnp.einsum(
        "ne,de->nd", query_grad_low, w_query, preferred_element_type=jnp.float32
    )
    grad_rows = grad_rows + jnp.einsum(
        "ne,de->nd", key_grad_low, w_key, preferred_element_type=jnp.float32
    )
    grad_rows = grad_rows + jnp.einsum(
        "ne,de->nd", value_grad_low, w_value, preferred_element_type=jnp.float32
    )
    matrix_grads = (grad_w_query, grad_w_key, grad_w_value, grad_w_out, grad_w_inner, grad_w_outer)
    vector_grads = (
        grad_b_query,
        grad_b_value,
        grad_b_out,
        grad_b_inner,
        grad_b_outer,
        grad_gain_one,
        grad_shift_one,
        grad_gain_two,
        grad_shift_two,
    )
    return (grad_rows, matrix_grads, vector_grads)


def accumulate(running, addend):
    if running is None:
        return addend
    return jax.tree.map(jnp.add, running, addend)


def on_device(
    tokens,
    lengths,
    cotangent,
    weight_query,
    weight_key,
    weight_value,
    weight_out,
    weight_inner,
    weight_outer,
    bias_query,
    bias_value,
    bias_out,
    bias_inner,
    bias_outer,
    gain_attn,
    shift_attn,
    gain_ffn,
    shift_ffn,
):
    vectors = (
        bias_query,
        bias_value,
        bias_out,
        bias_inner,
        bias_outer,
        gain_attn,
        shift_attn,
        gain_ffn,
        shift_ffn,
    )
    seq_total, slot_count, width = tokens.shape
    placed = lax.axis_index("ctx") * slot_count + jnp.arange(slot_count)
    per_micro = seq_total // MICRO
    row_valid = (placed[None, :] < lengths[:, None]).astype(jnp.float32)
    grad_all = cotangent.astype(jnp.float32) * row_valid[:, :, None]
    outputs = []
    input_grads = []
    matrix_sums = None
    vector_sums = None
    for micro_index in range(MICRO):
        low_end = micro_index * per_micro
        weights = fetch_weights(
            weight_query, weight_key, weight_value, weight_out, weight_inner, weight_outer
        )
        output, kept = forward_local(
            weights,
            vectors,
            tokens[low_end : low_end + per_micro],
            lengths[low_end : low_end + per_micro],
        )
        outputs.append(output)
    for micro_index in range(MICRO):
        low_end = micro_index * per_micro
        weights = fetch_weights(
            weight_query, weight_key, weight_value, weight_out, weight_inner, weight_outer
        )
        output, kept = forward_local(
            weights,
            vectors,
            tokens[low_end : low_end + per_micro],
            lengths[low_end : low_end + per_micro],
        )
        grad_block = grad_all[low_end : low_end + per_micro].reshape(per_micro * slot_count, width)
        grad_rows, matrix_grads, vector_grads = backward_local(weights, vectors, kept, grad_block)
        input_grads.append(grad_rows)
        matrix_sums = accumulate(matrix_sums, matrix_grads)
        vector_sums = accumulate(vector_sums, vector_grads)
    partial_sums = (
        lax.psum_scatter(matrix_sums[0], "dp", scatter_dimension=0, tiled=True),
        lax.psum_scatter(matrix_sums[1], "dp", scatter_dimension=0, tiled=True),
        lax.psum_scatter(matrix_sums[2], "dp", scatter_dimension=0, tiled=True),
        lax.psum_scatter(matrix_sums[3], "dp", scatter_dimension=0, tiled=True),
        lax.psum_scatter(matrix_sums[4], "dp", scatter_dimension=0, tiled=True),
        lax.psum_scatter(matrix_sums[5], "dp", scatter_dimension=0, tiled=True),
    )
    final_sums = (
        lax.psum_scatter(partial_sums[0], "ctx", scatter_dimension=1, tiled=True),
        lax.psum_scatter(partial_sums[1], "ctx", scatter_dimension=1, tiled=True),
        lax.psum_scatter(partial_sums[2], "ctx", scatter_dimension=1, tiled=True),
        lax.psum_scatter(partial_sums[3], "ctx", scatter_dimension=1, tiled=True),
        lax.psum_scatter(partial_sums[4], "ctx", scatter_dimension=1, tiled=True),
        lax.psum_scatter(partial_sums[5], "ctx", scatter_dimension=1, tiled=True),
    )
    vector_totals = lax.psum(
        (
            vector_sums[0],
            vector_sums[1],
            vector_sums[2],
            vector_sums[3],
            vector_sums[4],
            vector_sums[5],
            vector_sums[6],
            vector_sums[7],
            vector_sums[8],
        ),
        ("dp", "ctx"),
    )
    mixed = (
        jnp.concatenate(outputs, axis=0).reshape(seq_total, slot_count, width).astype(jnp.bfloat16)
    )
    grad_tokens = jnp.concatenate(input_grads, axis=0).reshape(seq_total, slot_count, width)
    return (
        mixed,
        grad_tokens,
        final_sums[0],
        final_sums[1],
        final_sums[2],
        final_sums[3],
        final_sums[4],
        final_sums[5],
        vector_totals[0],
        vector_totals[1],
        vector_totals[2],
        vector_totals[3],
        vector_totals[4],
        vector_totals[5],
        vector_totals[6],
        vector_totals[7],
        vector_totals[8],
    )


def solution(mesh):
    in_specs = (
        P("dp", "ctx", None),
        P("dp"),
        P("dp", "ctx", None),
        P("dp", "ctx"),
        P("dp", "ctx"),
        P("dp", "ctx"),
        P("dp", "ctx"),
        P("dp", "ctx"),
        P("dp", "ctx"),
        P(),
        P(),
        P(),
        P(),
        P(),
        P(),
        P(),
        P(),
        P(),
    )
    out_specs = (
        P("dp", "ctx", None),
        P("dp", "ctx", None),
        P("dp", "ctx"),
        P("dp", "ctx"),
        P("dp", "ctx"),
        P("dp", "ctx"),
        P("dp", "ctx"),
        P("dp", "ctx"),
        P(),
        P(),
        P(),
        P(),
        P(),
        P(),
        P(),
        P(),
        P(),
    )
    return jax.shard_map(
        on_device, mesh=mesh, in_specs=in_specs, out_specs=out_specs, check_vma=False
    )
```

profile of v0, /device:TPU:0, one launch (start us, length us, event | category | flops | bytes accessed | tf_op | source)
XLA Modules:
  0.0 1989.3 jit_solution(1128901141570793963)
XLA Ops:
  7.2 17.5 all_gather.37
  63.0 19.6 all-gather.13.cloned.1.call-done
  86.5 16.3 all_gather.40
  120.0 25.4 %all-gather.29.cloned.1.call-done = bf16[512,1024]{1,0:T(8,128)(2,1)} async-done(((bf16[512,256]{1,0:T(8,128)(2,1)}), bf16[512,1024]{1,0:T(8,128)(2,1)}) %all-gather.29.cloned.1.call-update) | async-done | bytes 1048592 | tf_op jit(solution)/shard_map/all_gather | solution.py:33
  145.5 27.9 %all-gather.17.cloned.1.call-done = bf16[1024,1024]{1,0:T(8,128)(2,1)} async-done(((bf16[128,1024]{1,0:T(8,128)(2,1)}), bf16[1024,1024]{1,0:T(8,128)(2,1)}) %all-gather.17.cloned.1.call-update) | async-done | bytes 2097168 | tf_op jit(solution)/shard_map/all_gather | solution.py:36
  193.2 62.4 %all-gather.21.cloned.1.call-done = bf16[4,512,1024]{2,1,0:T(8,128)(2,1)} async-done(((bf16[4,128,1024]{2,1,0:T(8,128)(2,1)}), bf16[4,512,1024]{2,1,0:T(8,128)(2,1)}) %all-gather.21.cloned.1.call-update) | async-done | bytes 4194320 | tf_op jit(solution)/shard_map/all_gather | solution.py:68
  272.6 63.9 %all-gather.15.cloned.1.call-done = bf16[4,512,1024]{2,1,0:T(8,128)(2,1)} async-done(((bf16[4,128,1024]{2,1,0:T(8,128)(2,1)}), bf16[4,512,1024]{2,1,0:T(8,128)(2,1)}) %all-gather.15.cloned.1.call-update) | async-done | bytes 4194320 | tf_op jit(solution)/shard_map/all_gather | solution.py:69
  369.8 77.4 %all-gather.35.cloned.1.call-done = bf16[4,512,1024]{2,1,0:T(8,128)(2,1)} async-done(((bf16[4,128,1024]{2,1,0:T(8,128)(2,1)}), bf16[4,512,1024]{2,1,0:T(8,128)(2,1)}) %all-gather.35.cloned.1.call-update) | async-done | bytes 4194320 | tf_op jit(solution)/shard_map/all_gather | solution.py:68
  464.4 63.6 %all-gather.33.cloned.1.call-done = bf16[4,512,1024]{2,1,0:T(8,128)(2,1)} async-done(((bf16[4,128,1024]{2,1,0:T(8,128)(2,1)}), bf16[4,512,1024]{2,1,0:T(8,128)(2,1)}) %all-gather.33.cloned.1.call-update) | async-done | bytes 4194320 | tf_op jit(solution)/shard_map/all_gather | solution.py:69
  547.2 35.6 %all-gather.27.cloned.1.call-done = bf16[1024,4096]{1,0:T(8,128)(2,1)} async-done(((bf16[128,4096]{1,0:T(8,128)(2,1)}), bf16[1024,4096]{1,0:T(8,128)(2,1)}) %all-gather.27.cloned.1.call-update) | async-done | bytes 8388624 | tf_op jit(solution)/shard_map/all_gather | solution.py:40
  594.0 49.1 %multiply_convert_fusion.3 = (bf16[512,4096]{1,0:T(8,128)(2,1)}, f32[512,4096]{1,0:T(8,128)}, bf16[512,4096]{1,0:T(8,128)(2,1)}, f32[512,4096]{1,0:T(8,128)}, f32[512,4096]{1,0:T(8,128)}) fusion(f32[4096]{0:T(1024)S(1)} %copy-done.109, f32[512,4096]{1,0:T(8,128)S(1)} %fusion.71, bf16[1024,4096]{1,0:T(8,128)(2,1)S(1)} %copy-done.105, ...), kind=kOutput, calls=%fused_computation.35 | convolution fusion | flops 4574412800 | bytes 52457472 | tf_op jit(solution)/shard_map/dot_general | solution.py:88
  673.6 27.1 %convert_reduce_fusion.1 = (f32[4096]{0:T(1024)}, bf16[512,4096]{1,0:T(8,128)(2,1)}, f32[4096]{0:T(1024)}, bf16[512,4096]{1,0:T(8,128)(2,1)}) fusion(f32[512,4096]{1,0:T(8,128)} %get-tuple-element.97, f32[512,4096]{1,0:T(8,128)} %get-tuple-element.130, f32[4096]{0:T(1024)S(1)} %copy-done.109, f32[512,4096]{1,0:T(8,128)} %fusion.90, ...), kind=kOutput, calls=%fused_computation.19 | convolution fusion | flops 4366262272 | bytes 59817984 | tf_op jit(solution)/shard_map/nd,fd->nf/dot_general | solution.py:137
  900.3 145.6 %reduce-scatter.23.cloned.1.call-done = f32[4,128,1024]{2,1,0:T(8,128)} async-done(((f32[4,512,1024]{2,1,0:T(8,128)}), f32[4,128,1024]{2,1,0:T(8,128)}) %reduce-scatter.23.cloned.1.call-update) | async-done | bytes 2097168 | tf_op jit(solution)/shard_map/reduce_scatter | solution.py:179
  1052.9 140.4 %reduce-scatter.21.cloned.1.call-done = f32[4,128,1024]{2,1,0:T(8,128)} async-done(((f32[4,512,1024]{2,1,0:T(8,128)}), f32[4,128,1024]{2,1,0:T(8,128)}) %reduce-scatter.21.cloned.1.call-update) | async-done | bytes 2097168 | tf_op jit(solution)/shard_map/reduce_scatter | solution.py:178
  1196.1 144.7 %reduce-scatter.17.cloned.1.call-done = f32[4,128,1024]{2,1,0:T(8,128)} async-done(((f32[4,512,1024]{2,1,0:T(8,128)}), f32[4,128,1024]{2,1,0:T(8,128)}) %reduce-scatter.17.cloned.1.call-update) | async-done | bytes 2097168 | tf_op jit(solution)/shard_map/reduce_scatter | solution.py:178
  1406.5 45.1 %reduce-scatter.33.cloned.1.call-done = f32[128,1024]{0,1:T(8,128)} async-done(((f32[1024,1024]{0,1:T(8,128)}), f32[128,1024]{0,1:T(8,128)}) %reduce-scatter.33.cloned.1.call-update) | async-done | bytes 524304 | tf_op jit(solution)/shard_map/reduce_scatter | solution.py:293
  1451.7 54.6 %reduce-scatter.29.cloned.1.call-done = f32[128,1024]{0,1:T(8,128)} async-done(((f32[1024,1024]{0,1:T(8,128)}), f32[128,1024]{0,1:T(8,128)}) %reduce-scatter.29.cloned.1.call-update) | async-done | bytes 524304 | tf_op jit(solution)/shard_map/reduce_scatter | solution.py:292
  1506.4 54.9 %reduce-scatter.37.cloned.1.call-done = f32[128,1024]{1,0:T(8,128)} async-done(((f32[1024,1024]{1,0:T(8,128)}), f32[128,1024]{1,0:T(8,128)}) %reduce-scatter.37.cloned.1.call-update) | async-done | bytes 524304 | tf_op jit(solution)/shard_map/reduce_scatter | solution.py:294
  1561.3 119.5 %reduce-scatter.41.cloned.1.call-done = f32[128,4096]{1,0:T(8,128)} async-done(((f32[1024,4096]{1,0:T(8,128)}), f32[128,4096]{1,0:T(8,128)}) %reduce-scatter.41.cloned.1.call-update) | async-done | bytes 2097168 | tf_op jit(solution)/shard_map/reduce_scatter | solution.py:295
  1680.8 119.5 %reduce-scatter.45.cloned.1.call-done = f32[512,1024]{1,0:T(8,128)} async-done(((f32[4096,1024]{1,0:T(8,128)}), f32[512,1024]{1,0:T(8,128)}) %reduce-scatter.45.cloned.1.call-update) | async-done | bytes 2097168 | tf_op jit(solution)/shard_map/reduce_scatter | solution.py:296
  1808.8 15.5 reduce-scatter.27.cloned.1.call-done
  1825.9 40.2 %all-reduce = (f32[1024]{0:T(1024)}, f32[1024]{0:T(1024)}, f32[1024]{0:T(1024)}, f32[4096]{0:T(1024)}, f32[1024]{0:T(1024)}, /*index=5*/f32[1024]{0:T(1024)}, f32[1024]{0:T(1024)}, f32[1024]{0:T(1024)}, f32[1024]{0:T(1024)}) all-reduce(f32[1024]{0:T(1024)S(1)} %add.418, ...), channel_id=1, replica_groups=mesh['dp'=8,'ctx'=4] {'dp','ctx'}, use_global_device_ids=true, to_apply=%region_40.41 | all-reduce | flops 12288 | bytes 98304 | tf_op jit(solution)/shard_map/psum | solution.py:306
  1891.2 44.8 %reduce-scatter.43.cloned.1.call-done = f32[128,1024]{1,0:T(8,128)} async-done(((f32[128,4096]{1,0:T(8,128)}), f32[128,1024]{1,0:T(8,128)}) %reduce-scatter.43.cloned.1.call-update) | async-done | bytes 524304 | tf_op jit(solution)/shard_map/reduce_scatter | solution.py:303
  1936.0 46.2 %reduce-scatter.47.cloned.1.call-done = f32[512,256]{1,0:T(8,128)} async-done(((f32[512,1024]{1,0:T(8,128)}), f32[512,256]{1,0:T(8,128)}) %reduce-scatter.47.cloned.1.call-update) | async-done | bytes 524304 | tf_op jit(solution)/shard_map/reduce_scatter | solution.py:304
  (420 shorter events, 516.2 us)
Async XLA Ops:
  41.1 132.3 %all-gather.17.cloned.1.call-start = ((), (), s32[]{:S(2)}) async-start(), calls=%async_computation.18 | async-start | bytes 2359296 | tf_op jit(solution)/shard_map/all_gather | solution.py:36
  56.4 199.2 %all-gather.21.cloned.1.call-start = ((), (), s32[]{:S(2)}) async-start(), calls=%async_computation.20 | async-start | bytes 5242880 | tf_op jit(solution)/shard_map/all_gather | solution.py:68
  63.0 273.6 %all-gather.15.cloned.1.call-start = ((), (), s32[]{:S(2)}) async-start(), calls=%async_computation.17 | async-start | bytes 5242880 | tf_op jit(solution)/shard_map/all_gather | solution.py:69
  86.5 278.4 %all-gather.23.cloned.1.call-start = ((), (), s32[]{:S(2)}) async-start(), calls=%async_computation.21 | async-start | bytes 2359296 | tf_op jit(solution)/shard_map/all_gather | solution.py:39
  102.9 344.3 %all-gather.35.cloned.1.call-start = ((), (), s32[]{:S(2)}) async-start(), calls=%async_computation.27 | async-start | bytes 5242880 | tf_op jit(solution)/shard_map/all_gather | solution.py:68
  107.0 421.0 %all-gather.33.cloned.1.call-start = ((), (), s32[]{:S(2)}) async-start(), calls=%async_computation.26 | async-start | bytes 5242880 | tf_op jit(solution)/shard_map/all_gather | solution.py:69
  109.3 473.6 %all-gather.27.cloned.1.call-start = ((), (), s32[]{:S(2)}) async-start(), calls=%async_computation.23 | async-start | bytes 9437184 | tf_op jit(solution)/shard_map/all_gather | solution.py:40
  114.5 528.5 %all-gather.31.cloned.1.call-start = ((), (), s32[]{:S(2)}) async-start(), calls=%async_computation.25 | async-start | bytes 9437184 | tf_op jit(solution)/shard_map/all_gather | solution.py:41
  145.5 753.0 %reduce-scatter.19.cloned.1.call-start = ((), (), s32[]{:S(2)}) async-start(), calls=%async_computation.29 | async-start | bytes 10485760 | tf_op jit(solution)/shard_map/reduce_scatter | solution.py:179
  754.0 291.9 %reduce-scatter.23.cloned.1.call-start = ((), (), s32[]{:S(2)}) async-start(), calls=%async_computation.31 | async-start | bytes 10485760 | tf_op jit(solution)/shard_map/reduce_scatter | solution.py:179
  784.1 409.2 %reduce-scatter.21.cloned.1.call-start = ((), (), s32[]{:S(2)}) async-start(), calls=%async_computation.30 | async-start | bytes 10485760 | tf_op jit(solution)/shard_map/reduce_scatter | solution.py:178
  824.7 516.1 %reduce-scatter.17.cloned.1.call-start = ((), (), s32[]{:S(2)}) async-start(), calls=%async_computation.28 | async-start | bytes 10485760 | tf_op jit(solution)/shard_map/reduce_scatter | solution.py:178
  865.2 540.6 %reduce-scatter.25.cloned.1.call-start = ((), (), s32[]{:S(2)}) async-start(), calls=%async_computation.32 | async-start | bytes 4718592 | tf_op jit(solution)/shard_map/reduce_scatter | solution.py:291
  887.1 564.5 %reduce-scatter.33.cloned.1.call-start = ((), (), s32[]{:S(2)}) async-start(), calls=%async_computation.36 | async-start | bytes 4718592 | tf_op jit(solution)/shard_map/reduce_scatter | solution.py:293
  1052.5 453.8 %reduce-scatter.29.cloned.1.call-start = ((), (), s32[]{:S(2)}) async-start(), calls=%async_computation.34 | async-start | bytes 4718592 | tf_op jit(solution)/shard_map/reduce_scatter | solution.py:292
  1348.4 212.9 %reduce-scatter.37.cloned.1.call-start = ((), (), s32[]{:S(2)}) async-start(), calls=%async_computation.38 | async-start | bytes 4718592 | tf_op jit(solution)/shard_map/reduce_scatter | solution.py:294
  1354.7 326.1 %reduce-scatter.41.cloned.1.call-start = ((), (), s32[]{:S(2)}) async-start(), calls=%async_computation.40 | async-start | bytes 18874368 | tf_op jit(solution)/shard_map/reduce_scatter | solution.py:295
  1381.8 418.5 %reduce-scatter.45.cloned.1.call-start = ((), (), s32[]{:S(2)}) async-start(), calls=%async_computation.42 | async-start | bytes 18874368 | tf_op jit(solution)/shard_map/reduce_scatter | solution.py:296
  1405.7 418.5 %reduce-scatter.27.cloned.1.call-start = ((), (), s32[]{:S(2)}) async-start(), calls=%async_computation.33 | async-start | bytes 655360 | tf_op jit(solution)/shard_map/reduce_scatter | solution.py:299
  1406.5 471.8 %reduce-scatter.35.cloned.1.call-start = ((), (), s32[]{:S(2)}) async-start(), calls=%async_computation.37 | async-start | bytes 655360 | tf_op jit(solution)/shard_map/reduce_scatter | solution.py:301
  1451.6 428.3 %reduce-scatter.31.cloned.1.call-start = ((), (), s32[]{:S(2)}) async-start(), calls=%async_computation.35 | async-start | bytes 655360 | tf_op jit(solution)/shard_map/reduce_scatter | solution.py:300
  1506.3 384.8 %reduce-scatter.39.cloned.1.call-start = ((), (), s32[]{:S(2)}) async-start(), calls=%async_computation.39 | async-start | bytes 655360 | tf_op jit(solution)/shard_map/reduce_scatter | solution.py:302
  1561.3 374.8 %reduce-scatter.43.cloned.1.call-start = ((), (), s32[]{:S(2)}) async-start(), calls=%async_computation.41 | async-start | bytes 2621440 | tf_op jit(solution)/shard_map/reduce_scatter | solution.py:303
  1680.8 301.4 %reduce-scatter.47.cloned.1.call-start = ((), (), s32[]{:S(2)}) async-start(), calls=%async_computation.43 | async-start | bytes 2621440 | tf_op jit(solution)/shard_map/reduce_scatter | solution.py:304
  (118 other events, 10274.2 us)
Sparse Core Ops, SparseCore 0:
  24.9 27.9 all-gather.18
  54.7 27.8 all-gather.12
  84.2 30.2 all-gather.24
  115.9 29.4 all-gather.28
  147.2 26.1 all-gather.16
  174.8 80.7 all-gather.20
  257.2 79.2 all-gather.14
  338.4 26.4 all-gather.22
  366.4 80.7 all-gather.34
  448.7 79.2 all-gather.32
  529.9 52.9 all-gather.26
  584.6 54.3 all-gather.30
  754.1 144.3 reduce-scatter.18
  900.7 145.1 reduce-scatter.22
  1048.1 145.1 reduce-scatter.20
  1195.6 145.1 reduce-scatter.16
  1344.6 52.0 reduce-scatter.24
  1400.3 51.3 reduce-scatter.32
  1455.0 51.2 reduce-scatter.28
  1509.9 51.3 reduce-scatter.36
  1564.8 115.9 reduce-scatter.40
  1684.3 115.9 reduce-scatter.44
  1893.9 42.0 reduce-scatter.42
  1939.0 43.1 reduce-scatter.46
  (4 shorter events, 81.1 us)
where the time goes:
time: 2000 us; the launch traced here: 1990 us
  waiting for transfers between devices  1350 us (68%)
  matrix products  341 us (17%)
  local copies, waits for them, and re-layouts  113 us (6%)
  blocking collectives  104 us (5%)
  other arithmetic  66.3 us (3%)
    reduce_scatter x2, waiting for transfers between devices, backward_local(): lax.psum_scatter(key_part, 'ctx', scatter_dimension=1, tiled=True)  285 us
    reduce_scatter x2, waiting for transfers between devices, backward_local(): lax.psum_scatter(value_part, 'ctx', scatter_dimension=1, tiled=True)  157 us
    all_gather x2, waiting for transfers between devices, forward_local(): lax.all_gather(key_local, 'ctx', axis=1, tiled=True)  140 us
    all_gather x2, waiting for transfers between devices, forward_local(): lax.all_gather(value_local, 'ctx', axis=1, tiled=True)  128 us
    reduce_scatter x1, waiting for transfers between devices, on_device(): lax.psum_scatter(matrix_sums[4], 'dp', scatter_dimension=0, tiled=True)  119 us
    reduce_scatter x1, waiting for transfers between devices, on_device(): lax.psum_scatter(matrix_sums[5], 'dp', scatter_dimension=0, tiled=True)  119 us
    dot_general x2, matrix products, forward_local(): jnp.dot(hidden_low, w_inner, preferred_element_type=jnp.float32) + b_inner  56.3 us
    reduce_scatter x1, waiting for transfers between devices, on_device(): lax.psum_scatter(matrix_sums[3], 'dp', scatter_dimension=0, tiled=True)  54.9 us
  transfers between devices with their start and end apart: 28, of which 23 were waited for; matrix products, arithmetic and copies ran while one was open for 20% of the time, Pallas kernels for 0%

commit v1 on v0

v1 whole, which is shorter than its diff:
```python
import functools

import jax
import jax.numpy as jnp
from jax import lax
from jax.experimental import pallas as pl
from jax.experimental.pallas import tpu as pltpu
from jax.sharding import PartitionSpec as P

HEAD_DIM = 64
PAIR = 128
EPS = 1e-05
SCALE = 0.125
LOG2E = 1.4426950408889634
VMEM = 56 * 1024 * 1024

f32 = jnp.float32
bf16 = jnp.bfloat16


def params():
    return pltpu.CompilerParams(vmem_limit_bytes=VMEM)


def cost(flops, moved, special=0):
    return pl.CostEstimate(flops=int(flops), bytes_accessed=int(moved), transcendentals=int(special))


def mm(a, b):
    return jnp.dot(a, b, preferred_element_type=f32)


def mm_nt(a, b):
    return lax.dot_general(a, b, (((1,), (1,)), ((), ())), preferred_element_type=f32)


def mm_tn(a, b):
    return lax.dot_general(a, b, (((0,), (0,)), ((), ())), preferred_element_type=f32)


def place(parts, starts, out_shape, puts):
    count = len(puts)

    def kernel(starts_ref, *refs):
        ins, out, held, sems_in, sems_out = refs[: len(parts)], *refs[len(parts) :]
        arriving, leaving = [], []
        for n, (part, which, where) in enumerate(puts):
            arriving.append(pltpu.make_async_copy(ins[part], where(held, starts_ref[which]), sems_in.at[n]))
            arriving[-1].start()
        for n, (part, which, where) in enumerate(puts):
            start = starts_ref[which]
            arriving[n].wait()
            leaving.append(pltpu.make_async_copy(where(held, start), where(out, start), sems_out.at[n]))
            leaving[-1].start()
        for copy in leaving:
            copy.wait()

    size = sum(p.size * p.dtype.itemsize for p in parts)
    return pl.pallas_call(
        kernel,
        grid_spec=pltpu.PrefetchScalarGridSpec(
            num_scalar_prefetch=1,
            grid=(1,),
            in_specs=[pl.BlockSpec(memory_space=pl.ANY)] * len(parts),
            out_specs=pl.BlockSpec(memory_space=pl.ANY),
            scratch_shapes=[
                pltpu.VMEM(out_shape.shape, out_shape.dtype),
                pltpu.SemaphoreType.DMA((count,)),
                pltpu.SemaphoreType.DMA((count,)),
            ],
        ),
        out_shape=out_shape,
        compiler_params=params(),
        cost_estimate=cost(0, 2 * size),
    )(starts, *parts)


def attention_forward(qkv, lengths):
    seqs, slots, three = qkv.shape
    pairs = three // (3 * PAIR)

    def kernel(len_ref, qkv_ref, out_ref, lse_ref):
        valid_count = len_ref[pl.program_id(0)]
        q2 = qkv_ref[0, :, 0:PAIR]
        k2 = qkv_ref[0, :, PAIR : 2 * PAIR]
        vt = qkv_ref[0, :, 2 * PAIR : 3 * PAIR].T
        lane = lax.broadcasted_iota(jnp.int32, (slots, PAIR), 1)
        row = lax.broadcasted_iota(jnp.int32, (slots, slots), 0)
        halves = []
        for h in range(2):
            qh = jnp.where((lane < HEAD_DIM) == (h == 0), q2, jnp.zeros_like(q2))
            st = mm_nt(k2, qh) * (SCALE * LOG2E)
            st = jnp.where(row < valid_count, st, -1e30)
            top = jnp.max(st, axis=0, keepdims=True)
            p = jnp.exp2(st - top)
            total = jnp.sum(p, axis=0, keepdims=True)
            p_low = (p * (1.0 / total)).astype(bf16)
            halves.append(mm(vt[h * HEAD_DIM : (h + 1) * HEAD_DIM, :], p_low))
            lse_ref[0, 0, h : h + 1, :] = top + jnp.log2(total)
        out_ref[0] = jnp.concatenate(halves, axis=0).T.astype(bf16)

    grid_spec = pltpu.PrefetchScalarGridSpec(
        num_scalar_prefetch=1,
        grid=(seqs, pairs),
        in_specs=[pl.BlockSpec((1, slots, 3 * PAIR), lambda s, j, n: (s, 0, j))],
        out_specs=[
            pl.BlockSpec((1, slots, PAIR), lambda s, j, n: (s, 0, j)),
            pl.BlockSpec((1, 1, 2, slots), lambda s, j, n: (s, j, 0, 0)),
        ],
    )
    work = seqs * pairs * 2 * slots * slots
    return pl.pallas_call(
        kernel,
        grid_spec=grid_spec,
        out_shape=[
            jax.ShapeDtypeStruct((seqs, slots, pairs * PAIR), bf16),
            jax.ShapeDtypeStruct((seqs, pairs, 2, slots), f32),
        ],
        compiler_params=params(),
        cost_estimate=cost(work * 4 * PAIR * 2, qkv.size * 2.7, work),
    )(lengths, qkv)


def attention_backward(qkv, grad_heads, lse, lengths):
    seqs, slots, three = qkv.shape
    pairs = three // (3 * PAIR)

    def kernel(len_ref, qkv_ref, gh_ref, lse_ref, out_ref, sums_ref):
        valid_count = len_ref[pl.program_id(0)]
        q2 = qkv_ref[0, :, 0:PAIR]
        k2 = qkv_ref[0, :, PAIR : 2 * PAIR]
        v2 = qkv_ref[0, :, 2 * PAIR : 3 * PAIR]
        g2 = gh_ref[0]
        kt = k2.T
        lane = lax.broadcasted_iota(jnp.int32, (slots, PAIR), 1)
        row = lax.broadcasted_iota(jnp.int32, (slots, slots), 0)
        grad_k, grad_v, grad_q = [], [], []
        for h in range(2):
            mine = (lane < HEAD_DIM) == (h == 0)
            qh = jnp.where(mine, q2, jnp.zeros_like(q2))
            gh = jnp.where(mine, g2, jnp.zeros_like(g2))
            st = mm_nt(k2, qh) * (SCALE * LOG2E)
            p = jnp.exp2(st - lse_ref[0, 0, h : h + 1, :])
            p = jnp.where(row < valid_count, p, 0.0)
            dp = mm_nt(v2, gh)
            inner_sum = jnp.sum(p * dp, axis=0, keepdims=True)
            ds = (p * (dp - inner_sum)).astype(bf16)
            grad_v.append(mm(p.astype(bf16), g2))
            grad_k.append(mm(ds, q2))
            grad_q.append(mm(kt[h * HEAD_DIM : (h + 1) * HEAD_DIM, :], ds))
        gq = (jnp.concatenate(grad_q, axis=0).T * SCALE).astype(bf16)
        gk = (jnp.where(lane < HEAD_DIM, grad_k[0], grad_k[1]) * SCALE).astype(bf16)
        gv = jnp.where(lane < HEAD_DIM, grad_v[0], grad_v[1]).astype(bf16)
        out_ref[0, :, 0:PAIR] = gq
        out_ref[0, :, PAIR : 2 * PAIR] = gk
        out_ref[0, :, 2 * PAIR : 3 * PAIR] = gv
        sums_ref[0, 0, 0:1, :] = jnp.sum(gq.astype(f32), axis=0, keepdims=True)
        sums_ref[0, 0, 1:2, :] = jnp.sum(gv.astype(f32), axis=0, keepdims=True)

    grid_spec = pltpu.PrefetchScalarGridSpec(
        num_scalar_prefetch=1,
        grid=(seqs, pairs),
        in_specs=[
            pl.BlockSpec((1, slots, 3 * PAIR), lambda s, j, n: (s, 0, j)),
            pl.BlockSpec((1, slots, PAIR), lambda s, j, n: (s, 0, j)),
            pl.BlockSpec((1, 1, 2, slots), lambda s, j, n: (s, j, 0, 0)),
        ],
        out_specs=[
            pl.BlockSpec((1, slots, 3 * PAIR), lambda s, j, n: (s, 0, j)),
            pl.BlockSpec((1, 1, 2, PAIR), lambda s, j, n: (s, j, 0, 0)),
        ],
    )
    work = seqs * pairs * 2 * slots * slots
    return pl.pallas_call(
        kernel,
        grid_spec=grid_spec,
        out_shape=[
            jax.ShapeDtypeStruct((seqs, slots, three), bf16),
            jax.ShapeDtypeStruct((seqs, pairs, 2, PAIR), f32),
        ],
        compiler_params=params(),
        cost_estimate=cost(work * 10 * PAIR * 2, qkv.size * 5, work),
    )(lengths, qkv, grad_heads, lse)


def project(x, w, bias, cols=768):
    rows, depth = x.shape
    width = bias.shape[1]

    def kernel(x_ref, w_ref, b_ref, out_ref):
        out_ref[...] = (mm(x_ref[...], w_ref[...]) + b_ref[...]).astype(bf16)

    return pl.pallas_call(
        kernel,
        grid=(width // cols,),
        in_specs=[
            pl.BlockSpec((rows, depth), lambda j: (0, 0)),
            pl.BlockSpec((depth, cols), lambda j: (0, j)),
            pl.BlockSpec((1, cols), lambda j: (0, j)),
        ],
        out_specs=pl.BlockSpec((rows, cols), lambda j: (0, j)),
        out_shape=jax.ShapeDtypeStruct((rows, width), bf16),
        compiler_params=params(),
        cost_estimate=cost(2 * rows * depth * width, 2 * (x.size + depth * width + rows * width)),
    )(x, w, bias)


def normed(summed):
    centred = summed - jnp.mean(summed, axis=-1, keepdims=True)
    rstd = lax.rsqrt(jnp.mean(centred * centred, axis=-1, keepdims=True) + EPS)
    return centred * rstd, rstd


def norm_back(grad_hat, hat, rstd):
    return rstd * (
        grad_hat
        - jnp.mean(grad_hat, axis=-1, keepdims=True)
        - hat * jnp.mean(grad_hat * hat, axis=-1, keepdims=True)
    )


def out_forward(heads, w_attn, x, b_out, gain, shift, rows=256):
    total, width = x.shape

    def kernel(h_ref, w_ref, x_ref, b_ref, g_ref, s_ref, hat_ref, rstd_ref, low_ref):
        summed = mm(h_ref[...], w_ref[...]) + b_ref[...] + x_ref[...].astype(f32)
        hat, rstd = normed(summed)
        hat_ref[...] = hat
        rstd_ref[...] = rstd
        low_ref[...] = (hat * g_ref[...] + s_ref[...]).astype(bf16)

    block = pl.BlockSpec((rows, width), lambda i: (i, 0))
    vec = pl.BlockSpec((1, width), lambda i: (0, 0))
    return pl.pallas_call(
        kernel,
        grid=(total // rows,),
        in_specs=[block, pl.BlockSpec((width, width), lambda i: (0, 3)), block, vec, vec, vec],
        out_specs=[block, pl.BlockSpec((rows, 1), lambda i: (i, 0)), block],
        out_shape=[
            jax.ShapeDtypeStruct((total, width), f32),
            jax.ShapeDtypeStruct((total, 1), f32),
            jax.ShapeDtypeStruct((total, width), bf16),
        ],
        compiler_params=params(),
        cost_estimate=cost(2 * total * width * width, total * width * 10 + width * width * 2),
    )(heads, w_attn, x, b_out, gain, shift)


def gelu_pair(x):
    density = jnp.exp2(x * x * (-0.5 * LOG2E))
    t = 1.0 / (jnp.abs(x) * (0.3275911 * 0.7071067811865476) + 1.0)
    poly = 1.061405429 * 0.5
    for coefficient in (-1.453152027, 1.421413741, -0.284496736, 0.254829592):
        poly = poly * t + coefficient * 0.5
    tail = poly * t * density
    phi = jnp.where(x < 0, tail, 1.0 - tail)
    active = x * phi
    slope = phi + x * density * 0.3989422804014327
    return active, slope


def ffn_one(hidden, w_inner, b_inner, cols=512, chunk=256):
    rows, depth = hidden.shape
    width = w_inner.shape[1]

    def kernel(h_ref, w_ref, b_ref, act_ref, slope_ref):
        for c in range(rows // chunk):
            part = pl.ds(c * chunk, chunk)
            inner = mm(h_ref[part, :], w_ref[...]) + b_ref[...]
            active, slope = gelu_pair(inner)
            act_ref[part, :] = active.astype(bf16)
            slope_ref[part, :] = slope.astype(bf16)

    out = pl.BlockSpec((rows, cols), lambda j: (0, j))
    return pl.pallas_call(
        kernel,
        grid=(width // cols,),
        in_specs=[
            pl.BlockSpec((rows, depth), lambda j: (0, 0)),
            pl.BlockSpec((depth, cols), lambda j: (0, j)),
            pl.BlockSpec((1, cols), lambda j: (0, j)),
        ],
        out_specs=[out, out],
        out_shape=[jax.ShapeDtypeStruct((rows, width), bf16)] * 2,
        compiler_params=params(),
        cost_estimate=cost(2 * rows * depth * width, 2 * (hidden.size + w_inner.size + 2 * rows * width), 2 * rows * width),
    )(hidden, w_inner, b_inner)


def ffn_two(active, w_outer, hat_one, cot, lengths, vectors, slots, rows=256):
    total, depth = active.shape
    width = w_outer.shape[1]
    per_seq = slots // rows

    def kernel(len_ref, a_ref, w_ref, hat_ref, cot_ref, vec_ref, mixed_ref, grad_ref, low_ref, sums_ref):
        i = pl.program_id(0)
        g_one, s_one, b_outer, g_two, s_two = (vec_ref[k : k + 1, :] for k in range(5))
        summed = mm(a_ref[...], w_ref[...]) + b_outer + (hat_ref[...] * g_one + s_one)
        hat, rstd = normed(summed)
        mixed_ref[...] = (hat * g_two + s_two).astype(bf16)
        slot = (i % per_seq) * rows + lax.broadcasted_iota(jnp.int32, (rows, width), 0)
        grad_y = jnp.where(slot < len_ref[i // per_seq], cot_ref[...].astype(f32), 0.0)
        grad = norm_back(grad_y * g_two, hat, rstd)
        grad_ref[...] = grad
        low = grad.astype(bf16)
        low_ref[...] = low

        @pl.when(i == 0)
        def _():
            sums_ref[...] = jnp.zeros_like(sums_ref)

        sums_ref[0:1, :] += jnp.sum(grad_y * hat, axis=0, keepdims=True)
        sums_ref[1:2, :] += jnp.sum(grad_y, axis=0, keepdims=True)
        sums_ref[2:3, :] += jnp.sum(low.astype(f32), axis=0, keepdims=True)

    block = pl.BlockSpec((rows, width), lambda i, n: (i, 0))
    grid_spec = pltpu.PrefetchScalarGridSpec(
        num_scalar_prefetch=1,
        grid=(total // rows,),
        in_specs=[
            pl.BlockSpec((rows, depth), lambda i, n: (i, 0)),
            pl.BlockSpec(w_outer.shape, lambda i, n: (0, 0)),
            block,
            block,
            pl.BlockSpec((8, width), lambda i, n: (0, 0)),
        ],
        out_specs=[block, block, block, pl.BlockSpec((8, width), lambda i, n: (0, 0))],
    )
    return pl.pallas_call(
        kernel,
        grid_spec=grid_spec,
        out_shape=[
            jax.ShapeDtypeStruct((total, width), bf16),
            jax.ShapeDtypeStruct((total, width), f32),
            jax.ShapeDtypeStruct((total, width), bf16),
            jax.ShapeDtypeStruct((8, width), f32),
        ],
        compiler_params=params(),
        cost_estimate=cost(2 * total * width * depth, active.size * 2 + w_outer.size * 2 + total * width * 14),
    )(lengths, active, w_outer, hat_one, cot, vectors)


def ffn_back(grad_low, start, hidden_t, active, slope, w_outer, w_inner, order, cols=512):
    rows, width = grad_low.shape
    count = order.shape[0]
    half = width // 2

    def kernel(ord_ref, g_ref, start_ref, ht_ref, a_ref, s_ref, wo_ref, wi_ref, grad_ref, dwo_ref, dws_ref, dwk_ref, bias_ref):
        j = pl.program_id(0)
        grad = g_ref[...]
        grad_active = mm_nt(grad, wo_ref[...])
        inner = (grad_active * s_ref[...].astype(f32)).astype(bf16)
        bias_ref[...] = jnp.sum(inner.astype(f32), axis=0, keepdims=True)
        dwo_ref[...] = mm_tn(a_ref[...], grad).astype(bf16)
        dws_ref[...] = mm(ht_ref[0:half, :], inner).astype(bf16)
        dwk_ref[...] = mm(ht_ref[half:width, :], inner).astype(bf16)

        @pl.when(j == 0)
        def _():
            grad_ref[...] = start_ref[...]

        grad_ref[...] += mm_nt(inner, wi_ref[...])

    whole = lambda j, o: (0, 0)
    grid_spec = pltpu.PrefetchScalarGridSpec(
        num_scalar_prefetch=1,
        grid=(count,),
        in_specs=[
            pl.BlockSpec((rows, width), whole),
            pl.BlockSpec((rows, width), whole),
            pl.BlockSpec((width, rows), whole),
            pl.BlockSpec((rows, cols), lambda j, o: (0, o[j])),
            pl.BlockSpec((rows, cols), lambda j, o: (0, o[j])),
            pl.BlockSpec((cols, width), lambda j, o: (o[j], 0)),
            pl.BlockSpec((width, cols), lambda j, o: (0, o[j])),
        ],
        out_specs=[
            pl.BlockSpec((rows, width), whole),
            pl.BlockSpec((cols, width), lambda j, o: (j, 0)),
            pl.BlockSpec((half, cols), lambda j, o: (0, j)),
            pl.BlockSpec((half, cols), lambda j, o: (0, j)),
            pl.BlockSpec((1, cols), lambda j, o: (0, j)),
        ],
    )
    return pl.pallas_call(
        kernel,
        grid_spec=grid_spec,
        out_shape=[
            jax.ShapeDtypeStruct((rows, width), f32),
            jax.ShapeDtypeStruct((count * cols, width), bf16),
            jax.ShapeDtypeStruct((half, count * cols), bf16),
            jax.ShapeDtypeStruct((half, count * cols), bf16),
            jax.ShapeDtypeStruct((1, count * cols), f32),
        ],
        compiler_params=params(),
        cost_estimate=cost(8 * rows * width * count * cols, 12 * count * cols * width + 12 * rows * width),
    )(order, grad_low, start, hidden_t, active, slope, w_outer, w_inner)


def out_back(grad_hidden, hat, rstd, gain, w_attn, heads_s, heads_k, rows=256):
    total, width = grad_hidden.shape
    half = width // 2
    steps = total // rows

    def kernel(gh_ref, hat_ref, rstd_ref, gain_ref, w_ref, hs_ref, hk_ref, one_ref, heads_ref, dws_ref, dwk_ref, sums_ref, acc_s, acc_k):
        i = pl.program_id(0)
        grad_y = gh_ref[...]
        hat = hat_ref[...]
        grad = norm_back(grad_y * gain_ref[...], hat, rstd_ref[...])
        one_ref[...] = grad
        low = grad.astype(bf16)
        heads_ref[...] = mm_nt(low, w_ref[...]).astype(bf16)

        @pl.when(i == 0)
        def _():
            sums_ref[...] = jnp.zeros_like(sums_ref)
            acc_s[...] = jnp.zeros_like(acc_s)
            acc_k[...] = jnp.zeros_like(acc_k)

        acc_s[...] += mm_tn(hs_ref[...], low)
        acc_k[...] += mm_tn(hk_ref[...], low)
        sums_ref[0:1, :] += jnp.sum(grad_y * hat, axis=0, keepdims=True)
        sums_ref[1:2, :] += jnp.sum(grad_y, axis=0, keepdims=True)
        sums_ref[2:3, :] += jnp.sum(low.astype(f32), axis=0, keepdims=True)

        @pl.when(i == steps - 1)
        def _():
            dws_ref[...] = acc_s[...].astype(bf16)
            dwk_ref[...] = acc_k[...].astype(bf16)

    block = pl.BlockSpec((rows, width), lambda i: (i, 0))
    halfblock = pl.BlockSpec((rows, half), lambda i: (i, 0))
    whole = lambda i: (0, 0)
    return pl.pallas_call(
        kernel,
        grid=(steps,),
        in_specs=[
            block,
            block,
            pl.BlockSpec((rows, 1), lambda i: (i, 0)),
            pl.BlockSpec((1, width), whole),
            pl.BlockSpec((width, width), lambda i: (0, 3)),
            halfblock,
            halfblock,
        ],
        out_specs=[
            block,
            block,
            pl.BlockSpec((half, width), whole),
            pl.BlockSpec((half, width), whole),
            pl.BlockSpec((8, width), whole),
        ],
        out_shape=[
            jax.ShapeDtypeStruct((total, width), f32),
            jax.ShapeDtypeStruct((total, width), bf16),
            jax.ShapeDtypeStruct((half, width), bf16),
            jax.ShapeDtypeStruct((half, width), bf16),
            jax.ShapeDtypeStruct((8, width), f32),
        ],
        scratch_shapes=[pltpu.VMEM((half, width), f32), pltpu.VMEM((half, width), f32)],
        compiler_params=params(),
        cost_estimate=cost(4 * total * width * width, total * width * 16 + width * width * 4),
    )(grad_hidden, hat, rstd, gain, w_attn, heads_s, heads_k)


def token_grads(grad_qkv, w_attn, grad_one, rows=256):
    total, three = grad_qkv.shape
    width = grad_one.shape[1]

    def kernel(g_ref, w_ref, one_ref, out_ref):
        out_ref[...] = (mm_nt(g_ref[...], w_ref[...]) + one_ref[...]).astype(bf16)

    return pl.pallas_call(
        kernel,
        grid=(total // rows,),
        in_specs=[
            pl.BlockSpec((rows, three), lambda i: (i, 0)),
            pl.BlockSpec((width, three), lambda i: (0, 0)),
            pl.BlockSpec((rows, width), lambda i: (i, 0)),
        ],
        out_specs=pl.BlockSpec((rows, width), lambda i: (i, 0)),
        out_shape=jax.ShapeDtypeStruct((total, width), bf16),
        compiler_params=params(),
        cost_estimate=cost(2 * total * three * width, 2 * (total * three + width * three) + total * width * 6),
    )(grad_qkv, w_attn, grad_one)


def swap(array, axis, size, mask):
    return lax.ppermute(array, axis, [(i, i ^ mask) for i in range(size)])


def shift(array, axis, size, by):
    return lax.ppermute(array, axis, [(i, (i + by) % size) for i in range(size)])


def gather_columns(shard, c):
    near = swap(shard, "ctx", 4, 1)
    odd = (c & 1) == 1
    pair = jnp.stack([jnp.where(odd, near, shard), jnp.where(odd, shard, near)])
    across = lax.ppermute(pair, "ctx", [(1, 2), (2, 1)])
    outwards = lax.ppermute(across, "ctx", [(1, 0), (2, 3)])
    middle = (c == 1) | (c == 2)
    other = jnp.where(middle, across, outwards)
    upper = c >= 2
    return [
        jnp.where(upper, other[0], pair[0]),
        jnp.where(upper, other[1], pair[1]),
        jnp.where(upper, pair[0], other[0]),
        jnp.where(upper, pair[1], other[1]),
    ]


def gather_rows(block, r, dp):
    if dp != 8:
        return lax.all_gather(block, "dp", axis=0, tiled=True)
    rows, width = block.shape
    half = rows // 2
    by_x = swap(block, "dp", dp, 2)
    by_y = swap(block, "dp", dp, 4)
    far_top = swap(by_x[:half], "dp", dp, 4)
    far_low = swap(by_y[half:], "dp", dp, 2)
    own = [block, by_x, by_y, far_top, far_low]
    twin = [swap(part, "dp", dp, 1) for part in own]

    def at(offset, count):
        return lambda out, start: out.at[pl.ds(pl.multiple_of(start + offset, half), count), :]

    puts = []
    for n, base in ((0, 0), (5, 1)):
        puts += [
            (n, base, at(0, rows)),
            (n + 1, base ^ 2, at(0, rows)),
            (n + 2, base ^ 4, at(0, rows)),
            (n + 3, base ^ 6, at(0, half)),
            (n + 4, base ^ 6, at(half, half)),
        ]
    starts = jnp.stack([(r ^ m) * rows for m in range(8)]).astype(jnp.int32)
    return place(own + twin, starts, jax.ShapeDtypeStruct((dp * rows, width), block.dtype), puts)


def to_sequences(slots, c, ctx):
    seqs, count, width = slots.shape
    per = seqs // ctx
    parts = []
    for d in range(ctx):
        part = lax.dynamic_slice(slots, (((c + d) % ctx) * per, 0, 0), (per, count, width))
        parts.append(shift(part, "ctx", ctx, d) if d else part)
    starts = jnp.stack([((c - d) % ctx) * count for d in range(ctx)]).astype(jnp.int32)
    at = lambda out, start: out.at[:, pl.ds(pl.multiple_of(start, count), count), :]
    shape = jax.ShapeDtypeStruct((per, ctx * count, width), slots.dtype)
    return place(parts, starts, shape, [(d, d, at) for d in range(ctx)])


def to_slots(whole, c, ctx):
    per, total, width = whole.shape
    count = total // ctx
    parts = []
    for d in range(ctx):
        part = lax.dynamic_slice(whole, (0, ((c + d) % ctx) * count, 0), (per, count, width))
        parts.append(shift(part, "ctx", ctx, d) if d else part)
    starts = jnp.stack([((c - d) % ctx) * per for d in range(ctx)]).astype(jnp.int32)
    at = lambda out, start: out.at[pl.ds(start, per), :, :]
    shape = jax.ShapeDtypeStruct((per * ctx, count, width), whole.dtype)
    return place(parts, starts, shape, [(d, d, at) for d in range(ctx)])


def scatter_rows(parts, r, dp):
    y, x = (r >> 2) & 1, (r >> 1) & 1

    def pick(array, yi, xi, h):
        blocks, rows, width = array.shape
        array = array.reshape(2, 2, 2, rows // 2, width)
        start = (0 if yi is None else yi, 0 if xi is None else xi, h, 0, 0)
        sizes = (2 if yi is None else 1, 2 if xi is None else 1, 1, rows // 2, width)
        out = lax.dynamic_slice(array, tuple(jnp.int32(s) for s in start), sizes)
        return out.reshape(sizes[0] * sizes[1], rows // 2, width).astype(f32)

    def summed(yi, xi, h):
        return [pick(kept, yi, xi, h) + pick(got, yi, xi, h) for kept, got in parts]

    def pack(arrays):
        return jnp.concatenate([a.astype(bf16) for a in arrays], axis=-1)

    widths = [kept.shape[-1] for kept, _ in parts]

    def unpack(array):
        pieces, at = [], 0
        for width in widths:
            pieces.append(lax.slice_in_dim(array, at, at + width, axis=2).astype(f32))
            at += width
        return pieces

    def add(left, right):
        return [a + b for a, b in zip(left, right)]

    def one(array, index):
        return lax.dynamic_slice_in_dim(array, index, 1, axis=0)

    got_x = swap(pack(summed(None, 1 - x, 0)), "dp", dp, 2)
    got_y = swap(pack(summed(1 - y, None, 1)), "dp", dp, 4)
    top = swap(pack(add(summed(1 - y, x, 0), unpack(one(got_x, 1 - y)))), "dp", dp, 4)
    low = swap(pack(add(summed(y, 1 - x, 1), unpack(one(got_y, 1 - x)))), "dp", dp, 2)
    top = add(add(summed(y, x, 0), unpack(one(got_x, y))), unpack(top))
    low = add(add(summed(y, x, 1), unpack(one(got_y, x))), unpack(low))
    return [jnp.concatenate([a[0], b[0]], axis=0) for a, b in zip(top, low)]


def scatter_columns(blocks, c):
    sizes = [b.shape[1] // 4 for b in blocks]
    pair = c >> 1

    def pack(arrays):
        return jnp.concatenate([a.astype(bf16) for a in arrays], axis=1)

    def unpack(array, times):
        pieces, at = [], 0
        for size in sizes:
            pieces.append(array[:, at : at + times * size].astype(f32))
            at += times * size
        return pieces

    def columns(array, start, count):
        return lax.dynamic_slice_in_dim(array, start, count, axis=1)

    other = [columns(b, (1 - pair) * 2 * s, 2 * s) for b, s in zip(blocks, sizes)]
    got = lax.ppermute(pack(other), "ctx", [(0, 1), (3, 2)])
    other = [a + b for a, b in zip(other, unpack(got, 2))]
    got = lax.ppermute(pack(other), "ctx", [(1, 2), (2, 1)])
    mine = [columns(b, pair * 2 * s, 2 * s) + g for b, s, g in zip(blocks, sizes, unpack(got, 2))]
    odd = c & 1
    got = swap(pack([columns(m, (1 - odd) * s, s) for m, s in zip(mine, sizes)]), "ctx", 4, 1)
    return [columns(m, odd * s, s) + g for m, s, g in zip(mine, sizes, unpack(got, 1))]


def sum_everywhere(vector, dp, ctx):
    for axis, size in (("dp", dp), ("ctx", ctx)):
        mask = 1
        while mask < size:
            vector = vector + swap(vector, axis, size, mask)
            mask *= 2
    return vector


def pair_columns(query, key, value):
    rows, width = query.shape
    pieces = []
    for j in range(width // PAIR):
        pieces += [a[:, j * PAIR : (j + 1) * PAIR] for a in (query, key, value)]
    return jnp.concatenate(pieces, axis=1)


def on_device(
    dp,
    ctx,
    tokens,
    lengths,
    cotangent,
    weight_query,
    weight_key,
    weight_value,
    weight_out,
    weight_inner,
    weight_outer,
    bias_query,
    bias_value,
    bias_out,
    bias_inner,
    bias_outer,
    gain_attn,
    shift_attn,
    gain_ffn,
    shift_ffn,
):
    seq_total, slot_count, width = tokens.shape
    units = bias_inner.shape[0]
    per = seq_total // ctx
    slots = slot_count * ctx
    rows = per * slots
    c = lax.axis_index("ctx")
    r = lax.axis_index("dp")
    core = r & 1
    paired = dp == 8

    own_lengths = lax.dynamic_slice(lengths, (c * per,), (per,))
    attn_shard = jnp.concatenate([pair_columns(weight_query, weight_key, weight_value), weight_out], axis=1)
    split = attn_shard.shape[1] - weight_out.shape[1]

    pieces = gather_columns(attn_shard, c)
    block = jnp.concatenate([p[:, :split] for p in pieces] + [p[:, split:] for p in pieces], axis=1)
    x = to_sequences(tokens, c, ctx).reshape(rows, width)
    w_attn = gather_rows(block, r, dp)
    w_inner = gather_rows(jnp.concatenate(gather_columns(weight_inner, c), axis=1), r, dp)
    w_outer = gather_rows(jnp.concatenate(gather_columns(weight_outer, c), axis=1), r, dp)
    cot = to_sequences(cotangent, c, ctx).reshape(rows, width)

    bias_qkv = pair_columns(bias_query[None], jnp.zeros_like(bias_query)[None], bias_value[None])
    qkv = project(x, w_attn, bias_qkv).reshape(per, slots, 3 * width)
    heads, lse = attention_forward(qkv, own_lengths)
    heads = heads.reshape(rows, width)
    hat_one, rstd_one, hidden_low = out_forward(
        heads, w_attn, x, bias_out[None], gain_attn[None], shift_attn[None]
    )
    active, slope = ffn_one(hidden_low, w_inner, bias_inner[None])
    vectors = jnp.stack([gain_attn, shift_attn, bias_outer, gain_ffn, shift_ffn] + [shift_ffn] * 3)
    mixed, grad_two, grad_outer, sums_two = ffn_two(
        active, w_outer, hat_one, cot, own_lengths, vectors, slots
    )
    mixed = to_slots(mixed.reshape(per, slots, width), c, ctx)

    def split_features(array):
        count, features = array.shape
        if not paired:
            return array[:, : features // 2], array[:, features // 2 :]
        array = array.reshape(count, 4, 2, features // 8)
        halves = [
            lax.dynamic_slice_in_dim(array, which, 1, axis=2).reshape(count, features // 2)
            for which in (1 - core, core)
        ]
        return halves

    hidden_t = jnp.concatenate([h.T for h in split_features(hidden_low)], axis=0)
    if paired:
        order_s = (jnp.arange(4) * 2 + (1 - core)).astype(jnp.int32)
        order_k = (jnp.arange(4) * 2 + core).astype(jnp.int32)
    else:
        order_s, order_k = jnp.arange(4, dtype=jnp.int32), jnp.arange(4, 8, dtype=jnp.int32)
    grad_hidden, outer_s, inner_s1, inner_k1, bias_1 = ffn_back(
        grad_outer, grad_two, hidden_t, active, slope, w_outer, w_inner, order_s
    )
    grad_hidden, outer_k, inner_s2, inner_k2, bias_2 = ffn_back(
        grad_outer, grad_hidden, hidden_t, active, slope, w_outer, w_inner, order_k
    )
    heads_s, heads_k = split_features(heads)
    grad_one, grad_heads, out_s, out_k, sums_one = out_back(
        grad_hidden, hat_one, rstd_one, gain_attn[None], w_attn, heads_s, heads_k
    )
    grad_qkv, sums_qkv = attention_backward(qkv, grad_heads.reshape(per, slots, width), lse, own_lengths)
    grad_qkv = grad_qkv.reshape(rows, 3 * width)
    x_s, x_k = split_features(x)
    qkv_s = mm_tn(x_s, grad_qkv).astype(bf16)
    qkv_k = mm_tn(x_k, grad_qkv).astype(bf16)
    grad_tokens = token_grads(grad_qkv, w_attn, grad_one)
    grad_tokens = to_slots(grad_tokens.reshape(per, slots, width), c, ctx).astype(f32)

    if paired:

        def twin(sent, kept):
            blocks = kept.reshape(4, kept.shape[0] // 4, kept.shape[1])
            return (blocks, swap(sent, "dp", dp, 1).reshape(blocks.shape))

        (sum_outer,) = scatter_columns(scatter_rows([twin(outer_s, outer_k)], r, dp), c)
        inner_1, inner_2, sum_out = scatter_columns(
            scatter_rows([twin(inner_s2, inner_k1), twin(inner_s1, inner_k2), twin(out_s, out_k)], r, dp), c
        )
        sum_inner = jnp.where(
            core == 0,
            jnp.concatenate([inner_2, inner_1], axis=1),
            jnp.concatenate([inner_1, inner_2], axis=1),
        )
        (sum_qkv,) = scatter_columns(scatter_rows([twin(qkv_s, qkv_k)], r, dp), c)
        b_1, b_2 = bias_1.reshape(4, -1), bias_2.reshape(4, -1)
        bias_units = jnp.where(core == 0, jnp.stack([b_2, b_1], axis=1), jnp.stack([b_1, b_2], axis=1)).reshape(units)
    else:

        def over_dp(array):
            return lax.psum_scatter(array.astype(f32), "dp", scatter_dimension=0, tiled=True)

        inner_full = jnp.concatenate(
            [jnp.concatenate([inner_s1, inner_s2], axis=1), jnp.concatenate([inner_k1, inner_k2], axis=1)], axis=0
        )
        (sum_outer,) = scatter_columns([over_dp(jnp.concatenate([outer_s, outer_k], axis=0))], c)
        sum_inner, sum_out = scatter_columns(
            [over_dp(inner_full), over_dp(jnp.concatenate([out_s, out_k], axis=0))], c
        )
        (sum_qkv,) = scatter_columns([over_dp(jnp.concatenate([qkv_s, qkv_k], axis=0))], c)
        bias_units = jnp.concatenate([bias_1[0], bias_2[0]])

    own_rows = sum_qkv.shape[0]
    sum_qkv = sum_qkv.reshape(own_rows, -1, 3, PAIR)
    sum_query, sum_key, sum_value = (sum_qkv[:, :, k].reshape(own_rows, -1) for k in range(3))

    sums_qkv = jnp.sum(sums_qkv, axis=0)
    packed = jnp.concatenate(
        [
            sums_qkv[:, 0].reshape(-1),
            sums_qkv[:, 1].reshape(-1),
            sums_one[2],
            bias_units,
            sums_two[2],
            sums_one[0],
            sums_one[1],
            sums_two[0],
            sums_two[1],
        ]
    )
    packed = sum_everywhere(packed.reshape(-1, 128), dp, ctx).reshape(-1)
    totals, at = [], 0
    for size in (width, width, width, units, width, width, width, width, width):
        totals.append(packed[at : at + size])
        at += size
    return (mixed, grad_tokens, sum_query, sum_key, sum_value, sum_out, sum_inner, sum_outer, *totals)


def solution(mesh):
    rows = P("dp", "ctx", None)
    matrix = P("dp", "ctx")
    in_specs = (rows, P("dp"), rows) + (matrix,) * 6 + (P(),) * 9
    out_specs = (rows, rows) + (matrix,) * 6 + (P(),) * 9
    step = functools.partial(on_device, mesh.shape["dp"], mesh.shape["ctx"])
    return jax.shard_map(step, mesh=mesh, in_specs=in_specs, out_specs=out_specs, check_vma=False)
```

time: 2000 us -> 810 us (0.41)
  waiting for transfers between devices: 1350 us -> 263 us
  matrix products: 341 us -> 11.4 us
  Pallas kernels: 0 us -> 239 us
  starting transfers between devices: 1.92 us -> 115 us
  blocking collectives: 104 us -> 0 us
    reduce_scatter x16 -> x0, waiting for transfers between devices: 952 us -> none  [the longest x2 285 us: backward_local(): lax.psum_scatter(key_part, 'ctx', scatter_dimension=1, tiled=True)]
    all_gather x12 -> x0, waiting for transfers between devices: 393 us -> none  [the longest x2 140 us: forward_local(): lax.all_gather(key_local, 'ctx', axis=1, tiled=True)]
    dot_general x48 -> x2, matrix products: 341 us -> 11.4 us  [mm_tn(): lax.dot_general(a, b, (((0,), (0,)), ((), ())), preferred_element_type=f32)]
    ppermute x0 -> x79, waiting for transfers between devices: none -> 263 us  [the longest x55 109 us: swap(): return lax.ppermute(array, axis, [(i, i ^ mask) for i in range(size)])]
    pallas_call x0 -> x17, Pallas kernels: none -> 239 us  [the longest x2 54.9 us: ffn_back(): pl.pallas_call(kernel, grid_spec=grid_spec, out_shape=[jax.ShapeDtypeStru...]
    ppermute x0 -> x79, starting transfers between devices: none -> 115 us  [the longest x12 62.6 us: shift(): lax.ppermute(array, axis, [(i, (i + by) % size) for i in range(size)])]
    all_gather x4 -> x0, blocking collectives: 64 us -> none  [the longest x1 17.5 us: fetch_weights(): lax.all_gather(w_key, 'ctx', axis=1, tiled=True)]
    reshape x12 -> x1, local copies, waits for them, and re-layouts: 56.3 us -> 3.23 us  [split_features(): array = array.reshape(count, 4, 2, features // 8)]
  transfers between devices with their start and end apart: 28 -> 79, of which waited for: 23 -> 28; matrix products, arithmetic and copies ran while one was open for 20% -> 21% of each run, Pallas kernels for 0% -> 13%
where the time goes in v1:
time: 810 us; the launch traced here: 804 us
  waiting for transfers between devices  263 us (32%)
  Pallas kernels  239 us (30%)
  starting transfers between devices  115 us (14%)
  local copies, waits for them, and re-layouts  113 us (14%)
  other arithmetic  60.9 us (8%)
  matrix products  11.4 us (1%)
    ppermute x55, waiting for transfers between devices, swap(): return lax.ppermute(array, axis, [(i, i ^ mask) for i in range(size)])  109 us
    ppermute x12, waiting for transfers between devices, shift(): lax.ppermute(array, axis, [(i, (i + by) % size) for i in range(size)])  79.3 us
    ppermute x12, starting transfers between devices, shift(): lax.ppermute(array, axis, [(i, (i + by) % size) for i in range(size)])  62.6 us
    ppermute x3, waiting for transfers between devices, gather_columns(): outwards = lax.ppermute(across, 'ctx', [(1, 0), (2, 3)])  60.3 us
    pallas_call x2, Pallas kernels, ffn_back(): pl.pallas_call(kernel, grid_spec=grid_spec, out_shape=[jax.ShapeDtypeStru...  54.9 us
    unnamed x158, local copies, waits for them, and re-layouts  46.8 us
    ppermute x55, starting transfers between devices, swap(): return lax.ppermute(array, axis, [(i, i ^ mask) for i in range(size)])  39.4 us
    pallas_call x7, Pallas kernels, place(): pl.pallas_call(kernel, grid_spec=pltpu.PrefetchScalarGridSpec(num_scalar_...  34.1 us
  transfers between devices with their start and end apart: 79, of which 28 were waited for; matrix products, arithmetic and copies ran while one was open for 21% of the time, Pallas kernels for 13%

profile of v1, /device:TPU:0, one launch (start us, length us, event | category | flops | bytes accessed | tf_op | source)
XLA Modules:
  0.0 804.1 jit_solution(16943226820428589807)
XLA Ops:
  27.6 27.5 %collective-permute-start.1 = (bf16[2,128,1024]{2,1,0:T(8,128)(2,1)S(1)}, bf16[2,128,1024]{2,1,0:T(8,128)(2,1)S(1)}, u32[]{:S(2)}, u32[]{:S(2)}) collective-permute-start(bf16[2,128,1024]{2,1,0:T(8,128)(2,1)S(1)} %get-tuple-element.146), channel_id=1, source_target_pairs={{0,2},{1,3},{2,0},{3,1},{4,6},{5,7},{6,4},{7,5},{8,10},{9,11},{10,... | collective-permute-start | bytes 1572872 | tf_op jit(solution)/shard_map/ppermute | solution.py:493
  72.6 24.5 %collective-permute-done.17 = bf16[2,128,1024]{2,1,0:T(8,128)(2,1)S(1)} collective-permute-done((bf16[2,128,1024]{2,1,0:T(8,128)(2,1)S(1)}, bf16[2,128,1024]{2,1,0:T(8,128)(2,1)S(1)}, u32[]{:S(2)}, u32[]{:S(2)}) %collective-permute-start.17) | collective-permute-done | bytes 524320 | tf_op jit(solution)/shard_map/ppermute | solution.py:501
  98.6 30.0 %collective-permute-done.29 = bf16[2,512,256]{2,1,0:T(8,128)(2,1)S(1)} collective-permute-done((bf16[2,512,256]{2,1,0:T(8,128)(2,1)S(1)}, bf16[2,512,256]{2,1,0:T(8,128)(2,1)S(1)}, u32[]{:S(2)}, u32[]{:S(2)}) %collective-permute-start.29) | collective-permute-done | bytes 524320 | tf_op jit(solution)/shard_map/ppermute | solution.py:501
  134.7 9.9 %collective-permute-done.39.refs_1_ = bf16[2,128,1024]{2,1,0:T(8,128)(2,1)} collective-permute-done((bf16[2,128,1024]{2,1,0:T(8,128)(2,1)S(1)}, bf16[2,128,1024]{2,1,0:T(8,128)(2,1)}, u32[]{:S(2)}, u32[]{:S(2)}) %collective-permute-start.39) | collective-permute-done | bytes 524320 | tf_op jit(solution)/shard_map/ppermute | solution.py:493
  145.1 9.9 %collective-permute-done.7.refs_2_ = bf16[128,4096]{1,0:T(8,128)(2,1)} collective-permute-done((bf16[128,4096]{1,0:T(8,128)(2,1)}, bf16[128,4096]{1,0:T(8,128)(2,1)}, u32[]{:S(2)}, u32[]{:S(2)}) %collective-permute-start.7) | collective-permute-done | bytes 1048608 | tf_op jit(solution)/shard_map/ppermute | solution.py:489
  160.8 17.2 %collective-permute-done.40.refs_2_ = bf16[2,128,1024]{2,1,0:T(8,128)(2,1)S(1)} collective-permute-done((bf16[2,128,1024]{2,1,0:T(8,128)(2,1)}, bf16[2,128,1024]{2,1,0:T(8,128)(2,1)S(1)}, u32[]{:S(2)}, u32[]{:S(2)}) %collective-permute-start.40) | collective-permute-done | bytes 524320 | tf_op jit(solution)/shard_map/ppermute | solution.py:493
  180.5 19.5 %collective-permute-done.19.refs_2_ = bf16[128,4096]{1,0:T(8,128)(2,1)} collective-permute-done((bf16[128,4096]{1,0:T(8,128)(2,1)}, bf16[128,4096]{1,0:T(8,128)(2,1)}, u32[]{:S(2)}, u32[]{:S(2)}) %collective-permute-start.19) | collective-permute-done | bytes 1048608 | tf_op jit(solution)/shard_map/ppermute | solution.py:489
  253.1 10.8 %shard_map.307 = bf16[1024,3072]{1,0:T(8,128)(2,1)} custom-call(bf16[1024,1024]{1,0:T(8,128)(2,1)} %bitcast.322, bf16[1024,4096]{1,0:T(8,128)(2,1)} %shard_map.306.w_ref, f32[1,3072]{1,0:T(1,128)} %copy-done.46), custom_call_target="tpu_custom_call" | custom-call | flops 6442450944 | bytes 14680064 | tf_op jit(solution)/shard_map/pallas_call | solution.py:193
  263.8 24.2 %shard_map.308 = (bf16[2,512,1024]{2,1,0:T(8,128)(2,1)}, f32[2,8,2,512]{3,2,1,0:T(2,128)}) custom-call(s32[2]{0:T(128)} %dynamic_slice.345.len_ref, bf16[2,512,3072]{2,1,0:T(8,128)(2,1)} %bitcast.410), custom_call_target="tpu_custom_call" | custom-call | flops 8589934592 | bytes 8493465 | tf_op jit(solution)/shard_map/pallas_call | solution.py:112
  293.3 13.4 %dynamic-slice_reduce_fusion = (bf16[1024,4,128]{2,1,0:T(4,128)(2,1)S(1)}, bf16[1024,4,128]{2,1,0:T(4,128)(2,1)S(1)}) fusion(bf16[1024,4,2,128]{3,2,1,0:T(2,128)(2,1)S(1)} %reshape_reshape.24, s32[]{:T(128)S(6)} %select_n.458, s32[]{:T(128)S(6)} %select_n.457), kind=kLoop, calls=%fused_computation.9 | loop fusion | bytes 4194312 | tf_op jit(solution)/shard_map/dynamic_slice | solution.py:716
  345.9 26.4 %shard_map.311 = (bf16[1024,4096]{1,0:T(8,128)(2,1)}, bf16[1024,4096]{1,0:T(8,128)(2,1)}) custom-call(bf16[1024,1024]{1,0:T(8,128)(2,1)} %get-tuple-element.46.h_ref, bf16[1024,4096]{1,0:T(8,128)(2,1)} %shard_map.310.w_ref.wi_ref, f32[1,4096]{1,0:T(1,128)} %bitcast.393), custom_call_target="tpu_custom_call" | custom-call | flops 8589934592 | bytes 27262976 | tf_op jit(solution)/shard_map/pallas_call | solution.py:275
  380.6 20.9 %shard_map.314 = (bf16[1024,1024]{1,0:T(8,128)(2,1)}, f32[1024,1024]{1,0:T(8,128)}, bf16[1024,1024]{1,0:T(8,128)(2,1)}, f32[8,1024]{1,0:T(8,128)}) custom-call(s32[2]{0:T(128)} %dynamic_slice.345.len_ref, bf16[1024,4096]{1,0:T(8,128)(2,1)} %get-tuple-element.47.a_ref, bf16[4096,1024]{1,0:T(8,128)(2,1)} %shard_map.312.w_ref.wo_ref, ...), custom_call_target="tpu_custom_call" | custom-call | flops 8589934592 | bytes 31457280 | tf_op jit(solution)/shard_map/pallas_call | solution.py:329
  403.9 27.4 %shard_map.316 = (f32[1024,1024]{1,0:T(8,128)}, bf16[2048,1024]{1,0:T(8,128)(2,1)}, bf16[512,2048]{1,0:T(8,128)(2,1)}, bf16[512,2048]{1,0:T(8,128)(2,1)}, f32[1,2048]{1,0:T(1,128)}) custom-call(s32[4]{0:T(128)} %fusion.61.ord_ref, bf16[1024,1024]{1,0:T(8,128)(2,1)} %get-tuple-element.50.g_ref, f32[1024,1024]{1,0:T(8,128)} %get-tuple-element.51.start_ref, ...), custom_call_target="tpu_custom_call" | custom-call | flops 17179869184 | bytes 37748736 | tf_op jit(solution)/shard_map/pallas_call | solution.py:385
  431.3 27.5 %shard_map.317 = (f32[1024,1024]{1,0:T(8,128)}, bf16[2048,1024]{1,0:T(8,128)(2,1)}, bf16[512,2048]{1,0:T(8,128)(2,1)}, bf16[512,2048]{1,0:T(8,128)(2,1)}, f32[1,2048]{1,0:T(1,128)}) custom-call(s32[4]{0:T(128)} %fusion.62.ord_ref, bf16[1024,1024]{1,0:T(8,128)(2,1)} %get-tuple-element.50.g_ref, f32[1024,1024]{1,0:T(8,128)} %get-tuple-element.53.start_ref, ...), custom_call_target="tpu_custom_call" | custom-call | flops 17179869184 | bytes 37748736 | tf_op jit(solution)/shard_map/pallas_call | solution.py:385
  458.9 13.6 %shard_map.318 = (f32[1024,1024]{1,0:T(8,128)}, bf16[1024,1024]{1,0:T(8,128)(2,1)}, bf16[512,1024]{1,0:T(8,128)(2,1)}, bf16[512,1024]{1,0:T(8,128)(2,1)}, f32[8,1024]{1,0:T(8,128)}) custom-call(f32[1024,1024]{1,0:T(8,128)} %get-tuple-element.54.gh_ref, f32[1024,1024]{1,0:T(8,128)} %get-tuple-element.48.hat_ref, f32[1024,1]{1,0:T(8,128)} %get-tuple-element.55.rstd_ref, ...), custom_call_target="tpu_custom_call" | custom-call | flops 4294967296 | bytes 20971520 | tf_op jit(solution)/shard_map/pallas_call | solution.py:434
  472.5 34.0 %shard_map.319 = (bf16[2,512,3072]{2,1,0:T(8,128)(2,1)}, f32[2,8,2,128]{3,2,1,0:T(2,128)}) custom-call(s32[2]{0:T(128)} %dynamic_slice.345.len_ref, bf16[2,512,3072]{2,1,0:T(8,128)(2,1)} %bitcast.411, bf16[2,512,1024]{2,1,0:T(8,128)(2,1)} %bitcast.392, f32[2,8,2,512]{3,2,1,0:T(2,128)} %get-tuple-element.57.lse_ref), custom_call_target="tpu_custom_call" | custom-call | flops 21474836480 | bytes 15728640 | tf_op jit(solution)/shard_map/pallas_call | solution.py:174
  522.6 12.1 %shard_map.320 = bf16[1024,1024]{1,0:T(8,128)(2,1)} custom-call(bf16[1024,3072]{1,0:T(8,128)(2,1)} %bitcast.413, bf16[1024,4096]{1,0:T(8,128)(2,1)} %shard_map.306.w_ref, f32[1024,1024]{1,0:T(8,128)} %get-tuple-element.59.one_ref), custom_call_target="tpu_custom_call" | custom-call | flops 6442450944 | bytes 18874368 | tf_op jit(solution)/shard_map/pallas_call | solution.py:473
  564.4 21.9 %collective-permute-start.46 = (bf16[2,128,1024]{2,1,0:T(8,128)(2,1)S(1)}, bf16[2,128,1024]{2,1,0:T(8,128)(2,1)S(1)}, u32[]{:S(2)}, u32[]{:S(2)}) collective-permute-start(bf16[2,128,1024]{2,1,0:T(8,128)(2,1)S(1)} %copy-done.32), channel_id=1, source_target_pairs={{0,2},{1,3},{2,0},{3,1},{4,6},{5,7},{6,4},{7,5},{8,10},{9,11},{10,... | collective-permute-start | bytes 1572872 | tf_op jit(solution)/shard_map/ppermute | solution.py:493
  586.3 29.0 %collective-permute-done.43.refs_2_ = bf16[2,128,1024]{2,1,0:T(8,128)(2,1)S(1)} collective-permute-done((bf16[2,128,1024]{2,1,0:T(8,128)(2,1)}, bf16[2,128,1024]{2,1,0:T(8,128)(2,1)S(1)}, u32[]{:S(2)}, u32[]{:S(2)}) %collective-permute-start.43) | collective-permute-done | bytes 524320 | tf_op jit(solution)/shard_map/ppermute | solution.py:493
  617.4 23.2 %collective-permute-done.46.refs_2_ = bf16[2,128,1024]{2,1,0:T(8,128)(2,1)S(1)} collective-permute-done((bf16[2,128,1024]{2,1,0:T(8,128)(2,1)S(1)}, bf16[2,128,1024]{2,1,0:T(8,128)(2,1)S(1)}, u32[]{:S(2)}, u32[]{:S(2)}) %collective-permute-start.46) | collective-permute-done | bytes 524320 | tf_op jit(solution)/shard_map/ppermute | solution.py:493
  693.1 9.3 %collective-permute-done.60 = bf16[1,64,5120]{2,1,0:T(8,128)(2,1)} collective-permute-done((bf16[1,64,5120]{2,1,0:T(8,128)(2,1)S(1)}, bf16[1,64,5120]{2,1,0:T(8,128)(2,1)}, u32[]{:S(2)}, u32[]{:S(2)}) %collective-permute-start.60) | collective-permute-done | bytes 655392 | tf_op jit(solution)/shard_map/ppermute | solution.py:489
  738.0 12.4 %collective-permute-done.67 = bf16[2,256,1024]{2,1,0:T(8,128)(2,1)S(1)} collective-permute-done((bf16[2,256,1024]{2,1,0:T(8,128)(2,1)S(1)}, bf16[2,256,1024]{2,1,0:T(8,128)(2,1)S(1)}, u32[]{:S(2)}, u32[]{:S(2)}) %collective-permute-start.67) | collective-permute-done | bytes 1048608 | tf_op jit(solution)/shard_map/ppermute | solution.py:489
  761.2 8.3 %collective-permute-done.68 = bf16[1,256,1024]{2,1,0:T(8,128)(2,1)S(1)} collective-permute-done((bf16[1,256,1024]{2,1,0:T(8,128)(2,1)S(1)}, bf16[1,256,1024]{2,1,0:T(8,128)(2,1)S(1)}, u32[]{:S(2)}, u32[]{:S(2)}) %collective-permute-start.68) | collective-permute-done | bytes 524320 | tf_op jit(solution)/shard_map/ppermute | solution.py:489
  773.2 9.3 %collective-permute-done.71 = bf16[512,512]{1,0:T(8,128)(2,1)S(1)} collective-permute-done((bf16[512,512]{1,0:T(8,128)(2,1)S(1)}, bf16[512,512]{1,0:T(8,128)(2,1)S(1)}, u32[]{:S(2)}, u32[]{:S(2)}) %collective-permute-start.71) | collective-permute-done | bytes 524320 | tf_op jit(solution)/shard_map/ppermute | solution.py:626
  (425 shorter events, 339.6 us)
Async XLA Ops:
  13.8 116.5 %collective-permute-start.2 = (bf16[2,128,1024]{2,1,0:T(8,128)(2,1)S(1)}, bf16[2,128,1024]{2,1,0:T(8,128)(2,1)S(1)}, u32[]{:S(2)}, u32[]{:S(2)}) collective-permute-start(bf16[2,128,1024]{2,1,0:T(8,128)(2,1)S(1)} %get-tuple-element.143), channel_id=1, source_target_pairs={{0,3},{1,0},{2,1},{3,2},{4,7},{5,4},{6,5},{7,6},{8,11},{9,8},{10,9... | collective-permute-start | bytes 1572872 | tf_op jit(solution)/shard_map/ppermute | solution.py:493
  16.3 114.2 %collective-permute-start = (bf16[2,128,1024]{2,1,0:T(8,128)(2,1)S(1)}, bf16[2,128,1024]{2,1,0:T(8,128)(2,1)S(1)}, u32[]{:S(2)}, u32[]{:S(2)}) collective-permute-start(bf16[2,128,1024]{2,1,0:T(8,128)(2,1)S(1)} %get-tuple-element.144), channel_id=1, source_target_pairs={{0,1},{1,2},{2,3},{3,0},{4,5},{5,6},{6,7},{7,4},{8,9},{9,10},{10,1... | collective-permute-start | bytes 1572872 | tf_op jit(solution)/shard_map/ppermute | solution.py:493
  27.6 105.8 %collective-permute-start.1 = (bf16[2,128,1024]{2,1,0:T(8,128)(2,1)S(1)}, bf16[2,128,1024]{2,1,0:T(8,128)(2,1)S(1)}, u32[]{:S(2)}, u32[]{:S(2)}) collective-permute-start(bf16[2,128,1024]{2,1,0:T(8,128)(2,1)S(1)} %get-tuple-element.146), channel_id=1, source_target_pairs={{0,2},{1,3},{2,0},{3,1},{4,6},{5,7},{6,4},{7,5},{8,10},{9,11},{10,... | collective-permute-start | bytes 1572872 | tf_op jit(solution)/shard_map/ppermute | solution.py:493
  69.5 64.7 %collective-permute-start.41 = (bf16[2,128,1024]{2,1,0:T(8,128)(2,1)S(1)}, bf16[2,128,1024]{2,1,0:T(8,128)(2,1)}, u32[]{:S(2)}, u32[]{:S(2)}) collective-permute-start(bf16[2,128,1024]{2,1,0:T(8,128)(2,1)S(1)} %get-tuple-element.139), channel_id=1, source_target_pairs={{0,3},{1,0},{2,1},{3,2},{4,7},{5,4},{6,5},{7,6},{8,11},{9,8},{10,9... | collective-permute-start | bytes 1572872 | tf_op jit(solution)/shard_map/ppermute | solution.py:493
  134.2 45.4 %collective-permute-start.30 = (bf16[512,1024]{1,0:T(8,128)(2,1)S(1)}, bf16[512,1024]{1,0:T(8,128)(2,1)S(1)}, u32[]{:S(2)}, u32[]{:S(2)}) collective-permute-start(bf16[512,1024]{1,0:T(8,128)(2,1)S(1)} %pad_maximum_fusion.4.refs_0_), channel_id=1, source_target_pairs={{0,8},{4,12},{8,0},{12,4},{16,24},{20,28},{24,16},{28,20},{1,9},{5... | collective-permute-start | bytes 3145736 | tf_op jit(solution)/shard_map/ppermute | solution.py:489
  144.6 55.3 %collective-permute-start.19 = (bf16[128,4096]{1,0:T(8,128)(2,1)}, bf16[128,4096]{1,0:T(8,128)(2,1)}, u32[]{:S(2)}, u32[]{:S(2)}) collective-permute-start(bf16[128,4096]{1,0:T(8,128)(2,1)} %pad_maximum_fusion.3.refs_0_), channel_id=1, source_target_pairs={{0,16},{4,20},{8,24},{12,28},{16,0},{20,4},{24,8},{28,12},{1,17},{... | collective-permute-start | bytes 3145736 | tf_op jit(solution)/shard_map/ppermute | solution.py:489
  155.0 47.0 %collective-permute-start.18 = (bf16[128,4096]{1,0:T(8,128)(2,1)}, bf16[128,4096]{1,0:T(8,128)(2,1)}, u32[]{:S(2)}, u32[]{:S(2)}) collective-permute-start(bf16[128,4096]{1,0:T(8,128)(2,1)} %pad_maximum_fusion.3.refs_0_), channel_id=1, source_target_pairs={{0,8},{4,12},{8,0},{12,4},{16,24},{20,28},{24,16},{28,20},{1,9},{5... | collective-permute-start | bytes 3145736 | tf_op jit(solution)/shard_map/ppermute | solution.py:489
  178.0 65.2 %collective-permute-start.10 = (bf16[128,4096]{1,0:T(8,128)(2,1)}, bf16[128,4096]{1,0:T(8,128)(2,1)}, u32[]{:S(2)}, u32[]{:S(2)}) collective-permute-start(bf16[128,4096]{1,0:T(8,128)(2,1)} %constant_dynamic-update-slice_fusion.7.refs_0_), channel_id=1, source_target_pairs={{0,4},{4,0},{8,12},{12,8},{16,20},{20,16},{24,28},{28,24},{1,5},{5... | collective-permute-start | bytes 3145736 | tf_op jit(solution)/shard_map/ppermute | solution.py:489
  243.2 48.1 %collective-permute-start.22 = (bf16[128,4096]{1,0:T(8,128)(2,1)}, bf16[128,4096]{1,0:T(8,128)(2,1)}, u32[]{:S(2)}, u32[]{:S(2)}) collective-permute-start(bf16[128,4096]{1,0:T(8,128)(2,1)} %pad_maximum_fusion.3.refs_0_), channel_id=1, source_target_pairs={{0,4},{4,0},{8,12},{12,8},{16,20},{20,16},{24,28},{28,24},{1,5},{5... | collective-permute-start | bytes 3145736 | tf_op jit(solution)/shard_map/ppermute | solution.py:489
  243.2 49.6 %collective-permute-start.33 = (bf16[256,1024]{1,0:T(8,128)(2,1)}, bf16[256,1024]{1,0:T(8,128)(2,1)}, u32[]{:S(2)}, u32[]{:S(2)}) collective-permute-start(bf16[256,1024]{1,0:T(8,128)(2,1)} %slice.433), channel_id=1, source_target_pairs={{0,8},{4,12},{8,0},{12,4},{16,24},{20,28},{24,16},{28,20},{1,9},{5... | collective-permute-start | bytes 1572872 | tf_op jit(solution)/shard_map/ppermute | solution.py:489
  244.8 48.3 %collective-permute-start.21 = (bf16[64,4096]{1,0:T(8,128)(2,1)}, bf16[64,4096]{1,0:T(8,128)(2,1)}, u32[]{:S(2)}, u32[]{:S(2)}) collective-permute-start(bf16[64,4096]{1,0:T(8,128)(2,1)} %slice.429), channel_id=1, source_target_pairs={{0,8},{4,12},{8,0},{12,4},{16,24},{20,28},{24,16},{28,20},{1,9},{5... | collective-permute-start | bytes 1572872 | tf_op jit(solution)/shard_map/ppermute | solution.py:489
  245.3 61.4 %collective-permute-start.20 = (bf16[64,4096]{1,0:T(8,128)(2,1)}, bf16[64,4096]{1,0:T(8,128)(2,1)}, u32[]{:S(2)}, u32[]{:S(2)}) collective-permute-start(bf16[64,4096]{1,0:T(8,128)(2,1)} %slice.428), channel_id=1, source_target_pairs={{0,16},{4,20},{8,24},{12,28},{16,0},{20,4},{24,8},{28,12},{1,17},{... | collective-permute-start | bytes 1572872 | tf_op jit(solution)/shard_map/ppermute | solution.py:489
  245.8 75.6 %collective-permute-start.24 = (bf16[128,4096]{1,0:T(8,128)(2,1)}, bf16[128,4096]{1,0:T(8,128)(2,1)}, u32[]{:S(2)}, u32[]{:S(2)}) collective-permute-start(bf16[128,4096]{1,0:T(8,128)(2,1)} %collective-permute-done.19.refs_2_), channel_id=1, source_target_pairs={{0,4},{4,0},{8,12},{12,8},{16,20},{20,16},{24,28},{28,24},{1,5},{5... | collective-permute-start | bytes 3145736 | tf_op jit(solution)/shard_map/ppermute | solution.py:489
  292.8 45.7 %collective-permute-start.23 = (bf16[128,4096]{1,0:T(8,128)(2,1)}, bf16[128,4096]{1,0:T(8,128)(2,1)}, u32[]{:S(2)}, u32[]{:S(2)}) collective-permute-start(bf16[128,4096]{1,0:T(8,128)(2,1)} %collective-permute-done.18.refs_1_), channel_id=1, source_target_pairs={{0,4},{4,0},{8,12},{12,8},{16,20},{20,16},{24,28},{28,24},{1,5},{5... | collective-permute-start | bytes 3145736 | tf_op jit(solution)/shard_map/ppermute | solution.py:489
  320.8 51.6 %collective-permute-start.34 = (bf16[512,1024]{1,0:T(8,128)(2,1)S(1)}, bf16[512,1024]{1,0:T(8,128)(2,1)}, u32[]{:S(2)}, u32[]{:S(2)}) collective-permute-start(bf16[512,1024]{1,0:T(8,128)(2,1)S(1)} %pad_maximum_fusion.4.refs_0_), channel_id=1, source_target_pairs={{0,4},{4,0},{8,12},{12,8},{16,20},{20,16},{24,28},{28,24},{1,5},{5... | collective-permute-start | bytes 3145736 | tf_op jit(solution)/shard_map/ppermute | solution.py:489
  321.1 51.3 %collective-permute-start.36 = (bf16[512,1024]{1,0:T(8,128)(2,1)}, bf16[512,1024]{1,0:T(8,128)(2,1)}, u32[]{:S(2)}, u32[]{:S(2)}) collective-permute-start(bf16[512,1024]{1,0:T(8,128)(2,1)} %copy-done.7), channel_id=1, source_target_pairs={{0,4},{4,0},{8,12},{12,8},{16,20},{20,16},{24,28},{28,24},{1,5},{5... | collective-permute-start | bytes 3145736 | tf_op jit(solution)/shard_map/ppermute | solution.py:489
  321.4 51.1 %collective-permute-start.35 = (bf16[512,1024]{1,0:T(8,128)(2,1)}, bf16[512,1024]{1,0:T(8,128)(2,1)}, u32[]{:S(2)}, u32[]{:S(2)}) collective-permute-start(bf16[512,1024]{1,0:T(8,128)(2,1)} %copy-done.9), channel_id=1, source_target_pairs={{0,4},{4,0},{8,12},{12,8},{16,20},{20,16},{24,28},{28,24},{1,5},{5... | collective-permute-start | bytes 3145736 | tf_op jit(solution)/shard_map/ppermute | solution.py:489
  534.7 119.0 %collective-permute-start.48 = (bf16[512,3072]{1,0:T(8,128)(2,1)}, bf16[512,3072]{1,0:T(8,128)(2,1)}, u32[]{:S(2)}, u32[]{:S(2)}) collective-permute-start(bf16[512,3072]{1,0:T(8,128)(2,1)} %convolution_convert_fusion), channel_id=1, source_target_pairs={{0,4},{4,0},{8,12},{12,8},{16,20},{20,16},{24,28},{28,24},{1,5},{5... | collective-permute-start | bytes 9437192 | tf_op jit(solution)/shard_map/ppermute | solution.py:489
  551.6 63.7 %collective-permute-start.43 = (bf16[2,128,1024]{2,1,0:T(8,128)(2,1)}, bf16[2,128,1024]{2,1,0:T(8,128)(2,1)S(1)}, u32[]{:S(2)}, u32[]{:S(2)}) collective-permute-start(bf16[2,128,1024]{2,1,0:T(8,128)(2,1)} %get-tuple-element.136), channel_id=1, source_target_pairs={{0,2},{1,3},{2,0},{3,1},{4,6},{5,7},{6,4},{7,5},{8,10},{9,11},{10,... | collective-permute-start | bytes 1572872 | tf_op jit(solution)/shard_map/ppermute | solution.py:493
  554.1 95.7 %collective-permute-start.42 = (bf16[2,128,1024]{2,1,0:T(8,128)(2,1)S(1)}, bf16[2,128,1024]{2,1,0:T(8,128)(2,1)S(1)}, u32[]{:S(2)}, u32[]{:S(2)}) collective-permute-start(bf16[2,128,1024]{2,1,0:T(8,128)(2,1)S(1)} %get-tuple-element.137), channel_id=1, source_target_pairs={{0,1},{1,2},{2,3},{3,0},{4,5},{5,6},{6,7},{7,4},{8,9},{9,10},{10,1... | collective-permute-start | bytes 1572872 | tf_op jit(solution)/shard_map/ppermute | solution.py:493
  557.4 59.1 %collective-permute-start.47 = (bf16[2,128,1024]{2,1,0:T(8,128)(2,1)S(1)}, bf16[2,128,1024]{2,1,0:T(8,128)(2,1)S(1)}, u32[]{:S(2)}, u32[]{:S(2)}) collective-permute-start(bf16[2,128,1024]{2,1,0:T(8,128)(2,1)S(1)} %copy-done.33), channel_id=1, source_target_pairs={{0,3},{1,0},{2,1},{3,2},{4,7},{5,4},{6,5},{7,6},{8,11},{9,8},{10,9... | collective-permute-start | bytes 1572872 | tf_op jit(solution)/shard_map/ppermute | solution.py:493
  564.4 76.2 %collective-permute-start.46 = (bf16[2,128,1024]{2,1,0:T(8,128)(2,1)S(1)}, bf16[2,128,1024]{2,1,0:T(8,128)(2,1)S(1)}, u32[]{:S(2)}, u32[]{:S(2)}) collective-permute-start(bf16[2,128,1024]{2,1,0:T(8,128)(2,1)S(1)} %copy-done.32), channel_id=1, source_target_pairs={{0,2},{1,3},{2,0},{3,1},{4,6},{5,7},{6,4},{7,5},{8,10},{9,11},{10,... | collective-permute-start | bytes 1572872 | tf_op jit(solution)/shard_map/ppermute | solution.py:493
  616.5 48.3 %collective-permute-start.59 = (bf16[2,64,5120]{2,1,0:T(8,128)(2,1)}, bf16[2,64,5120]{2,1,0:T(8,128)(2,1)}, u32[]{:S(2)}, u32[]{:S(2)}) collective-permute-start(bf16[2,64,5120]{2,1,0:T(8,128)(2,1)} %pad_maximum_fusion.1), channel_id=1, source_target_pairs={{0,8},{4,12},{8,0},{12,4},{16,24},{20,28},{24,16},{28,20},{1,9},{5... | collective-permute-start | bytes 3932168 | tf_op jit(solution)/shard_map/ppermute | solution.py:489
  641.8 63.2 %collective-permute-start.66 = (bf16[2048,1024]{1,0:T(8,128)(2,1)}, bf16[2048,1024]{1,0:T(8,128)(2,1)}, u32[]{:S(2)}, u32[]{:S(2)}) collective-permute-start(bf16[2048,1024]{1,0:T(8,128)(2,1)} %get-tuple-element.67), channel_id=1, source_target_pairs={{0,4},{4,0},{8,12},{12,8},{16,20},{20,16},{24,28},{28,24},{1,5},{5... | collective-permute-start | bytes 12582920 | tf_op jit(solution)/shard_map/ppermute | solution.py:489
  (104 other events, 2488.1 us)

commit v2 on v1

v2 whole, which is shorter than its diff:
```python
import functools

import jax
import jax.numpy as jnp
from jax import lax
from jax.experimental import pallas as pl
from jax.experimental.pallas import tpu as pltpu
from jax.sharding import PartitionSpec as P

HEAD_DIM = 64
PAIR = 128
EPS = 1e-05
SCALE = 0.125
LOG2E = 1.4426950408889634
VMEM = 56 * 1024 * 1024

f32 = jnp.float32
bf16 = jnp.bfloat16


def params():
    return pltpu.CompilerParams(vmem_limit_bytes=VMEM)


def cost(flops, moved, special=0):
    return pl.CostEstimate(flops=int(flops * 12), bytes_accessed=int(moved * 12), transcendentals=int(special * 12))


ANY = pl.BlockSpec(memory_space=pl.ANY)


def mm(a, b):
    return jnp.dot(a, b, preferred_element_type=f32)


def mm_nt(a, b):
    return lax.dot_general(a, b, (((1,), (1,)), ((), ())), preferred_element_type=f32)


def mm_tn(a, b):
    return lax.dot_general(a, b, (((0,), (0,)), ((), ())), preferred_element_type=f32)


def place(parts, starts, out_shape, puts):
    count = len(puts)

    def kernel(starts_ref, *refs):
        ins, out, held, sems_in, sems_out = refs[: len(parts)], *refs[len(parts) :]
        arriving, leaving = [], []
        for n, (part, which, where) in enumerate(puts):
            arriving.append(pltpu.make_async_copy(ins[part], where(held, starts_ref[which]), sems_in.at[n]))
            arriving[-1].start()
        for n, (part, which, where) in enumerate(puts):
            start = starts_ref[which]
            arriving[n].wait()
            leaving.append(pltpu.make_async_copy(where(held, start), where(out, start), sems_out.at[n]))
            leaving[-1].start()
        for copy in leaving:
            copy.wait()

    size = sum(p.size * p.dtype.itemsize for p in parts)
    return pl.pallas_call(
        kernel,
        grid_spec=pltpu.PrefetchScalarGridSpec(
            num_scalar_prefetch=1,
            grid=(1,),
            in_specs=[pl.BlockSpec(memory_space=pl.ANY)] * len(parts),
            out_specs=pl.BlockSpec(memory_space=pl.ANY),
            scratch_shapes=[
                pltpu.VMEM(out_shape.shape, out_shape.dtype),
                pltpu.SemaphoreType.DMA((count,)),
                pltpu.SemaphoreType.DMA((count,)),
            ],
        ),
        out_shape=out_shape,
        compiler_params=params(),
        cost_estimate=cost(0, 2 * size),
    )(starts, *parts)


def attention_forward(qkv, lengths):
    seqs, slots, three = qkv.shape
    pairs = three // (3 * PAIR)

    def kernel(len_ref, qkv_ref, out_ref, lse_ref):
        valid_count = len_ref[pl.program_id(0)]
        q2 = qkv_ref[0, :, 0:PAIR]
        k2 = qkv_ref[0, :, PAIR : 2 * PAIR]
        vt = qkv_ref[0, :, 2 * PAIR : 3 * PAIR].T
        lane = lax.broadcasted_iota(jnp.int32, (slots, PAIR), 1)
        row = lax.broadcasted_iota(jnp.int32, (slots, slots), 0)
        halves = []
        for h in range(2):
            qh = jnp.where((lane < HEAD_DIM) == (h == 0), q2, jnp.zeros_like(q2))
            st = mm_nt(k2, qh) * (SCALE * LOG2E)
            st = jnp.where(row < valid_count, st, -1e30)
            top = jnp.max(st, axis=0, keepdims=True)
            p = jnp.exp2(st - top)
            total = jnp.sum(p, axis=0, keepdims=True)
            p_low = (p * (1.0 / total)).astype(bf16)
            halves.append(mm(vt[h * HEAD_DIM : (h + 1) * HEAD_DIM, :], p_low))
            lse_ref[0, 0, h : h + 1, :] = top + jnp.log2(total)
        out_ref[0] = jnp.concatenate(halves, axis=0).T.astype(bf16)

    grid_spec = pltpu.PrefetchScalarGridSpec(
        num_scalar_prefetch=1,
        grid=(seqs, pairs),
        in_specs=[pl.BlockSpec((1, slots, 3 * PAIR), lambda s, j, n: (s, 0, j))],
        out_specs=[
            pl.BlockSpec((1, slots, PAIR), lambda s, j, n: (s, 0, j)),
            pl.BlockSpec((1, 1, 2, slots), lambda s, j, n: (s, j, 0, 0)),
        ],
    )
    work = seqs * pairs * 2 * slots * slots
    return pl.pallas_call(
        kernel,
        grid_spec=grid_spec,
        out_shape=[
            jax.ShapeDtypeStruct((seqs, slots, pairs * PAIR), bf16),
            jax.ShapeDtypeStruct((seqs, pairs, 2, slots), f32),
        ],
        compiler_params=params(),
        cost_estimate=cost(work * 4 * PAIR * 2, qkv.size * 2.7, work),
    )(lengths, qkv)


def attention_backward(qkv, grad_heads, lse, lengths, seq, waits=()):
    _, slots, three = qkv.shape
    pairs = three // (3 * PAIR)

    def kernel(len_ref, qkv_ref, gh_ref, lse_ref, *refs):
        out_ref, sums_ref = refs[-2:]
        valid_count = len_ref[seq]
        q2 = qkv_ref[0, :, 0:PAIR]
        k2 = qkv_ref[0, :, PAIR : 2 * PAIR]
        v2 = qkv_ref[0, :, 2 * PAIR : 3 * PAIR]
        g2 = gh_ref[...]
        kt = k2.T
        lane = lax.broadcasted_iota(jnp.int32, (slots, PAIR), 1)
        row = lax.broadcasted_iota(jnp.int32, (slots, slots), 0)
        grad_k, grad_v, grad_q = [], [], []
        for h in range(2):
            mine = (lane < HEAD_DIM) == (h == 0)
            qh = jnp.where(mine, q2, jnp.zeros_like(q2))
            gh = jnp.where(mine, g2, jnp.zeros_like(g2))
            st = mm_nt(k2, qh) * (SCALE * LOG2E)
            p = jnp.exp2(st - lse_ref[0, 0, h : h + 1, :])
            p = jnp.where(row < valid_count, p, 0.0)
            dp = mm_nt(v2, gh)
            inner_sum = jnp.sum(p * dp, axis=0, keepdims=True)
            ds = (p * (dp - inner_sum)).astype(bf16)
            grad_v.append(mm(p.astype(bf16), g2))
            grad_k.append(mm(ds, q2))
            grad_q.append(mm(kt[h * HEAD_DIM : (h + 1) * HEAD_DIM, :], ds))
        gq = (jnp.concatenate(grad_q, axis=0).T * SCALE).astype(bf16)
        gk = (jnp.where(lane < HEAD_DIM, grad_k[0], grad_k[1]) * SCALE).astype(bf16)
        gv = jnp.where(lane < HEAD_DIM, grad_v[0], grad_v[1]).astype(bf16)
        out_ref[:, 0:PAIR] = gq
        out_ref[:, PAIR : 2 * PAIR] = gk
        out_ref[:, 2 * PAIR : 3 * PAIR] = gv
        sums_ref[0, 0:1, :] = jnp.sum(gq.astype(f32), axis=0, keepdims=True)
        sums_ref[0, 1:2, :] = jnp.sum(gv.astype(f32), axis=0, keepdims=True)

    grid_spec = pltpu.PrefetchScalarGridSpec(
        num_scalar_prefetch=1,
        grid=(pairs,),
        in_specs=[
            pl.BlockSpec((1, slots, 3 * PAIR), lambda j, n: (seq, 0, j)),
            pl.BlockSpec((slots, PAIR), lambda j, n: (seq, j)),
            pl.BlockSpec((1, 1, 2, slots), lambda j, n: (seq, j, 0, 0)),
        ]
        + [ANY] * len(waits),
        out_specs=[
            pl.BlockSpec((slots, 3 * PAIR), lambda j, n: (0, j)),
            pl.BlockSpec((1, 2, PAIR), lambda j, n: (j, 0, 0)),
        ],
    )
    work = pairs * 2 * slots * slots
    return pl.pallas_call(
        kernel,
        grid_spec=grid_spec,
        out_shape=[
            jax.ShapeDtypeStruct((slots, three), bf16),
            jax.ShapeDtypeStruct((pairs, 2, PAIR), f32),
        ],
        compiler_params=params(),
        cost_estimate=cost(work * 10 * PAIR * 2, slots * three * 5, work),
    )(lengths, qkv, grad_heads, lse, *waits)


def project(x, w, bias, waits=(), cols=768):
    rows, depth = x.shape
    width = bias.shape[1]

    def kernel(x_ref, w_ref, b_ref, *refs):
        refs[-1][...] = (mm(x_ref[...], w_ref[...]) + b_ref[...]).astype(bf16)

    return pl.pallas_call(
        kernel,
        grid=(width // cols,),
        in_specs=[
            pl.BlockSpec((rows, depth), lambda j: (0, 0)),
            pl.BlockSpec((depth, cols), lambda j: (0, j)),
            pl.BlockSpec((1, cols), lambda j: (0, j)),
        ]
        + [ANY] * len(waits),
        out_specs=pl.BlockSpec((rows, cols), lambda j: (0, j)),
        out_shape=jax.ShapeDtypeStruct((rows, width), bf16),
        compiler_params=params(),
        cost_estimate=cost(2 * rows * depth * width, 2 * (x.size + depth * width + rows * width)),
    )(x, w, bias, *waits)


def normed(summed):
    centred = summed - jnp.mean(summed, axis=-1, keepdims=True)
    rstd = lax.rsqrt(jnp.mean(centred * centred, axis=-1, keepdims=True) + EPS)
    return centred * rstd, rstd


def norm_back(grad_hat, hat, rstd):
    return rstd * (
        grad_hat
        - jnp.mean(grad_hat, axis=-1, keepdims=True)
        - hat * jnp.mean(grad_hat * hat, axis=-1, keepdims=True)
    )


def joined(w_ref, c, cols=slice(None)):
    part = w_ref[:, c, :, cols]
    return part.reshape(part.shape[0] * part.shape[1], part.shape[2])


def reordered(ref, features, first=0, count=8, block=128):
    parts = []
    for k in range(first, first + count):
        start = pl.multiple_of(features[k] * block, block)
        parts.append(ref[:, pl.ds(start, block)].T)
    return jnp.concatenate(parts, axis=0)


def out_forward(heads, w_mid, x, b_out, gain, shift, features, rows=256):
    total, width = x.shape
    blocks, ctx, depth, _ = w_mid.shape
    cols = width // ctx

    def kernel(feat_ref, h_ref, w_ref, x_ref, b_ref, g_ref, s_ref, hat_ref, rstd_ref, low_ref, turned_ref):
        h = h_ref[...]
        attended = jnp.concatenate([mm(h, joined(w_ref, c)) for c in range(ctx)], axis=1)
        summed = attended + b_ref[...] + x_ref[...].astype(f32)
        hat, rstd = normed(summed)
        hat_ref[...] = hat
        rstd_ref[...] = rstd
        low_ref[...] = (hat * g_ref[...] + s_ref[...]).astype(bf16)
        turned_ref[...] = reordered(low_ref, feat_ref)

    block = pl.BlockSpec((rows, width), lambda i, f: (i, 0))
    vec = pl.BlockSpec((1, width), lambda i, f: (0, 0))
    weight = pl.BlockSpec((blocks, ctx, depth, cols), lambda i, f: (0, 0, 0, 4))
    grid_spec = pltpu.PrefetchScalarGridSpec(
        num_scalar_prefetch=1,
        grid=(total // rows,),
        in_specs=[block, weight, block, vec, vec, vec],
        out_specs=[
            block,
            pl.BlockSpec((rows, 1), lambda i, f: (i, 0)),
            block,
            pl.BlockSpec((width, rows), lambda i, f: (0, i)),
        ],
    )
    return pl.pallas_call(
        kernel,
        grid_spec=grid_spec,
        out_shape=[
            jax.ShapeDtypeStruct((total, width), f32),
            jax.ShapeDtypeStruct((total, 1), f32),
            jax.ShapeDtypeStruct((total, width), bf16),
            jax.ShapeDtypeStruct((width, total), bf16),
        ],
        compiler_params=params(),
        cost_estimate=cost(2 * total * width * width, total * width * 12 + width * width * 2),
    )(features, heads, w_mid, x, b_out, gain, shift)


def gelu_pair(x):
    density = jnp.exp2(x * x * (-0.5 * LOG2E))
    t = 1.0 / (jnp.abs(x) * (0.3275911 * 0.7071067811865476) + 1.0)
    poly = 1.061405429 * 0.5
    for coefficient in (-1.453152027, 1.421413741, -0.284496736, 0.254829592):
        poly = poly * t + coefficient * 0.5
    tail = poly * t * density
    phi = jnp.where(x < 0, tail, 1.0 - tail)
    active = x * phi
    slope = phi + x * density * 0.3989422804014327
    return active, slope


def ffn_one(hidden, w_mid, b_inner, cols=512, chunk=256):
    rows, depth = hidden.shape
    width = b_inner.shape[1]
    blocks, ctx, deep, _ = w_mid.shape
    per = width // ctx // cols

    def kernel(h_ref, w_ref, b_ref, act_ref, slope_ref):
        w = joined(w_ref, 0)
        for c in range(rows // chunk):
            part = pl.ds(c * chunk, chunk)
            inner = mm(h_ref[part, :], w) + b_ref[...]
            active, slope = gelu_pair(inner)
            act_ref[part, :] = active.astype(bf16)
            slope_ref[part, :] = slope.astype(bf16)

    out = pl.BlockSpec((rows, cols), lambda j: (0, j))
    return pl.pallas_call(
        kernel,
        grid=(width // cols,),
        in_specs=[
            pl.BlockSpec((rows, depth), lambda j: (0, 0)),
            pl.BlockSpec((blocks, 1, deep, cols), lambda j: (0, j // per, 0, j % per)),
            pl.BlockSpec((1, cols), lambda j: (0, j)),
        ],
        out_specs=[out, out],
        out_shape=[jax.ShapeDtypeStruct((rows, width), bf16)] * 2,
        compiler_params=params(),
        cost_estimate=cost(2 * rows * depth * width, 2 * (hidden.size + depth * width + 2 * rows * width), 2 * rows * width),
    )(hidden, w_mid, b_inner)


def ffn_two(active, w_outer, hat_one, cot, lengths, vectors, slots, rows=256):
    total, depth = active.shape
    width = hat_one.shape[1]
    ctx = w_outer.shape[1]
    per_seq = slots // rows

    def kernel(len_ref, a_ref, w_ref, hat_ref, cot_ref, vec_ref, mixed_ref, grad_ref, low_ref, sums_ref):
        i = pl.program_id(0)
        g_one, s_one, b_outer, g_two, s_two = (vec_ref[k : k + 1, :] for k in range(5))
        a = a_ref[...]
        outer = jnp.concatenate([mm(a, joined(w_ref, c)) for c in range(ctx)], axis=1)
        summed = outer + b_outer + (hat_ref[...] * g_one + s_one)
        hat, rstd = normed(summed)
        mixed_ref[...] = (hat * g_two + s_two).astype(bf16)
        slot = (i % per_seq) * rows + lax.broadcasted_iota(jnp.int32, (rows, width), 0)
        grad_y = jnp.where(slot < len_ref[i // per_seq], cot_ref[...].astype(f32), 0.0)
        grad = norm_back(grad_y * g_two, hat, rstd)
        grad_ref[...] = grad
        low = grad.astype(bf16)
        low_ref[...] = low

        @pl.when(i == 0)
        def _():
            sums_ref[...] = jnp.zeros_like(sums_ref)

        sums_ref[0:1, :] += jnp.sum(grad_y * hat, axis=0, keepdims=True)
        sums_ref[1:2, :] += jnp.sum(grad_y, axis=0, keepdims=True)
        sums_ref[2:3, :] += jnp.sum(low.astype(f32), axis=0, keepdims=True)

    block = pl.BlockSpec((rows, width), lambda i, n: (i, 0))
    grid_spec = pltpu.PrefetchScalarGridSpec(
        num_scalar_prefetch=1,
        grid=(total // rows,),
        in_specs=[
            pl.BlockSpec((rows, depth), lambda i, n: (i, 0)),
            pl.BlockSpec(w_outer.shape, lambda i, n: (0, 0, 0, 0)),
            block,
            block,
            pl.BlockSpec((8, width), lambda i, n: (0, 0)),
        ],
        out_specs=[block, block, block, pl.BlockSpec((8, width), lambda i, n: (0, 0))],
    )
    return pl.pallas_call(
        kernel,
        grid_spec=grid_spec,
        out_shape=[
            jax.ShapeDtypeStruct((total, width), bf16),
            jax.ShapeDtypeStruct((total, width), f32),
            jax.ShapeDtypeStruct((total, width), bf16),
            jax.ShapeDtypeStruct((8, width), f32),
        ],
        compiler_params=params(),
        cost_estimate=cost(2 * total * width * depth, active.size * 2 + w_outer.size * 2 + total * width * 14),
    )(lengths, active, w_outer, hat_one, cot, vectors)


def ffn_back(grad_low, start, hidden_t, active, slope, w_outer, w_mid, order, waits=(), cols=512):
    rows, width = grad_low.shape
    count = order.shape[0]
    half = width // 2
    blocks, ctx, deep, _ = w_mid.shape
    per = active.shape[1] // ctx // cols
    outer_rows = w_outer.shape[2]
    outer_cols = w_outer.shape[3]

    def kernel(ord_ref, g_ref, start_ref, ht_ref, a_ref, s_ref, wo_ref, wi_ref, *refs):
        grad_ref, dwo_ref, dws_ref, dwk_ref, bias_ref = refs[-5:]
        j = pl.program_id(0)
        grad = g_ref[...]
        grad_active = sum(
            mm_nt(grad[:, c * outer_cols : (c + 1) * outer_cols], joined(wo_ref, c)) for c in range(ctx)
        )
        inner = (grad_active * s_ref[...].astype(f32)).astype(bf16)
        bias_ref[...] = jnp.sum(inner.astype(f32), axis=0, keepdims=True)
        dwo_ref[...] = mm_tn(a_ref[...], grad).astype(bf16)
        dws_ref[...] = mm(ht_ref[0:half, :], inner).astype(bf16)
        dwk_ref[...] = mm(ht_ref[half:width, :], inner).astype(bf16)

        @pl.when(j == 0)
        def _():
            grad_ref[...] = start_ref[...]

        grad_ref[...] += mm_nt(inner, joined(wi_ref, 0))

    whole = lambda j, o: (0, 0)
    grid_spec = pltpu.PrefetchScalarGridSpec(
        num_scalar_prefetch=1,
        grid=(count,),
        in_specs=[
            pl.BlockSpec((rows, width), whole),
            pl.BlockSpec((rows, width), whole),
            pl.BlockSpec((width, rows), whole),
            pl.BlockSpec((rows, cols), lambda j, o: (0, o[j])),
            pl.BlockSpec((rows, cols), lambda j, o: (0, o[j])),
            pl.BlockSpec((cols // outer_rows, ctx, outer_rows, outer_cols), lambda j, o: (o[j], 0, 0, 0)),
            pl.BlockSpec((blocks, 1, deep, cols), lambda j, o: (0, o[j] // per, 0, o[j] % per)),
        ]
        + [ANY] * len(waits),
        out_specs=[
            pl.BlockSpec((rows, width), whole),
            pl.BlockSpec((cols, width), lambda j, o: (j, 0)),
            pl.BlockSpec((half, cols), lambda j, o: (0, j)),
            pl.BlockSpec((half, cols), lambda j, o: (0, j)),
            pl.BlockSpec((1, cols), lambda j, o: (0, j)),
        ],
    )
    return pl.pallas_call(
        kernel,
        grid_spec=grid_spec,
        out_shape=[
            jax.ShapeDtypeStruct((rows, width), f32),
            jax.ShapeDtypeStruct((count * cols, width), bf16),
            jax.ShapeDtypeStruct((half, count * cols), bf16),
            jax.ShapeDtypeStruct((half, count * cols), bf16),
            jax.ShapeDtypeStruct((1, count * cols), f32),
        ],
        compiler_params=params(),
        cost_estimate=cost(8 * rows * width * count * cols, 12 * count * cols * width + 12 * rows * width),
    )(order, grad_low, start, hidden_t, active, slope, w_outer, w_mid, *waits)


def out_back(grad_hidden, hat, rstd, gain, w_mid, heads, features, waits=(), rows=256):
    total, width = grad_hidden.shape
    half = width // 2
    steps = total // rows
    blocks, ctx, depth, _ = w_mid.shape
    cols = width // ctx

    def kernel(feat_ref, gh_ref, hat_ref, rstd_ref, gain_ref, w_ref, h_ref, *refs):
        one_ref, heads_ref, dws_ref, dwk_ref, sums_ref, acc = refs[-6:]
        i = pl.program_id(0)
        grad_y = gh_ref[...]
        hat = hat_ref[...]
        grad = norm_back(grad_y * gain_ref[...], hat, rstd_ref[...])
        one_ref[...] = grad
        low = grad.astype(bf16)
        heads_ref[...] = sum(mm_nt(low[:, c * cols : (c + 1) * cols], joined(w_ref, c)) for c in range(ctx)).astype(bf16)

        @pl.when(i == 0)
        def _():
            sums_ref[...] = jnp.zeros_like(sums_ref)
            acc[...] = jnp.zeros_like(acc)

        acc[...] += mm(reordered(h_ref, feat_ref), low)
        sums_ref[0:1, :] += jnp.sum(grad_y * hat, axis=0, keepdims=True)
        sums_ref[1:2, :] += jnp.sum(grad_y, axis=0, keepdims=True)
        sums_ref[2:3, :] += jnp.sum(low.astype(f32), axis=0, keepdims=True)

        @pl.when(i == steps - 1)
        def _():
            dws_ref[...] = acc[0:half, :].astype(bf16)
            dwk_ref[...] = acc[half:width, :].astype(bf16)

    block = pl.BlockSpec((rows, width), lambda i, f: (i, 0))
    whole = lambda i, f: (0, 0)
    grid_spec = pltpu.PrefetchScalarGridSpec(
        num_scalar_prefetch=1,
        grid=(steps,),
        in_specs=[
            block,
            block,
            pl.BlockSpec((rows, 1), lambda i, f: (i, 0)),
            pl.BlockSpec((1, width), whole),
            pl.BlockSpec((blocks, ctx, depth, cols), lambda i, f: (0, 0, 0, 4)),
            block,
        ]
        + [ANY] * len(waits),
        out_specs=[
            block,
            block,
            pl.BlockSpec((half, width), whole),
            pl.BlockSpec((half, width), whole),
            pl.BlockSpec((8, width), whole),
        ],
        scratch_shapes=[pltpu.VMEM((width, width), f32)],
    )
    return pl.pallas_call(
        kernel,
        grid_spec=grid_spec,
        out_shape=[
            jax.ShapeDtypeStruct((total, width), f32),
            jax.ShapeDtypeStruct((total, width), bf16),
            jax.ShapeDtypeStruct((half, width), bf16),
            jax.ShapeDtypeStruct((half, width), bf16),
            jax.ShapeDtypeStruct((8, width), f32),
        ],
        compiler_params=params(),
        cost_estimate=cost(4 * total * width * width, total * width * 16 + width * width * 4),
    )(features, grad_hidden, hat, rstd, gain, w_mid, heads, *waits)


def attn_weight_grads(x, grads, features, part, got=None, waits=(), cols=768):
    total, width = x.shape
    count = len(grads)
    slots, three = grads[0].shape
    half = width // 2
    blocks = half // 128

    def kernel(feat_ref, x_ref, *refs):
        out_ref, turned = refs[-2:]

        @pl.when(pl.program_id(0) == 0)
        def _():
            turned[...] = reordered(x_ref, feat_ref, part * blocks, blocks)

        value = sum(mm(turned[:, n * slots : (n + 1) * slots], refs[n][...]) for n in range(count))
        if got is not None:
            value = value + refs[count][...].astype(f32)
        out_ref[...] = value.astype(bf16)

    column = pl.BlockSpec((slots, cols), lambda j, f: (0, j))
    out = pl.BlockSpec((half, cols), lambda j, f: (0, j))
    extra = [] if got is None else [got]
    grid_spec = pltpu.PrefetchScalarGridSpec(
        num_scalar_prefetch=1,
        grid=(three // cols,),
        in_specs=[pl.BlockSpec((total, width), lambda j, f: (0, 0))]
        + [column] * count
        + [out] * len(extra)
        + [ANY] * len(waits),
        out_specs=out,
        scratch_shapes=[pltpu.VMEM((half, total), bf16)],
    )
    return pl.pallas_call(
        kernel,
        grid_spec=grid_spec,
        out_shape=jax.ShapeDtypeStruct((half, three), bf16),
        compiler_params=params(),
        cost_estimate=cost(total * width * three, 2 * (total * width + total * three + width * three)),
    )(features, x, *grads, *extra, *waits)


def token_grads(grad_qkv, w_attn, grad_one, seq, waits=(), rows=256):
    slots, three = grad_qkv.shape
    width = grad_one.shape[1]
    steps = slots // rows

    def kernel(g_ref, w_ref, one_ref, *refs):
        refs[-1][...] = (mm_nt(g_ref[...], w_ref[...]) + one_ref[...]).astype(bf16)

    return pl.pallas_call(
        kernel,
        grid=(steps,),
        in_specs=[
            pl.BlockSpec((rows, three), lambda i: (i, 0)),
            pl.BlockSpec((width, three), lambda i: (0, 0)),
            pl.BlockSpec((rows, width), lambda i: (seq * steps + i, 0)),
        ]
        + [ANY] * len(waits),
        out_specs=pl.BlockSpec((rows, width), lambda i: (i, 0)),
        out_shape=jax.ShapeDtypeStruct((slots, width), bf16),
        compiler_params=params(),
        cost_estimate=cost(2 * slots * three * width, 2 * (slots * three + width * three) + slots * width * 6),
    )(grad_qkv, w_attn, grad_one, *waits)


def swap(array, axis, size, mask):
    return lax.ppermute(array, axis, [(i, i ^ mask) for i in range(size)])


def shift(array, axis, size, by):
    return lax.ppermute(array, axis, [(i, (i + by) % size) for i in range(size)])


def after(array, *earlier):
    return lax.optimization_barrier((array, *earlier))[0]


def after_all(array, earlier):
    return after(array, *earlier) if earlier else array


class Columns:
    def __init__(self, shard, c):
        self.c, self.shard = c, shard

    def first(self):
        self.near = swap(self.shard, "ctx", 4, 1)
        return self.near

    def second(self):
        odd = (self.c & 1) == 1
        self.pair = jnp.stack(
            [jnp.where(odd, self.near, self.shard), jnp.where(odd, self.shard, self.near)]
        )
        self.across = lax.ppermute(self.pair, "ctx", [(1, 2), (2, 1)])
        return self.across

    def third(self):
        self.outwards = lax.ppermute(self.across, "ctx", [(1, 0), (2, 3)])
        return self.outwards

    def pieces(self):
        middle = (self.c == 1) | (self.c == 2)
        other = jnp.where(middle, self.across, self.outwards)
        upper = self.c >= 2
        return jnp.concatenate([jnp.where(upper, other, self.pair), jnp.where(upper, self.pair, other)])


def gather_rows(block, r, dp):
    if dp != 8:
        return lax.all_gather(block, "dp", axis=0, tiled=True), ()
    rows, width = block.shape
    half = rows // 2
    by_x = swap(block, "dp", dp, 2)
    by_y = swap(block, "dp", dp, 4)
    far_top = swap(by_x[:half], "dp", dp, 4)
    far_low = swap(by_y[half:], "dp", dp, 2)
    own = [block, by_x, by_y, far_top, far_low]
    twin = [swap(part, "dp", dp, 1) for part in own]

    def at(offset, count):
        return lambda out, start: out.at[pl.ds(pl.multiple_of(start + offset, half), count), :]

    puts = []
    for n, base in ((0, 0), (5, 1)):
        puts += [
            (n, base, at(0, rows)),
            (n + 1, base ^ 2, at(0, rows)),
            (n + 2, base ^ 4, at(0, rows)),
            (n + 3, base ^ 6, at(0, half)),
            (n + 4, base ^ 6, at(half, half)),
        ]
    starts = jnp.stack([(r ^ m) * rows for m in range(8)]).astype(jnp.int32)
    shape = jax.ShapeDtypeStruct((dp * rows, width), block.dtype)
    return place(own + twin, starts, shape, puts), (by_x, by_y)


class Exchange:
    def __init__(self, array, c, ctx, gather):
        self.c, self.ctx, self.gather = c, ctx, gather
        if gather:
            seqs, self.count, self.width = array.shape
            self.per = seqs // ctx
        else:
            self.per, total, self.width = array.shape
            self.count = total // ctx
        self.dtype = array.dtype
        self.parts = [self.piece(array, (c + d) % ctx) for d in range(ctx)]
        self.pieces = tuple(self.parts)

    def piece(self, array, index):
        start = (index * self.per, 0, 0) if self.gather else (0, index * self.count, 0)
        return lax.dynamic_slice(array, start, (self.per, self.count, self.width))

    def send(self, *which):
        for d in which or range(1, self.ctx):
            self.parts[d] = shift(self.parts[d], "ctx", self.ctx, d)
        return self.parts

    def arrive(self, *earlier):
        self.parts = list(lax.optimization_barrier((*self.parts, *earlier))[: self.ctx])

    def placed(self):
        step = self.count if self.gather else self.per
        starts = jnp.stack([((self.c - d) % self.ctx) * step for d in range(self.ctx)]).astype(jnp.int32)
        if self.gather:
            at = lambda out, start: out.at[:, pl.ds(pl.multiple_of(start, step), step), :]
            shape = (self.per, self.ctx * self.count, self.width)
        else:
            at = lambda out, start: out.at[pl.ds(start, step), :, :]
            shape = (self.per * self.ctx, self.count, self.width)
        return place(self.parts, starts, jax.ShapeDtypeStruct(shape, self.dtype), [(d, d, at) for d in range(self.ctx)])


class RowSum:
    def __init__(self, parts, r, dp):
        self.parts, self.dp = parts, dp
        self.y, self.x = (r >> 2) & 1, (r >> 1) & 1
        self.widths = [kept.shape[-1] for _, kept in parts]

    def pick(self, array, yi, xi, h):
        _, rows, width = array.shape
        array = array.reshape(2, 2, 2, rows // 2, width)
        start = (0 if yi is None else yi, 0 if xi is None else xi, h, 0, 0)
        sizes = (2 if yi is None else 1, 2 if xi is None else 1, 1, rows // 2, width)
        out = lax.dynamic_slice(array, tuple(jnp.int32(s) for s in start), sizes)
        return out.reshape(sizes[0] * sizes[1], rows // 2, width).astype(f32)

    def summed(self, yi, xi, h):
        return [
            self.pick(kept, yi, xi, h) if got is None else self.pick(got, yi, xi, h) + self.pick(kept, yi, xi, h)
            for got, kept in self.parts
        ]

    def pack(self, arrays):
        return jnp.concatenate([a.astype(bf16) for a in arrays], axis=-1)

    def plus(self, arrays, packed, index=None):
        if index is not None:
            packed = lax.dynamic_slice_in_dim(packed, index, 1, axis=0)
        out, at = [], 0
        for array, width in zip(arrays, self.widths):
            out.append(array + lax.slice_in_dim(packed, at, at + width, axis=2).astype(f32))
            at += width
        return out

    def first_sends(self):
        self.sends = (self.pack(self.summed(None, 1 - self.x, 0)), self.pack(self.summed(1 - self.y, None, 1)))
        return self.sends

    def first(self):
        self.got_x = swap(self.sends[0], "dp", self.dp, 2)
        self.got_y = swap(self.sends[1], "dp", self.dp, 4)
        return (self.got_x, self.got_y)

    def first_there(self, *earlier):
        self.got_x, self.got_y = lax.optimization_barrier((self.got_x, self.got_y, *earlier))[:2]

    def second_there(self, *earlier):
        self.top, self.low = lax.optimization_barrier((self.top, self.low, *earlier))[:2]

    def second_sends(self):
        y, x = self.y, self.x
        self.sends = (
            self.pack(self.plus(self.summed(1 - y, x, 0), self.got_x, 1 - y)),
            self.pack(self.plus(self.summed(y, 1 - x, 1), self.got_y, 1 - x)),
        )
        return self.sends

    def second(self):
        self.top = swap(self.sends[0], "dp", self.dp, 4)
        self.low = swap(self.sends[1], "dp", self.dp, 2)
        return (self.top, self.low)

    def result(self):
        y, x = self.y, self.x
        top = self.plus(self.plus(self.summed(y, x, 0), self.got_x, y), self.top)
        low = self.plus(self.plus(self.summed(y, x, 1), self.got_y, x), self.low)
        return [jnp.concatenate([a[0], b[0]], axis=0) for a, b in zip(top, low)]


class ColumnSum:
    def __init__(self, blocks, c):
        self.blocks, self.c = blocks, c
        self.sizes = [b.shape[1] // 4 for b in blocks]
        self.pair, self.odd = c >> 1, c & 1

    def pack(self, arrays):
        return jnp.concatenate([a.astype(bf16) for a in arrays], axis=1)

    def unpack(self, array, times):
        pieces, at = [], 0
        for size in self.sizes:
            pieces.append(array[:, at : at + times * size].astype(f32))
            at += times * size
        return pieces

    def columns(self, arrays, index, times):
        return [
            lax.dynamic_slice_in_dim(a, index * times * s, times * s, axis=1) for a, s in zip(arrays, self.sizes)
        ]

    def first_send(self):
        self.other = self.columns(self.blocks, 1 - self.pair, 2)
        self.send = self.pack(self.other)
        return self.send

    def first(self):
        self.got = lax.ppermute(self.send, "ctx", [(0, 1), (3, 2)])
        return self.got

    def there(self, *earlier):
        self.got = after(self.got, *earlier)

    def second_send(self):
        self.send = self.pack([a + b for a, b in zip(self.other, self.unpack(self.got, 2))])
        return self.send

    def second(self):
        self.got = lax.ppermute(self.send, "ctx", [(1, 2), (2, 1)])
        return self.got

    def third_send(self):
        mine = self.columns(self.blocks, self.pair, 2)
        self.mine = [a + b for a, b in zip(mine, self.unpack(self.got, 2))]
        self.send = self.pack(self.columns(self.mine, 1 - self.odd, 1))
        return self.send

    def third(self):
        self.got = swap(self.send, "ctx", 4, 1)
        return self.got

    def result(self):
        return [a + b for a, b in zip(self.columns(self.mine, self.odd, 1), self.unpack(self.got, 1))]

    def whole(self):
        for stage in ("first", "second", "third"):
            getattr(self, stage + "_send")()
            getattr(self, stage)()
        return self.result()


def pair_columns(query, key, value):
    rows, width = query.shape
    pieces = []
    for j in range(width // PAIR):
        pieces += [a[:, j * PAIR : (j + 1) * PAIR] for a in (query, key, value)]
    return jnp.concatenate(pieces, axis=1)


def on_device(
    dp,
    ctx,
    tokens,
    lengths,
    cotangent,
    weight_query,
    weight_key,
    weight_value,
    weight_out,
    weight_inner,
    weight_outer,
    bias_query,
    bias_value,
    bias_out,
    bias_inner,
    bias_outer,
    gain_attn,
    shift_attn,
    gain_ffn,
    shift_ffn,
):
    seq_total, slot_count, width = tokens.shape
    units = bias_inner.shape[0]
    per = seq_total // ctx
    slots = slot_count * ctx
    rows = per * slots
    c = lax.axis_index("ctx")
    r = lax.axis_index("dp")
    core = r & 1
    paired = dp == 8

    own_lengths = lax.dynamic_slice(lengths, (c * per,), (per,))
    attn_shard = pair_columns(weight_query, weight_key, weight_value)
    attn = Columns(attn_shard, c)
    mid = Columns(jnp.concatenate([weight_inner, weight_out], axis=1), c)
    outer = Columns(weight_outer, c)
    attn.first()
    mid.shard = after(mid.shard, attn.near)
    attn.second()
    mid.first()
    attn.across, mid.near, outer.shard = lax.optimization_barrier((attn.across, mid.near, outer.shard))
    attn.third()
    mid.second()
    outer.first()
    attn.outwards, mid.across, outer.near, tokens = lax.optimization_barrier(
        (attn.outwards, mid.across, outer.near, tokens)
    )
    mid.third()
    outer.second()
    x = Exchange(tokens, c, ctx, True)
    x.send(2)
    block = jnp.concatenate([p for p in attn.pieces()], axis=1)
    w_attn, early = gather_rows(block, r, dp)
    x.parts[1], x.parts[3], mid.outwards, outer.across = lax.optimization_barrier(
        (x.parts[1], x.parts[3], mid.outwards, outer.across)
    )
    x.send(1, 3)
    w_mid = lax.all_gather(after_all(mid.pieces(), early), "dp", axis=0)
    outer.across = after(outer.across, x.parts[2])
    outer.third()
    x.arrive(outer.outwards)
    x = x.placed().reshape(rows, width)
    cot = Exchange(after(cotangent, x), c, ctx, True)
    cot.send()

    if paired:
        order_s = (jnp.arange(4) * 2 + (1 - core)).astype(jnp.int32)
        order_k = (jnp.arange(4) * 2 + core).astype(jnp.int32)
    else:
        order_s, order_k = jnp.arange(4, dtype=jnp.int32), jnp.arange(4, 8, dtype=jnp.int32)
    features = jnp.concatenate([order_s, order_k])

    bias_qkv = pair_columns(bias_query[None], jnp.zeros_like(bias_query)[None], bias_value[None])
    qkv = project(x, w_attn, bias_qkv, cot.pieces).reshape(per, slots, 3 * width)
    outer.outwards = after(outer.outwards, qkv)
    w_outer = lax.all_gather(outer.pieces(), "dp", axis=0)
    heads, lse = attention_forward(qkv, own_lengths)
    heads = heads.reshape(rows, width)
    hat_one, rstd_one, hidden_low, hidden_t = out_forward(
        heads, w_mid, x, bias_out[None], gain_attn[None], shift_attn[None], features
    )
    active, slope = ffn_one(hidden_low, w_mid, bias_inner[None])
    cot.arrive(hidden_low)
    cot = cot.placed().reshape(rows, width)
    vectors = jnp.stack([gain_attn, shift_attn, bias_outer, gain_ffn, shift_ffn] + [shift_ffn] * 3)
    mixed, grad_two, grad_outer, sums_two = ffn_two(
        active, w_outer, hat_one, cot, own_lengths, vectors, slots
    )
    mixed = Exchange(mixed.reshape(per, slots, width), c, ctx, False)
    mixed.send()

    def from_twin(sent):
        return swap(sent, "dp", dp, 1) if paired else sent

    def part(got, kept):
        blocks = (4, kept.shape[0] // 4, kept.shape[1])
        return (got.reshape(blocks), kept.reshape(blocks))

    grad_hidden, outer_s, inner_s1, inner_k1, bias_1 = ffn_back(
        grad_outer, grad_two, hidden_t, active, slope, w_outer, w_mid, order_s, mixed.pieces
    )
    got_outer = from_twin(outer_s)
    grad_hidden, outer_k, inner_s2, inner_k2, bias_2 = ffn_back(
        grad_outer, grad_hidden, hidden_t, active, slope, w_outer, w_mid, order_k, (mixed.parts[1],)
    )
    got_inner_1, got_inner_2 = from_twin(inner_s2), from_twin(inner_s1)
    hold = (mixed.parts[3],)
    if paired:
        sum_c = RowSum([part(after(got_outer, outer_k), outer_k)], r, dp)
        hold = (*hold, *sum_c.first_sends())
        sum_c.first()
    grad_one, grad_heads, out_s, out_k, sums_one = out_back(
        grad_hidden, hat_one, rstd_one, gain_attn[None], w_mid, heads, features, waits=hold
    )
    got_out = from_twin(out_s)
    got_inner_1, got_inner_2, out_k = lax.optimization_barrier((got_inner_1, got_inner_2, out_k))
    mixed.arrive(out_k)
    mixed = mixed.placed()
    grad_qkv, sums_qkv, slot_grads = [], [], []
    last = per - 1
    hold = (mixed, got_inner_1, got_inner_2)
    for n in range(per):
        grad, sums = attention_backward(qkv, grad_heads, lse, own_lengths, n, waits=hold)
        grad_qkv.append(grad)
        sums_qkv.append(sums)
        hold = ()
        if paired and n == 0:
            got_out = after(got_out, grad)
            sum_b = RowSum([part(got_inner_1, inner_k1), part(got_inner_2, inner_k2), part(got_out, out_k)], r, dp)
            sum_c.first_there(grad)
            hold = (*sum_c.second_sends(), *sum_b.first_sends())
            sum_c.second()
            sum_b.first()
        if n < last:
            tokens_n = token_grads(grad, w_attn, grad_one, n, waits=hold)
            slot_grads.append(Exchange(tokens_n[None], c, ctx, False))
            hold = slot_grads[-1].pieces
            if paired and n == 0:
                sum_c.second_there(tokens_n)
                hold = (*hold, sum_c.top, sum_c.low)
            slot_grads[-1].send()
    hold = []
    for exchange in slot_grads:
        exchange.arrive(grad_qkv[last])
        hold.append(exchange.placed())
    slot_grads = list(hold)
    if paired:
        cols_c = ColumnSum(sum_c.result(), c)
        sum_b.first_there(grad_qkv[last])
        hold = [*hold, after(cols_c.first_send(), grad_qkv[last]), *sum_b.second_sends()]
        cols_c.first()
        sum_b.second()
    qkv_s = attn_weight_grads(x, grad_qkv, features, 0, waits=hold)
    got_qkv = from_twin(qkv_s)
    hold = []
    if paired:
        cols_c.there(qkv_s)
        hold.append(cols_c.second_send())
        cols_c.second()
    tokens_n = token_grads(grad_qkv[last], w_attn, grad_one, last, waits=hold)
    slots_n = Exchange(tokens_n[None], c, ctx, False)
    slots_n.send()
    if paired:
        sum_b.second_there(tokens_n)
        cols_b = ColumnSum(sum_b.result(), c)
        cols_c.there(tokens_n)
        hold = (cols_b.first_send(), cols_c.third_send(), *slots_n.pieces)
        cols_b.first()
        cols_c.third()
        qkv_k = attn_weight_grads(x, grad_qkv, features, 1, after(got_qkv, tokens_n), hold)
        sum_a = RowSum([(None, qkv_k.reshape(4, qkv_k.shape[0] // 4, qkv_k.shape[1]))], r, dp)
        cols_c.there(qkv_k)
        sends = sum_a.first_sends()
        sum_a.first()
        cols_b.there(*sends)
        cols_b.second_send()
        cols_b.second()
        (sum_outer,) = cols_c.result()
        slots_n.arrive(cols_b.send)
        sum_a.first_there(cols_b.send, *slots_n.parts)
        sends = sum_a.second_sends()
        sum_a.second()
        cols_b.there(*sends)
        cols_b.third_send()
        cols_b.third()
        slots_n.arrive(cols_b.send)
        sum_a.second_there(cols_b.send)
        cols_a = ColumnSum(sum_a.result(), c)
        cols_a.first_send()
        cols_a.first()
    else:
        qkv_k = attn_weight_grads(x, grad_qkv, features, 1)
    slot_grads.append(slots_n.placed())
    grad_tokens = jnp.stack(slot_grads, axis=1)
    grad_tokens = grad_tokens.reshape(seq_total, slot_count, width).astype(f32)

    if paired:
        cols_b.there(cols_a.send)
        inner_1, inner_2, sum_out = cols_b.result()
        cols_a.second_send()
        cols_a.second()
        cols_a.third_send()
        cols_a.third()
        (sum_qkv,) = cols_a.result()
        sum_inner = jnp.where(
            core == 0,
            jnp.concatenate([inner_2, inner_1], axis=1),
            jnp.concatenate([inner_1, inner_2], axis=1),
        )
        b_1, b_2 = bias_1.reshape(4, -1), bias_2.reshape(4, -1)
        bias_units = jnp.where(core == 0, jnp.stack([b_2, b_1], axis=1), jnp.stack([b_1, b_2], axis=1)).reshape(units)
    else:

        def over_dp(*arrays):
            array = jnp.concatenate(arrays, axis=0)
            return lax.psum_scatter(array.astype(f32), "dp", scatter_dimension=0, tiled=True)

        inner_s, inner_k = jnp.concatenate([inner_s1, inner_s2], axis=1), jnp.concatenate([inner_k1, inner_k2], axis=1)
        (sum_outer,) = ColumnSum([over_dp(outer_s, outer_k)], c).whole()
        sum_inner, sum_out = ColumnSum([over_dp(inner_s, inner_k), over_dp(out_s, out_k)], c).whole()
        (sum_qkv,) = ColumnSum([over_dp(qkv_s, qkv_k)], c).whole()
        bias_units = jnp.concatenate([bias_1[0], bias_2[0]])

    own_rows = sum_qkv.shape[0]
    sum_qkv = sum_qkv.reshape(own_rows, -1, 3, PAIR)
    sum_query, sum_key, sum_value = (sum_qkv[:, :, k].reshape(own_rows, -1) for k in range(3))

    sums_qkv = sum(sums_qkv)
    packed = jnp.concatenate(
        [
            sums_qkv[:, 0].reshape(-1),
            sums_qkv[:, 1].reshape(-1),
            sums_one[2],
            bias_units,
            sums_two[2],
            sums_one[0],
            sums_one[1],
            sums_two[0],
            sums_two[1],
        ]
    )
    packed = lax.all_gather(packed.reshape(-1, 128), ("dp", "ctx"))
    if paired:
        packed = after(packed, cols_a.send)
    packed = jnp.sum(packed, axis=0).reshape(-1)
    totals, at = [], 0
    for size in (width, width, width, units, width, width, width, width, width):
        totals.append(packed[at : at + size])
        at += size
    return (mixed, grad_tokens, sum_query, sum_key, sum_value, sum_out, sum_inner, sum_outer, *totals)


def solution(mesh):
    rows = P("dp", "ctx", None)
    matrix = P("dp", "ctx")
    in_specs = (rows, P("dp"), rows) + (matrix,) * 6 + (P(),) * 9
    out_specs = (rows, rows) + (matrix,) * 6 + (P(),) * 9
    step = functools.partial(on_device, mesh.shape["dp"], mesh.shape["ctx"])
    return jax.shard_map(step, mesh=mesh, in_specs=in_specs, out_specs=out_specs, check_vma=False)
```

time: 810 us -> 569 us (0.70)
  waiting for transfers between devices: 263 us -> 80.1 us
  local copies, waits for them, and re-layouts: 113 us -> 52.4 us
  Pallas kernels: 239 us -> 253 us
  between operations: 2.32 us -> 15.7 us
  matrix products: 11.4 us -> 0 us
  other arithmetic: 60.9 us -> 52.2 us
    ppermute x55 -> x32, waiting for transfers between devices: 109 us -> 27.9 us  [swap(): return lax.ppermute(array, axis, [(i, i ^ mask) for i in range(size)])]
    ppermute x12, waiting for transfers between devices: 74.1 us -> 19.1 us  [the longest x3 18.2 us: third(): self.outwards = lax.ppermute(self.across, 'ctx', [(1, 0), (2, 3)])]
    ppermute x12 -> x15, waiting for transfers between devices: 79.3 us -> 33.2 us  [shift(): lax.ppermute(array, axis, [(i, (i + by) % size) for i in range(size)])]
    unnamed x158 -> x170, local copies, waits for them, and re-layouts: 46.8 us -> 15.6 us
    pallas_call x3 -> x6, Pallas kernels: 33.8 us -> 59.2 us  [the longest x2 18.4 us: attn_weight_grads(): pl.pallas_call(kernel, grid_spec=grid_spec, out_shape=jax.ShapeDtypeStruc...]
    dynamic_slice x9 -> x5, local copies, waits for them, and re-layouts: 33.6 us -> 10 us  [piece(): return lax.dynamic_slice(array, start, (self.per, self.count, self.width))]
    ppermute x12 -> x15, starting transfers between devices: 62.6 us -> 42 us  [shift(): lax.ppermute(array, axis, [(i, (i + by) % size) for i in range(size)])]
    pallas_call x7 -> x6, Pallas kernels: 34.1 us -> 20.9 us  [place(): pl.pallas_call(kernel, grid_spec=pltpu.PrefetchScalarGridSpec(num_scalar_...]
  transfers between devices with their start and end apart: 79 -> 62, of which waited for: 28 -> 13; matrix products, arithmetic and copies ran while one was open for 21% -> 15% of each run, Pallas kernels for 13% -> 42%
where the time goes in v2:
time: 569 us; the launch traced here: 561 us
  Pallas kernels  253 us (44%)
  starting transfers between devices  107 us (19%)
  waiting for transfers between devices  80.1 us (14%)
  local copies, waits for them, and re-layouts  52.4 us (9%)
  other arithmetic  52.2 us (9%)
  between operations  15.7 us (3%)
    pallas_call x2, Pallas kernels, ffn_back(): pl.pallas_call(kernel, grid_spec=grid_spec, out_shape=[jax.ShapeDtypeStru...  54.3 us
    ppermute x32, starting transfers between devices, swap(): return lax.ppermute(array, axis, [(i, i ^ mask) for i in range(size)])  44.9 us
    ppermute x15, starting transfers between devices, shift(): lax.ppermute(array, axis, [(i, (i + by) % size) for i in range(size)])  42 us
    pallas_call x2, Pallas kernels, attention_backward(): pl.pallas_call(kernel, grid_spec=grid_spec, out_shape=[jax.ShapeDtypeStru...  37.1 us
    ppermute x15, waiting for transfers between devices, shift(): lax.ppermute(array, axis, [(i, (i + by) % size) for i in range(size)])  33.2 us
    ppermute x32, waiting for transfers between devices, swap(): return lax.ppermute(array, axis, [(i, i ^ mask) for i in range(size)])  27.9 us
    pallas_call x1, Pallas kernels, ffn_one(): pl.pallas_call(kernel, grid=(width // cols,), in_specs=[pl.BlockSpec((row...  26.5 us
    pallas_call x1, Pallas kernels, attention_forward(): pl.pallas_call(kernel, grid_spec=grid_spec, out_shape=[jax.ShapeDtypeStru...  24.2 us
  transfers between devices with their start and end apart: 62, of which 13 were waited for; matrix products, arithmetic and copies ran while one was open for 15% of the time, Pallas kernels for 42%

profile of v2, /device:TPU:0, one launch (start us, length us, event | category | flops | bytes accessed | tf_op | source)
XLA Modules:
  0.0 560.7 jit_solution(9390145630648247998)
XLA Ops:
  15.0 4.9 collective-permute-done
  26.3 6.6 %collective-permute-done.2 = bf16[128,1280]{1,0:T(8,128)(2,1)S(1)} collective-permute-done((bf16[128,1280]{1,0:T(8,128)(2,1)S(1)}, bf16[128,1280]{1,0:T(8,128)(2,1)S(1)}, u32[]{:S(2)}, u32[]{:S(2)}) %collective-permute-start.2) | collective-permute-done | bytes 327712 | tf_op jit(solution)/shard_map/ppermute | solution.py:585
  38.7 12.5 %collective-permute-done.5 = bf16[512,256]{1,0:T(8,128)(2,1)S(1)} collective-permute-done((bf16[512,256]{1,0:T(8,128)(2,1)S(1)}, bf16[512,256]{1,0:T(8,128)(2,1)S(1)}, u32[]{:S(2)}, u32[]{:S(2)}) %collective-permute-start.5) | collective-permute-done | bytes 262176 | tf_op jit(solution)/shard_map/ppermute | solution.py:585
  59.8 9.9 %collective-permute-done.6 = bf16[2,128,1280]{2,1,0:T(8,128)(2,1)S(1)} collective-permute-done((bf16[2,128,1280]{2,1,0:T(8,128)(2,1)}, bf16[2,128,1280]{2,1,0:T(8,128)(2,1)S(1)}, u32[]{:S(2)}, u32[]{:S(2)}) %collective-permute-start.6) | collective-permute-done | bytes 655392 | tf_op jit(solution)/shard_map/ppermute | solution.py:617
  83.7 25.2 %collective-permute-done.9.refs_2_ = bf16[2,128,1024]{2,1,0:T(8,128)(2,1)} collective-permute-done((bf16[2,128,1024]{2,1,0:T(8,128)(2,1)}, bf16[2,128,1024]{2,1,0:T(8,128)(2,1)}, u32[]{:S(2)}, u32[]{:S(2)}) %collective-permute-start.9) | collective-permute-done | bytes 524320 | tf_op jit(solution)/shard_map/ppermute | solution.py:589
  113.0 8.3 %collective-permute-done.11 = bf16[2,512,256]{2,1,0:T(8,128)(2,1)} collective-permute-done((bf16[2,512,256]{2,1,0:T(8,128)(2,1)S(1)}, bf16[2,512,256]{2,1,0:T(8,128)(2,1)}, u32[]{:S(2)}, u32[]{:S(2)}) %collective-permute-start.11) | collective-permute-done | bytes 524320 | tf_op jit(solution)/shard_map/ppermute | solution.py:617
  130.3 6.1 %shard_map.306.w_ref = bf16[1024,3072]{1,0:T(8,128)(2,1)} custom-call(s32[8]{0:T(128)} %stack.168.starts_ref, bf16[128,3072]{1,0:T(8,128)(2,1)} %copy-done.3, bf16[128,3072]{1,0:T(8,128)(2,1)} %copy-done.14, bf16[128,3072]{1,0:T(8,128)(2,1)} %copy-done.13, bf16[64,3072]{1,0:T(8,128)(2,1)} %collective-permute-done.14.refs_3_, ...), custom_call_target="tpu_custom_call" | custom-call | bytes 150994944 | tf_op jit(solution)/shard_map/pallas_call | solution.py:62
  136.4 10.9 %shard_map.307 = bf16[1024,3072]{1,0:T(8,128)(2,1)} custom-call(bf16[1024,1024]{1,0:T(8,128)(2,1)} %bitcast.287, bf16[1024,3072]{1,0:T(8,128)(2,1)} %shard_map.306.w_ref, f32[1,3072]{1,0:T(1,128)} %copy-done.63, bf16[2,128,1024]{2,1,0:T(8,128)(2,1)} %get-tuple-element.138.refs_0_, bf16[2,128,1024]{2,1,0:T(8,128)(2,1)} %get-tuple-element.275.refs_1_, ...), custom_call_target="tpu_custom_call" | custom-call | flops 77309411328 | bytes 176160768 | tf_op jit(solution)/shard_map/pallas_call | solution.py:198
  150.0 24.2 %shard_map.308 = (bf16[2,512,1024]{2,1,0:T(8,128)(2,1)}, f32[2,8,2,512]{3,2,1,0:T(2,128)}) custom-call(s32[2]{0:T(128)} %dynamic_slice.321.len_ref, bf16[2,512,3072]{2,1,0:T(8,128)(2,1)} %bitcast.366), custom_call_target="tpu_custom_call" | custom-call | flops 103079215104 | bytes 101921584 | tf_op jit(solution)/shard_map/pallas_call | solution.py:115
  174.2 10.1 %shard_map.309 = (f32[1024,1024]{1,0:T(8,128)}, f32[1024,1]{1,0:T(8,128)}, bf16[1024,1024]{1,0:T(8,128)(2,1)}, bf16[1024,1024]{1,0:T(8,128)(2,1)}) custom-call(s32[8]{0:T(128)} %pad_add_fusion.1.feat_ref, bf16[1024,1024]{1,0:T(8,128)(2,1)} %bitcast.369, bf16[8,4,128,1280]{3,2,1,0:T(8,128)(2,1)} %bitcast.340, bf16[1024,1024]{1,0:T(8,128)(2,1)} %bitcast.288, ...), custom_call_target="tpu_custom_call" | custom-call | flops 25769803776 | bytes 176160768 | tf_op jit(solution)/shard_map/pallas_call | solution.py:270
  187.5 26.5 %shard_map.310 = (bf16[1024,4096]{1,0:T(8,128)(2,1)}, bf16[1024,4096]{1,0:T(8,128)(2,1)}) custom-call(bf16[1024,1024]{1,0:T(8,128)(2,1)} %get-tuple-element.134.h_ref, bf16[8,4,128,1280]{3,2,1,0:T(8,128)(2,1)} %bitcast.341, f32[1,4096]{1,0:T(1,128)} %bitcast.348), custom_call_target="tpu_custom_call" | custom-call | flops 103079215104 | bytes 327155712 | tf_op jit(solution)/shard_map/pallas_call | solution.py:313
  213.9 20.1 %shard_map.312 = (bf16[1024,1024]{1,0:T(8,128)(2,1)}, f32[1024,1024]{1,0:T(8,128)}, bf16[1024,1024]{1,0:T(8,128)(2,1)}, f32[8,1024]{1,0:T(8,128)}) custom-call(s32[2]{0:T(128)} %dynamic_slice.321.len_ref, bf16[1024,4096]{1,0:T(8,128)(2,1)} %get-tuple-element.135.a_ref, bf16[8,4,512,256]{3,2,1,0:T(8,128)(2,1)} %bitcast.345, ...), custom_call_target="tpu_custom_call" | custom-call | flops 103079215104 | bytes 377487360 | tf_op jit(solution)/shard_map/pallas_call | solution.py:370
  240.5 27.1 %shard_map.313 = (f32[1024,1024]{1,0:T(8,128)}, bf16[2048,1024]{1,0:T(8,128)(2,1)}, bf16[512,2048]{1,0:T(8,128)(2,1)}, bf16[512,2048]{1,0:T(8,128)(2,1)}, f32[1,2048]{1,0:T(1,128)}) custom-call(s32[4]{0:T(128)} %copy-done.59, bf16[1024,1024]{1,0:T(8,128)(2,1)} %get-tuple-element.143.g_ref, f32[1024,1024]{1,0:T(8,128)} %get-tuple-element.144.start_ref, ...), custom_call_target="tpu_custom_call" | custom-call | flops 206158430208 | bytes 452984832 | tf_op jit(solution)/shard_map/pallas_call | solution.py:434
  274.2 27.2 %shard_map.314 = (f32[1024,1024]{1,0:T(8,128)}, bf16[2048,1024]{1,0:T(8,128)(2,1)}, bf16[512,2048]{1,0:T(8,128)(2,1)}, bf16[512,2048]{1,0:T(8,128)(2,1)}, f32[1,2048]{1,0:T(1,128)}) custom-call(s32[4]{0:T(128)} %copy-done.58, bf16[1024,1024]{1,0:T(8,128)(2,1)} %get-tuple-element.143.g_ref, f32[1024,1024]{1,0:T(8,128)} %get-tuple-element.147.start_ref, ...), custom_call_target="tpu_custom_call" | custom-call | flops 206158430208 | bytes 452984832 | tf_op jit(solution)/shard_map/pallas_call | solution.py:434
  311.0 14.3 %shard_map.315 = (f32[1024,1024]{1,0:T(8,128)}, bf16[1024,1024]{1,0:T(8,128)(2,1)}, bf16[512,1024]{1,0:T(8,128)(2,1)}, bf16[512,1024]{1,0:T(8,128)(2,1)}, f32[8,1024]{1,0:T(8,128)}) custom-call(s32[8]{0:T(128)} %pad_add_fusion.1.feat_ref, f32[1024,1024]{1,0:T(8,128)} %get-tuple-element.150.gh_ref, f32[1024,1024]{1,0:T(8,128)} %get-tuple-element.137.hat_ref, ...), custom_call_target="tpu_custom_call" | custom-call | flops 51539607552 | bytes 251658240 | tf_op jit(solution)/shard_map/pallas_call | solution.py:504
  328.5 18.7 %shard_map.317 = (bf16[512,3072]{1,0:T(8,128)(2,1)}, f32[8,2,128]{2,1,0:T(2,128)}) custom-call(s32[2]{0:T(128)} %dynamic_slice.321.len_ref, bf16[2,512,3072]{2,1,0:T(8,128)(2,1)} %bitcast.367, bf16[1024,1024]{1,0:T(8,128)(2,1)} %get-tuple-element.161.gh_ref, f32[2,8,2,512]{3,2,1,0:T(2,128)} %get-tuple-element.162.lse_ref, ...), custom_call_target="tpu_custom_call" | custom-call | flops 128849018880 | bytes 94371840 | tf_op jit(solution)/shard_map/pallas_call | solution.py:179
  360.9 8.0 %shard_map.318 = bf16[512,1024]{1,0:T(8,128)(2,1)} custom-call(bf16[512,3072]{1,0:T(8,128)(2,1)} %get-tuple-element.165.g_ref.refs_0_, bf16[1024,3072]{1,0:T(8,128)(2,1)} %shard_map.306.w_ref, f32[1024,1024]{1,0:T(8,128)} %get-tuple-element.166.one_ref, bf16[1,256,1024]{2,1,0:T(8,128)(2,1)} %copy-done.33, bf16[1,256,1024]{2,1,0:T(8,128)(2,1)} %copy-done.34, ...), custom_call_target="tpu_custom_call" | custom-call | flops 38654705664 | bytes 150994944 | tf_op jit(solution)/shard_map/pallas_call | solution.py:568
  371.1 13.0 %collective-permute-start.34 = (bf16[1,128,1024]{2,1,0:T(8,128)(2,1)}, bf16[1,128,1024]{2,1,0:T(8,128)(2,1)}, u32[]{:S(2)}, u32[]{:S(2)}) collective-permute-start(bf16[1,128,1024]{2,1,0:T(8,128)(2,1)} %get-tuple-element.292.refs_2_), channel_id=1, source_target_pairs={{0,2},{1,3},{2,0},{3,1},{4,6},{5,7},{6,4},{7,5},{8,10},{9,11},{10,... | collective-permute-start | bytes 786440 | tf_op jit(solution)/shard_map/ppermute | solution.py:589
  386.1 18.4 %shard_map.319 = (bf16[512,3072]{1,0:T(8,128)(2,1)}, f32[8,2,128]{2,1,0:T(2,128)}) custom-call(s32[2]{0:T(128)} %dynamic_slice.321.len_ref, bf16[2,512,3072]{2,1,0:T(8,128)(2,1)} %bitcast.368, bf16[1024,1024]{1,0:T(8,128)(2,1)} %get-tuple-element.161.gh_ref, f32[2,8,2,512]{3,2,1,0:T(2,128)} %get-tuple-element.162.lse_ref, ...), custom_call_target="tpu_custom_call" | custom-call | flops 128849018880 | bytes 94371840 | tf_op jit(solution)/shard_map/pallas_call | solution.py:179
  422.2 8.8 %shard_map.321 = bf16[512,3072]{1,0:T(8,128)(2,1)} custom-call(s32[8]{0:T(128)} %pad_add_fusion.1.feat_ref, bf16[1024,1024]{1,0:T(8,128)(2,1)} %bitcast.289, bf16[512,3072]{1,0:T(8,128)(2,1)} %get-tuple-element.165.g_ref.refs_0_, bf16[512,3072]{1,0:T(8,128)(2,1)} %get-tuple-element.175.refs_1_.g_ref, bf16[4,128,1024]{2,1,0:T(8,128)(2,1)} %shard_map.320.refs_2_, ...), custom_call_target="tpu_custom_call" | custom-call | flops 38654705664 | bytes 176160768 | tf_op jit(solution)/shard_map/pallas_call | solution.py:551
  433.1 8.3 %shard_map.322 = bf16[512,1024]{1,0:T(8,128)(2,1)} custom-call(bf16[512,3072]{1,0:T(8,128)(2,1)} %get-tuple-element.175.refs_1_.g_ref, bf16[1024,3072]{1,0:T(8,128)(2,1)} %shard_map.306.w_ref, f32[1024,1024]{1,0:T(8,128)} %get-tuple-element.166.one_ref, bf16[512,512]{1,0:T(8,128)(2,1)} %copy-done.30), custom_call_target="tpu_custom_call" | custom-call | flops 38654705664 | bytes 150994944 | tf_op jit(solution)/shard_map/pallas_call | solution.py:568
  445.1 11.4 %collective-permute-start.42 = (bf16[1,128,1024]{2,1,0:T(8,128)(2,1)}, bf16[1,128,1024]{2,1,0:T(8,128)(2,1)}, u32[]{:S(2)}, u32[]{:S(2)}) collective-permute-start(bf16[1,128,1024]{2,1,0:T(8,128)(2,1)} %get-tuple-element.288.refs_7_), channel_id=1, source_target_pairs={{0,2},{1,3},{2,0},{3,1},{4,6},{5,7},{6,4},{7,5},{8,10},{9,11},{10,... | collective-permute-start | bytes 786440 | tf_op jit(solution)/shard_map/ppermute | solution.py:589
  466.9 9.6 %shard_map.323 = bf16[512,3072]{1,0:T(8,128)(2,1)} custom-call(s32[8]{0:T(128)} %pad_add_fusion.1.feat_ref, bf16[1024,1024]{1,0:T(8,128)(2,1)} %bitcast.290, bf16[512,3072]{1,0:T(8,128)(2,1)} %get-tuple-element.165.g_ref.refs_0_, bf16[512,3072]{1,0:T(8,128)(2,1)} %get-tuple-element.175.refs_1_.g_ref, bf16[512,3072]{1,0:T(8,128)(2,1)} %collective-permute-done.47.refs_2_, ...), custom_call_target="tpu_custom_call" | custom-call | flops 38654705664 | bytes 176160768 | tf_op jit(solution)/shard_map/pallas_call | solution.py:551
  537.2 10.5 %collective-permute-start.56 = (bf16[128,768]{0,1:T(8,128)(2,1)S(1)}, bf16[128,768]{0,1:T(8,128)(2,1)S(1)}, u32[]{:S(2)}, u32[]{:S(2)}) collective-permute-start(bf16[128,768]{0,1:T(8,128)(2,1)S(1)} %dynamic-slice_convert_fusion.1), channel_id=1, source_target_pairs={{0,1},{1,0},{2,3},{3,2},{4,5},{5,4},{6,7},{7,6},{8,9},{9,8},{10,11... | collective-permute-start | bytes 589832 | tf_op jit(solution)/shard_map/ppermute | solution.py:585
  (389 shorter events, 204.4 us)
Async XLA Ops:
  7.2 167.0 %all-gather.8.cloned.1.call-start = ((), (), s32[]{:S(2)}) async-start(), calls=%async_computation.1 | async-start | bytes 11796480 | tf_op jit(solution)/shard_map/all_gather | solution.py:887
  73.3 140.6 %all-gather.10.cloned.1.call-start = ((), (), s32[]{:S(2)}) async-start(), calls=%async_computation.2 | async-start | bytes 9437184 | tf_op jit(solution)/shard_map/all_gather | solution.py:905
  73.6 35.3 %collective-permute-start.9 = (bf16[2,128,1024]{2,1,0:T(8,128)(2,1)}, bf16[2,128,1024]{2,1,0:T(8,128)(2,1)}, u32[]{:S(2)}, u32[]{:S(2)}) collective-permute-start(bf16[2,128,1024]{2,1,0:T(8,128)(2,1)} %get-tuple-element.277), channel_id=1, source_target_pairs={{0,2},{1,3},{2,0},{3,1},{4,6},{5,7},{6,4},{7,5},{8,10},{9,11},{10,... | collective-permute-start | bytes 1572872 | tf_op jit(solution)/shard_map/ppermute | solution.py:589
  76.3 34.5 %collective-permute-start.8 = (bf16[2,128,1024]{2,1,0:T(8,128)(2,1)}, bf16[2,128,1024]{2,1,0:T(8,128)(2,1)}, u32[]{:S(2)}, u32[]{:S(2)}) collective-permute-start(bf16[2,128,1024]{2,1,0:T(8,128)(2,1)} %get-tuple-element.121), channel_id=1, source_target_pairs={{0,1},{1,2},{2,3},{3,0},{4,5},{5,6},{6,7},{7,4},{8,9},{9,10},{10,1... | collective-permute-start | bytes 1572872 | tf_op jit(solution)/shard_map/ppermute | solution.py:589
  128.0 56.4 %collective-permute-start.23 = (bf16[2,128,1024]{2,1,0:T(8,128)(2,1)}, bf16[2,128,1024]{2,1,0:T(8,128)(2,1)}, u32[]{:S(2)}, u32[]{:S(2)}) collective-permute-start(bf16[2,128,1024]{2,1,0:T(8,128)(2,1)} %get-tuple-element.273.refs_3_), channel_id=1, source_target_pairs={{0,3},{1,0},{2,1},{3,2},{4,7},{5,4},{6,5},{7,6},{8,11},{9,8},{10,9... | collective-permute-start | bytes 1572872 | tf_op jit(solution)/shard_map/ppermute | solution.py:589
  128.0 56.3 %collective-permute-start.22 = (bf16[2,128,1024]{2,1,0:T(8,128)(2,1)}, bf16[2,128,1024]{2,1,0:T(8,128)(2,1)}, u32[]{:S(2)}, u32[]{:S(2)}) collective-permute-start(bf16[2,128,1024]{2,1,0:T(8,128)(2,1)} %get-tuple-element.274.refs_2_), channel_id=1, source_target_pairs={{0,2},{1,3},{2,0},{3,1},{4,6},{5,7},{6,4},{7,5},{8,10},{9,11},{10,... | collective-permute-start | bytes 1572872 | tf_op jit(solution)/shard_map/ppermute | solution.py:589
  128.8 55.5 %collective-permute-start.21 = (bf16[2,128,1024]{2,1,0:T(8,128)(2,1)}, bf16[2,128,1024]{2,1,0:T(8,128)(2,1)}, u32[]{:S(2)}, u32[]{:S(2)}) collective-permute-start(bf16[2,128,1024]{2,1,0:T(8,128)(2,1)} %get-tuple-element.275.refs_1_), channel_id=1, source_target_pairs={{0,1},{1,2},{2,3},{3,0},{4,5},{5,6},{6,7},{7,4},{8,9},{9,10},{10,1... | collective-permute-start | bytes 1572872 | tf_op jit(solution)/shard_map/ppermute | solution.py:589
  149.5 398.2 %all-gather.6.cloned.1.call-start = ((), (), s32[]{:S(2)}) async-start(), calls=%async_computation | async-start | bytes 1622016 | tf_op jit(solution)/shard_map/all_gather | solution.py:1071
  237.0 73.3 %collective-permute-start.26 = (bf16[2,128,1024]{2,1,0:T(8,128)(2,1)}, bf16[2,128,1024]{2,1,0:T(8,128)(2,1)}, u32[]{:S(2)}, u32[]{:S(2)}) collective-permute-start(bf16[2,128,1024]{2,1,0:T(8,128)(2,1)} %get-tuple-element.269.refs_3_), channel_id=1, source_target_pairs={{0,3},{1,0},{2,1},{3,2},{4,7},{5,4},{6,5},{7,6},{8,11},{9,8},{10,9... | collective-permute-start | bytes 1572872 | tf_op jit(solution)/shard_map/ppermute | solution.py:589
  239.1 86.2 %collective-permute-start.25 = (bf16[2,128,1024]{2,1,0:T(8,128)(2,1)}, bf16[2,128,1024]{2,1,0:T(8,128)(2,1)}, u32[]{:S(2)}, u32[]{:S(2)}) collective-permute-start(bf16[2,128,1024]{2,1,0:T(8,128)(2,1)} %get-tuple-element.270.refs_2_), channel_id=1, source_target_pairs={{0,2},{1,3},{2,0},{3,1},{4,6},{5,7},{6,4},{7,5},{8,10},{9,11},{10,... | collective-permute-start | bytes 1572872 | tf_op jit(solution)/shard_map/ppermute | solution.py:589
  239.1 35.2 %collective-permute-start.24 = (bf16[2,128,1024]{2,1,0:T(8,128)(2,1)}, bf16[2,128,1024]{2,1,0:T(8,128)(2,1)}, u32[]{:S(2)}, u32[]{:S(2)}) collective-permute-start(bf16[2,128,1024]{2,1,0:T(8,128)(2,1)} %get-tuple-element.271.refs_1_), channel_id=1, source_target_pairs={{0,1},{1,2},{2,3},{3,0},{4,5},{5,6},{6,7},{7,4},{8,9},{9,10},{10,1... | collective-permute-start | bytes 1572872 | tf_op jit(solution)/shard_map/ppermute | solution.py:589
  267.6 57.6 %collective-permute-start.28 = (bf16[512,2048]{1,0:T(8,128)(2,1)}, bf16[512,2048]{1,0:T(8,128)(2,1)}, u32[]{:S(2)}, u32[]{:S(2)}) collective-permute-start(bf16[512,2048]{1,0:T(8,128)(2,1)} %get-tuple-element.149), channel_id=1, source_target_pairs={{0,4},{4,0},{8,12},{12,8},{16,20},{20,16},{24,28},{28,24},{1,5},{5... | collective-permute-start | bytes 6291464 | tf_op jit(solution)/shard_map/ppermute | solution.py:585
  267.7 35.2 %collective-permute-start.29 = (bf16[2048,1024]{1,0:T(8,128)(2,1)}, bf16[2048,1024]{1,0:T(8,128)(2,1)}, u32[]{:S(2)}, u32[]{:S(2)}) collective-permute-start(bf16[2048,1024]{1,0:T(8,128)(2,1)} %get-tuple-element.152), channel_id=1, source_target_pairs={{0,4},{4,0},{8,12},{12,8},{16,20},{20,16},{24,28},{28,24},{1,5},{5... | collective-permute-start | bytes 12582920 | tf_op jit(solution)/shard_map/ppermute | solution.py:585
  305.8 45.9 %collective-permute-start.30 = (bf16[2,256,1024]{2,1,0:T(8,128)(2,1)}, bf16[2,256,1024]{2,1,0:T(8,128)(2,1)}, u32[]{:S(2)}, u32[]{:S(2)}) collective-permute-start(bf16[2,256,1024]{2,1,0:T(8,128)(2,1)} %fusion.4.refs_1_), channel_id=1, source_target_pairs={{0,8},{4,12},{8,0},{12,4},{16,24},{20,28},{24,16},{28,20},{1,9},{5... | collective-permute-start | bytes 3145736 | tf_op jit(solution)/shard_map/ppermute | solution.py:585
  310.3 41.4 %collective-permute-start.31 = (bf16[2,256,1024]{2,1,0:T(8,128)(2,1)}, bf16[2,256,1024]{2,1,0:T(8,128)(2,1)}, u32[]{:S(2)}, u32[]{:S(2)}) collective-permute-start(bf16[2,256,1024]{2,1,0:T(8,128)(2,1)} %fusion.5.refs_2_), channel_id=1, source_target_pairs={{0,16},{4,20},{8,24},{12,28},{16,0},{20,4},{24,8},{28,12},{1,17},{... | collective-permute-start | bytes 3145736 | tf_op jit(solution)/shard_map/ppermute | solution.py:585
  357.5 58.8 %collective-permute-start.39 = (bf16[2,64,5120]{2,1,0:T(8,128)(2,1)}, bf16[2,64,5120]{2,1,0:T(8,128)(2,1)}, u32[]{:S(2)}, u32[]{:S(2)}) collective-permute-start(bf16[2,64,5120]{2,1,0:T(8,128)(2,1)} %pad_maximum_fusion.1.refs_2_), channel_id=1, source_target_pairs={{0,8},{4,12},{8,0},{12,4},{16,24},{20,28},{24,16},{28,20},{1,9},{5... | collective-permute-start | bytes 3932168 | tf_op jit(solution)/shard_map/ppermute | solution.py:585
  360.2 56.1 %collective-permute-start.40 = (bf16[2,64,5120]{2,1,0:T(8,128)(2,1)}, bf16[2,64,5120]{2,1,0:T(8,128)(2,1)}, u32[]{:S(2)}, u32[]{:S(2)}) collective-permute-start(bf16[2,64,5120]{2,1,0:T(8,128)(2,1)} %pad_maximum_fusion.2.refs_3_), channel_id=1, source_target_pairs={{0,16},{4,20},{8,24},{12,28},{16,0},{20,4},{24,8},{28,12},{1,17},{... | collective-permute-start | bytes 3932168 | tf_op jit(solution)/shard_map/ppermute | solution.py:585
  371.1 38.8 %collective-permute-start.35 = (bf16[1,128,1024]{2,1,0:T(8,128)(2,1)}, bf16[1,128,1024]{2,1,0:T(8,128)(2,1)S(1)}, u32[]{:S(2)}, u32[]{:S(2)}) collective-permute-start(bf16[1,128,1024]{2,1,0:T(8,128)(2,1)} %get-tuple-element.291.refs_3_), channel_id=1, source_target_pairs={{0,3},{1,0},{2,1},{3,2},{4,7},{5,4},{6,5},{7,6},{8,11},{9,8},{10,9... | collective-permute-start | bytes 786440 | tf_op jit(solution)/shard_map/ppermute | solution.py:589
  371.1 42.4 %collective-permute-start.34 = (bf16[1,128,1024]{2,1,0:T(8,128)(2,1)}, bf16[1,128,1024]{2,1,0:T(8,128)(2,1)}, u32[]{:S(2)}, u32[]{:S(2)}) collective-permute-start(bf16[1,128,1024]{2,1,0:T(8,128)(2,1)} %get-tuple-element.292.refs_2_), channel_id=1, source_target_pairs={{0,2},{1,3},{2,0},{3,1},{4,6},{5,7},{6,4},{7,5},{8,10},{9,11},{10,... | collective-permute-start | bytes 786440 | tf_op jit(solution)/shard_map/ppermute | solution.py:589
  419.9 38.7 %collective-permute-start.44 = (bf16[1,64,5120]{2,1,0:T(8,128)(2,1)S(1)}, bf16[1,64,5120]{2,1,0:T(8,128)(2,1)}, u32[]{:S(2)}, u32[]{:S(2)}) collective-permute-start(bf16[1,64,5120]{2,1,0:T(8,128)(2,1)S(1)} %pad_maximum_fusion.6.refs_4_), channel_id=1, source_target_pairs={{0,16},{4,20},{8,24},{12,28},{16,0},{20,4},{24,8},{28,12},{1,17},{... | collective-permute-start | bytes 1966088 | tf_op jit(solution)/shard_map/ppermute | solution.py:585
  421.4 37.2 %collective-permute-start.45 = (bf16[1,64,5120]{2,1,0:T(8,128)(2,1)S(1)}, bf16[1,64,5120]{2,1,0:T(8,128)(2,1)}, u32[]{:S(2)}, u32[]{:S(2)}) collective-permute-start(bf16[1,64,5120]{2,1,0:T(8,128)(2,1)S(1)} %pad_maximum_fusion.7.refs_5_), channel_id=1, source_target_pairs={{0,8},{4,12},{8,0},{12,4},{16,24},{20,28},{24,16},{28,20},{1,9},{5... | collective-permute-start | bytes 1966088 | tf_op jit(solution)/shard_map/ppermute | solution.py:585
  431.0 35.8 %collective-permute-start.47 = (bf16[512,3072]{1,0:T(8,128)(2,1)}, bf16[512,3072]{1,0:T(8,128)(2,1)}, u32[]{:S(2)}, u32[]{:S(2)}) collective-permute-start(bf16[512,3072]{1,0:T(8,128)(2,1)} %shard_map.321), channel_id=1, source_target_pairs={{0,4},{4,0},{8,12},{12,8},{16,20},{20,16},{24,28},{28,24},{1,5},{5... | collective-permute-start | bytes 9437192 | tf_op jit(solution)/shard_map/ppermute | solution.py:585
  443.6 44.5 %collective-permute-start.43 = (bf16[1,128,1024]{2,1,0:T(8,128)(2,1)}, bf16[1,128,1024]{2,1,0:T(8,128)(2,1)}, u32[]{:S(2)}, u32[]{:S(2)}) collective-permute-start(bf16[1,128,1024]{2,1,0:T(8,128)(2,1)} %get-tuple-element.287.refs_8_), channel_id=1, source_target_pairs={{0,3},{1,0},{2,1},{3,2},{4,7},{5,4},{6,5},{7,6},{8,11},{9,8},{10,9... | collective-permute-start | bytes 786440 | tf_op jit(solution)/shard_map/ppermute | solution.py:589
  445.1 44.5 %collective-permute-start.42 = (bf16[1,128,1024]{2,1,0:T(8,128)(2,1)}, bf16[1,128,1024]{2,1,0:T(8,128)(2,1)}, u32[]{:S(2)}, u32[]{:S(2)}) collective-permute-start(bf16[1,128,1024]{2,1,0:T(8,128)(2,1)} %get-tuple-element.288.refs_7_), channel_id=1, source_target_pairs={{0,2},{1,3},{2,0},{3,1},{4,6},{5,7},{6,4},{7,5},{8,10},{9,11},{10,... | collective-permute-start | bytes 786440 | tf_op jit(solution)/shard_map/ppermute | solution.py:589
  (102 other events, 1535.9 us)
Sparse Core Ops, SparseCore 0:
  73.4 65.3 all-gather.7
  149.6 53.4 all-gather.9
  410.0 61.5 all-gather.5

commit v3 on v2

--- a/solution.py
+++ b/solution.py
@@ -294,7 +294,7 @@
     return active, slope
 
 
-def ffn_one(hidden, w_mid, b_inner, cols=512, chunk=256):
+def ffn_one(hidden, w_mid, b_inner, cols=1024, chunk=256):
     rows, depth = hidden.shape
     width = b_inner.shape[1]
     blocks, ctx, deep, _ = w_mid.shape
@@ -930,10 +930,10 @@
     )
     got_outer = from_twin(outer_s)
     grad_hidden, outer_k, inner_s2, inner_k2, bias_2 = ffn_back(
-        grad_outer, grad_hidden, hidden_t, active, slope, w_outer, w_mid, order_k, (mixed.parts[1],)
+        grad_outer, grad_hidden, hidden_t, active, slope, w_outer, w_mid, order_k, (mixed.parts[3],)
     )
     got_inner_1, got_inner_2 = from_twin(inner_s2), from_twin(inner_s1)
-    hold = (mixed.parts[3],)
+    hold = (mixed.parts[1],)
     if paired:
         sum_c = RowSum([part(after(got_outer, outer_k), outer_k)], r, dp)
         hold = (*hold, *sum_c.first_sends())

time: 569 us -> 551 us (0.968)
  starting transfers between devices: 107 us -> 89.1 us
    ppermute x15, starting transfers between devices: 42 us -> 24.4 us  [shift(): lax.ppermute(array, axis, [(i, (i + by) % size) for i in range(size)])]
  transfers between devices with their start and end apart: 62 -> 62, of which waited for: 13 -> 13; matrix products, arithmetic and copies ran while one was open for 15% -> 16% of each run, Pallas kernels for 42% -> 42%
where the time goes in v3:
time: 551 us; the launch traced here: 544 us
  Pallas kernels  251 us (46%)
  starting transfers between devices  89.1 us (16%)
  waiting for transfers between devices  82.7 us (15%)
  local copies, waits for them, and re-layouts  53.1 us (10%)
  other arithmetic  52.2 us (9%)
  between operations  15.7 us (3%)
    pallas_call x2, Pallas kernels, ffn_back(): pl.pallas_call(kernel, grid_spec=grid_spec, out_shape=[jax.ShapeDtypeStru...  54.3 us
    ppermute x32, starting transfers between devices, swap(): return lax.ppermute(array, axis, [(i, i ^ mask) for i in range(size)])  43.8 us
    pallas_call x2, Pallas kernels, attention_backward(): pl.pallas_call(kernel, grid_spec=grid_spec, out_shape=[jax.ShapeDtypeStru...  37.1 us
    ppermute x15, waiting for transfers between devices, shift(): lax.ppermute(array, axis, [(i, (i + by) % size) for i in range(size)])  29.9 us
    ppermute x32, waiting for transfers between devices, swap(): return lax.ppermute(array, axis, [(i, i ^ mask) for i in range(size)])  28.8 us
    ppermute x15, starting transfers between devices, shift(): lax.ppermute(array, axis, [(i, (i + by) % size) for i in range(size)])  24.4 us
    pallas_call x1, Pallas kernels, attention_forward(): pl.pallas_call(kernel, grid_spec=grid_spec, out_shape=[jax.ShapeDtypeStru...  24.2 us
    pallas_call x1, Pallas kernels, ffn_one(): pl.pallas_call(kernel, grid=(width // cols,), in_specs=[pl.BlockSpec((row...  24.1 us
  transfers between devices with their start and end apart: 62, of which 13 were waited for; matrix products, arithmetic and copies ran while one was open for 16% of the time, Pallas kernels for 42%

profile of v3, /device:TPU:0, one launch (start us, length us, event | category | flops | bytes accessed | tf_op | source)
XLA Modules:
  0.0 543.5 jit_solution(11250727462111842483)
XLA Ops:
  15.0 4.9 collective-permute-done
  26.3 6.6 %collective-permute-done.2 = bf16[128,1280]{1,0:T(8,128)(2,1)S(1)} collective-permute-done((bf16[128,1280]{1,0:T(8,128)(2,1)S(1)}, bf16[128,1280]{1,0:T(8,128)(2,1)S(1)}, u32[]{:S(2)}, u32[]{:S(2)}) %collective-permute-start.2) | collective-permute-done | bytes 327712 | tf_op jit(solution)/shard_map/ppermute | solution.py:585
  38.7 12.5 %collective-permute-done.5 = bf16[512,256]{1,0:T(8,128)(2,1)S(1)} collective-permute-done((bf16[512,256]{1,0:T(8,128)(2,1)S(1)}, bf16[512,256]{1,0:T(8,128)(2,1)S(1)}, u32[]{:S(2)}, u32[]{:S(2)}) %collective-permute-start.5) | collective-permute-done | bytes 262176 | tf_op jit(solution)/shard_map/ppermute | solution.py:585
  59.8 9.9 %collective-permute-done.6 = bf16[2,128,1280]{2,1,0:T(8,128)(2,1)S(1)} collective-permute-done((bf16[2,128,1280]{2,1,0:T(8,128)(2,1)}, bf16[2,128,1280]{2,1,0:T(8,128)(2,1)S(1)}, u32[]{:S(2)}, u32[]{:S(2)}) %collective-permute-start.6) | collective-permute-done | bytes 655392 | tf_op jit(solution)/shard_map/ppermute | solution.py:617
  83.7 25.2 %collective-permute-done.9.refs_2_ = bf16[2,128,1024]{2,1,0:T(8,128)(2,1)} collective-permute-done((bf16[2,128,1024]{2,1,0:T(8,128)(2,1)}, bf16[2,128,1024]{2,1,0:T(8,128)(2,1)}, u32[]{:S(2)}, u32[]{:S(2)}) %collective-permute-start.9) | collective-permute-done | bytes 524320 | tf_op jit(solution)/shard_map/ppermute | solution.py:589
  113.1 8.3 %collective-permute-done.11 = bf16[2,512,256]{2,1,0:T(8,128)(2,1)} collective-permute-done((bf16[2,512,256]{2,1,0:T(8,128)(2,1)S(1)}, bf16[2,512,256]{2,1,0:T(8,128)(2,1)}, u32[]{:S(2)}, u32[]{:S(2)}) %collective-permute-start.11) | collective-permute-done | bytes 524320 | tf_op jit(solution)/shard_map/ppermute | solution.py:617
  130.3 6.1 %shard_map.306.w_ref = bf16[1024,3072]{1,0:T(8,128)(2,1)} custom-call(s32[8]{0:T(128)} %stack.168.starts_ref, bf16[128,3072]{1,0:T(8,128)(2,1)} %copy-done.3, bf16[128,3072]{1,0:T(8,128)(2,1)} %copy-done.14, bf16[128,3072]{1,0:T(8,128)(2,1)} %copy-done.13, bf16[64,3072]{1,0:T(8,128)(2,1)} %collective-permute-done.14.refs_3_, ...), custom_call_target="tpu_custom_call" | custom-call | bytes 150994944 | tf_op jit(solution)/shard_map/pallas_call | solution.py:62
  136.4 10.9 %shard_map.307 = bf16[1024,3072]{1,0:T(8,128)(2,1)} custom-call(bf16[1024,1024]{1,0:T(8,128)(2,1)} %bitcast.287, bf16[1024,3072]{1,0:T(8,128)(2,1)} %shard_map.306.w_ref, f32[1,3072]{1,0:T(1,128)} %copy-done.63, bf16[2,128,1024]{2,1,0:T(8,128)(2,1)} %get-tuple-element.138.refs_0_, bf16[2,128,1024]{2,1,0:T(8,128)(2,1)} %get-tuple-element.275.refs_1_, ...), custom_call_target="tpu_custom_call" | custom-call | flops 77309411328 | bytes 176160768 | tf_op jit(solution)/shard_map/pallas_call | solution.py:198
  150.1 24.2 %shard_map.308 = (bf16[2,512,1024]{2,1,0:T(8,128)(2,1)}, f32[2,8,2,512]{3,2,1,0:T(2,128)}) custom-call(s32[2]{0:T(128)} %dynamic_slice.321.len_ref, bf16[2,512,3072]{2,1,0:T(8,128)(2,1)} %bitcast.366), custom_call_target="tpu_custom_call" | custom-call | flops 103079215104 | bytes 101921584 | tf_op jit(solution)/shard_map/pallas_call | solution.py:115
  174.3 10.1 %shard_map.309 = (f32[1024,1024]{1,0:T(8,128)}, f32[1024,1]{1,0:T(8,128)}, bf16[1024,1024]{1,0:T(8,128)(2,1)}, bf16[1024,1024]{1,0:T(8,128)(2,1)}) custom-call(s32[8]{0:T(128)} %pad_add_fusion.1.feat_ref, bf16[1024,1024]{1,0:T(8,128)(2,1)} %bitcast.369, bf16[8,4,128,1280]{3,2,1,0:T(8,128)(2,1)} %bitcast.340, bf16[1024,1024]{1,0:T(8,128)(2,1)} %bitcast.288, ...), custom_call_target="tpu_custom_call" | custom-call | flops 25769803776 | bytes 176160768 | tf_op jit(solution)/shard_map/pallas_call | solution.py:270
  187.5 24.1 %shard_map.310 = (bf16[1024,4096]{1,0:T(8,128)(2,1)}, bf16[1024,4096]{1,0:T(8,128)(2,1)}) custom-call(bf16[1024,1024]{1,0:T(8,128)(2,1)} %get-tuple-element.134.h_ref, bf16[8,4,128,1280]{3,2,1,0:T(8,128)(2,1)} %bitcast.341, f32[1,4096]{1,0:T(1,128)} %bitcast.348), custom_call_target="tpu_custom_call" | custom-call | flops 103079215104 | bytes 327155712 | tf_op jit(solution)/shard_map/pallas_call | solution.py:313
  211.6 20.1 %shard_map.312 = (bf16[1024,1024]{1,0:T(8,128)(2,1)}, f32[1024,1024]{1,0:T(8,128)}, bf16[1024,1024]{1,0:T(8,128)(2,1)}, f32[8,1024]{1,0:T(8,128)}) custom-call(s32[2]{0:T(128)} %dynamic_slice.321.len_ref, bf16[1024,4096]{1,0:T(8,128)(2,1)} %get-tuple-element.135.a_ref, bf16[8,4,512,256]{3,2,1,0:T(8,128)(2,1)} %bitcast.345, ...), custom_call_target="tpu_custom_call" | custom-call | flops 103079215104 | bytes 377487360 | tf_op jit(solution)/shard_map/pallas_call | solution.py:370
  238.1 27.1 %shard_map.313 = (f32[1024,1024]{1,0:T(8,128)}, bf16[2048,1024]{1,0:T(8,128)(2,1)}, bf16[512,2048]{1,0:T(8,128)(2,1)}, bf16[512,2048]{1,0:T(8,128)(2,1)}, f32[1,2048]{1,0:T(1,128)}) custom-call(s32[4]{0:T(128)} %copy-done.59, bf16[1024,1024]{1,0:T(8,128)(2,1)} %get-tuple-element.143.g_ref, f32[1024,1024]{1,0:T(8,128)} %get-tuple-element.144.start_ref, ...), custom_call_target="tpu_custom_call" | custom-call | flops 206158430208 | bytes 452984832 | tf_op jit(solution)/shard_map/pallas_call | solution.py:434
  267.3 27.2 %shard_map.314 = (f32[1024,1024]{1,0:T(8,128)}, bf16[2048,1024]{1,0:T(8,128)(2,1)}, bf16[512,2048]{1,0:T(8,128)(2,1)}, bf16[512,2048]{1,0:T(8,128)(2,1)}, f32[1,2048]{1,0:T(1,128)}) custom-call(s32[4]{0:T(128)} %copy-done.58, bf16[1024,1024]{1,0:T(8,128)(2,1)} %get-tuple-element.143.g_ref, f32[1024,1024]{1,0:T(8,128)} %get-tuple-element.147.start_ref, ...), custom_call_target="tpu_custom_call" | custom-call | flops 206158430208 | bytes 452984832 | tf_op jit(solution)/shard_map/pallas_call | solution.py:434
  304.0 14.3 %shard_map.315 = (f32[1024,1024]{1,0:T(8,128)}, bf16[1024,1024]{1,0:T(8,128)(2,1)}, bf16[512,1024]{1,0:T(8,128)(2,1)}, bf16[512,1024]{1,0:T(8,128)(2,1)}, f32[8,1024]{1,0:T(8,128)}) custom-call(s32[8]{0:T(128)} %pad_add_fusion.1.feat_ref, f32[1024,1024]{1,0:T(8,128)} %get-tuple-element.150.gh_ref, f32[1024,1024]{1,0:T(8,128)} %get-tuple-element.137.hat_ref, ...), custom_call_target="tpu_custom_call" | custom-call | flops 51539607552 | bytes 251658240 | tf_op jit(solution)/shard_map/pallas_call | solution.py:504
  321.6 18.7 %shard_map.317 = (bf16[512,3072]{1,0:T(8,128)(2,1)}, f32[8,2,128]{2,1,0:T(2,128)}) custom-call(s32[2]{0:T(128)} %dynamic_slice.321.len_ref, bf16[2,512,3072]{2,1,0:T(8,128)(2,1)} %bitcast.367, bf16[1024,1024]{1,0:T(8,128)(2,1)} %get-tuple-element.161.gh_ref, f32[2,8,2,512]{3,2,1,0:T(2,128)} %get-tuple-element.162.lse_ref, ...), custom_call_target="tpu_custom_call" | custom-call | flops 128849018880 | bytes 94371840 | tf_op jit(solution)/shard_map/pallas_call | solution.py:179
  353.9 8.0 %shard_map.318 = bf16[512,1024]{1,0:T(8,128)(2,1)} custom-call(bf16[512,3072]{1,0:T(8,128)(2,1)} %get-tuple-element.165.g_ref.refs_0_, bf16[1024,3072]{1,0:T(8,128)(2,1)} %shard_map.306.w_ref, f32[1024,1024]{1,0:T(8,128)} %get-tuple-element.166.one_ref, bf16[1,256,1024]{2,1,0:T(8,128)(2,1)} %copy-done.33, bf16[1,256,1024]{2,1,0:T(8,128)(2,1)} %copy-done.34, ...), custom_call_target="tpu_custom_call" | custom-call | flops 38654705664 | bytes 150994944 | tf_op jit(solution)/shard_map/pallas_call | solution.py:568
  368.6 18.4 %shard_map.319 = (bf16[512,3072]{1,0:T(8,128)(2,1)}, f32[8,2,128]{2,1,0:T(2,128)}) custom-call(s32[2]{0:T(128)} %dynamic_slice.321.len_ref, bf16[2,512,3072]{2,1,0:T(8,128)(2,1)} %bitcast.368, bf16[1024,1024]{1,0:T(8,128)(2,1)} %get-tuple-element.161.gh_ref, f32[2,8,2,512]{3,2,1,0:T(2,128)} %get-tuple-element.162.lse_ref, ...), custom_call_target="tpu_custom_call" | custom-call | flops 128849018880 | bytes 94371840 | tf_op jit(solution)/shard_map/pallas_call | solution.py:179
  405.6 8.8 %shard_map.321 = bf16[512,3072]{1,0:T(8,128)(2,1)} custom-call(s32[8]{0:T(128)} %pad_add_fusion.1.feat_ref, bf16[1024,1024]{1,0:T(8,128)(2,1)} %bitcast.289, bf16[512,3072]{1,0:T(8,128)(2,1)} %get-tuple-element.165.g_ref.refs_0_, bf16[512,3072]{1,0:T(8,128)(2,1)} %get-tuple-element.175.refs_1_.g_ref, bf16[4,128,1024]{2,1,0:T(8,128)(2,1)} %shard_map.320.refs_2_, ...), custom_call_target="tpu_custom_call" | custom-call | flops 38654705664 | bytes 176160768 | tf_op jit(solution)/shard_map/pallas_call | solution.py:551
  416.4 8.3 %shard_map.322 = bf16[512,1024]{1,0:T(8,128)(2,1)} custom-call(bf16[512,3072]{1,0:T(8,128)(2,1)} %get-tuple-element.175.refs_1_.g_ref, bf16[1024,3072]{1,0:T(8,128)(2,1)} %shard_map.306.w_ref, f32[1024,1024]{1,0:T(8,128)} %get-tuple-element.166.one_ref, bf16[512,512]{1,0:T(8,128)(2,1)} %copy-done.30), custom_call_target="tpu_custom_call" | custom-call | flops 38654705664 | bytes 150994944 | tf_op jit(solution)/shard_map/pallas_call | solution.py:568
  443.8 9.7 %shard_map.323 = bf16[512,3072]{1,0:T(8,128)(2,1)} custom-call(s32[8]{0:T(128)} %pad_add_fusion.1.feat_ref, bf16[1024,1024]{1,0:T(8,128)(2,1)} %bitcast.290, bf16[512,3072]{1,0:T(8,128)(2,1)} %get-tuple-element.165.g_ref.refs_0_, bf16[512,3072]{1,0:T(8,128)(2,1)} %get-tuple-element.175.refs_1_.g_ref, bf16[512,3072]{1,0:T(8,128)(2,1)} %collective-permute-done.47.refs_2_, ...), custom_call_target="tpu_custom_call" | custom-call | flops 38654705664 | bytes 176160768 | tf_op jit(solution)/shard_map/pallas_call | solution.py:551
  458.9 5.6 %collective-permute-done.46 = bf16[128,2560]{1,0:T(8,128)(2,1)S(1)} collective-permute-done((bf16[128,2560]{1,0:T(8,128)(2,1)S(1)}, bf16[128,2560]{1,0:T(8,128)(2,1)S(1)}, u32[]{:S(2)}, u32[]{:S(2)}) %collective-permute-start.46) | collective-permute-done | bytes 655392 | tf_op jit(solution)/shard_map/ppermute | solution.py:787
  470.6 4.7 collective-permute-done.41.refs_1_
  519.3 11.3 %collective-permute-start.56 = (bf16[128,768]{0,1:T(8,128)(2,1)S(1)}, bf16[128,768]{0,1:T(8,128)(2,1)S(1)}, u32[]{:S(2)}, u32[]{:S(2)}) collective-permute-start(bf16[128,768]{0,1:T(8,128)(2,1)S(1)} %dynamic-slice_convert_fusion.1), channel_id=1, source_target_pairs={{0,1},{1,0},{2,3},{3,2},{4,5},{5,4},{6,7},{7,6},{8,9},{9,8},{10,11... | collective-permute-start | bytes 589832 | tf_op jit(solution)/shard_map/ppermute | solution.py:585
  (389 shorter events, 203.0 us)
Async XLA Ops:
  7.2 167.1 %all-gather.8.cloned.1.call-start = ((), (), s32[]{:S(2)}) async-start(), calls=%async_computation.1 | async-start | bytes 11796480 | tf_op jit(solution)/shard_map/all_gather | solution.py:887
  73.3 138.3 %all-gather.10.cloned.1.call-start = ((), (), s32[]{:S(2)}) async-start(), calls=%async_computation.2 | async-start | bytes 9437184 | tf_op jit(solution)/shard_map/all_gather | solution.py:905
  73.6 35.3 %collective-permute-start.9 = (bf16[2,128,1024]{2,1,0:T(8,128)(2,1)}, bf16[2,128,1024]{2,1,0:T(8,128)(2,1)}, u32[]{:S(2)}, u32[]{:S(2)}) collective-permute-start(bf16[2,128,1024]{2,1,0:T(8,128)(2,1)} %get-tuple-element.277), channel_id=1, source_target_pairs={{0,2},{1,3},{2,0},{3,1},{4,6},{5,7},{6,4},{7,5},{8,10},{9,11},{10,... | collective-permute-start | bytes 1572872 | tf_op jit(solution)/shard_map/ppermute | solution.py:589
  76.3 34.5 %collective-permute-start.8 = (bf16[2,128,1024]{2,1,0:T(8,128)(2,1)}, bf16[2,128,1024]{2,1,0:T(8,128)(2,1)}, u32[]{:S(2)}, u32[]{:S(2)}) collective-permute-start(bf16[2,128,1024]{2,1,0:T(8,128)(2,1)} %get-tuple-element.121), channel_id=1, source_target_pairs={{0,1},{1,2},{2,3},{3,0},{4,5},{5,6},{6,7},{7,4},{8,9},{9,10},{10,1... | collective-permute-start | bytes 1572872 | tf_op jit(solution)/shard_map/ppermute | solution.py:589
  77.0 33.2 %collective-permute-start.15 = (bf16[64,3072]{1,0:T(8,128)(2,1)}, bf16[64,3072]{1,0:T(8,128)(2,1)}, u32[]{:S(2)}, u32[]{:S(2)}) collective-permute-start(bf16[64,3072]{1,0:T(8,128)(2,1)} %slice.321), channel_id=1, source_target_pairs={{0,8},{4,12},{8,0},{12,4},{16,24},{20,28},{24,16},{28,20},{1,9},{5... | collective-permute-start | bytes 1179656 | tf_op jit(solution)/shard_map/ppermute | solution.py:585
  79.3 31.0 %collective-permute-start.14 = (bf16[64,3072]{1,0:T(8,128)(2,1)}, bf16[64,3072]{1,0:T(8,128)(2,1)}, u32[]{:S(2)}, u32[]{:S(2)}) collective-permute-start(bf16[64,3072]{1,0:T(8,128)(2,1)} %slice.320), channel_id=1, source_target_pairs={{0,16},{4,20},{8,24},{12,28},{16,0},{20,4},{24,8},{28,12},{1,17},{... | collective-permute-start | bytes 1179656 | tf_op jit(solution)/shard_map/ppermute | solution.py:585
  79.8 32.8 %collective-permute-start.10 = (bf16[2,128,1024]{2,1,0:T(8,128)(2,1)}, bf16[2,128,1024]{2,1,0:T(8,128)(2,1)}, u32[]{:S(2)}, u32[]{:S(2)}) collective-permute-start(bf16[2,128,1024]{2,1,0:T(8,128)(2,1)} %get-tuple-element.122), channel_id=1, source_target_pairs={{0,3},{1,0},{2,1},{3,2},{4,7},{5,4},{6,5},{7,6},{8,11},{9,8},{10,9... | collective-permute-start | bytes 1572872 | tf_op jit(solution)/shard_map/ppermute | solution.py:589
  128.0 56.4 %collective-permute-start.23 = (bf16[2,128,1024]{2,1,0:T(8,128)(2,1)}, bf16[2,128,1024]{2,1,0:T(8,128)(2,1)}, u32[]{:S(2)}, u32[]{:S(2)}) collective-permute-start(bf16[2,128,1024]{2,1,0:T(8,128)(2,1)} %get-tuple-element.273.refs_3_), channel_id=1, source_target_pairs={{0,3},{1,0},{2,1},{3,2},{4,7},{5,4},{6,5},{7,6},{8,11},{9,8},{10,9... | collective-permute-start | bytes 1572872 | tf_op jit(solution)/shard_map/ppermute | solution.py:589
  128.0 56.4 %collective-permute-start.22 = (bf16[2,128,1024]{2,1,0:T(8,128)(2,1)}, bf16[2,128,1024]{2,1,0:T(8,128)(2,1)}, u32[]{:S(2)}, u32[]{:S(2)}) collective-permute-start(bf16[2,128,1024]{2,1,0:T(8,128)(2,1)} %get-tuple-element.274.refs_2_), channel_id=1, source_target_pairs={{0,2},{1,3},{2,0},{3,1},{4,6},{5,7},{6,4},{7,5},{8,10},{9,11},{10,... | collective-permute-start | bytes 1572872 | tf_op jit(solution)/shard_map/ppermute | solution.py:589
  128.8 55.6 %collective-permute-start.21 = (bf16[2,128,1024]{2,1,0:T(8,128)(2,1)}, bf16[2,128,1024]{2,1,0:T(8,128)(2,1)}, u32[]{:S(2)}, u32[]{:S(2)}) collective-permute-start(bf16[2,128,1024]{2,1,0:T(8,128)(2,1)} %get-tuple-element.275.refs_1_), channel_id=1, source_target_pairs={{0,1},{1,2},{2,3},{3,0},{4,5},{5,6},{6,7},{7,4},{8,9},{9,10},{10,1... | collective-permute-start | bytes 1572872 | tf_op jit(solution)/shard_map/ppermute | solution.py:589
  149.5 381.0 %all-gather.6.cloned.1.call-start = ((), (), s32[]{:S(2)}) async-start(), calls=%async_computation | async-start | bytes 1622016 | tf_op jit(solution)/shard_map/all_gather | solution.py:1071
  234.6 32.7 %collective-permute-start.26 = (bf16[2,128,1024]{2,1,0:T(8,128)(2,1)}, bf16[2,128,1024]{2,1,0:T(8,128)(2,1)}, u32[]{:S(2)}, u32[]{:S(2)}) collective-permute-start(bf16[2,128,1024]{2,1,0:T(8,128)(2,1)} %get-tuple-element.269.refs_3_), channel_id=1, source_target_pairs={{0,3},{1,0},{2,1},{3,2},{4,7},{5,4},{6,5},{7,6},{8,11},{9,8},{10,9... | collective-permute-start | bytes 1572872 | tf_op jit(solution)/shard_map/ppermute | solution.py:589
  236.6 81.7 %collective-permute-start.25 = (bf16[2,128,1024]{2,1,0:T(8,128)(2,1)}, bf16[2,128,1024]{2,1,0:T(8,128)(2,1)}, u32[]{:S(2)}, u32[]{:S(2)}) collective-permute-start(bf16[2,128,1024]{2,1,0:T(8,128)(2,1)} %get-tuple-element.270.refs_2_), channel_id=1, source_target_pairs={{0,2},{1,3},{2,0},{3,1},{4,6},{5,7},{6,4},{7,5},{8,10},{9,11},{10,... | collective-permute-start | bytes 1572872 | tf_op jit(solution)/shard_map/ppermute | solution.py:589
  236.6 66.7 %collective-permute-start.24 = (bf16[2,128,1024]{2,1,0:T(8,128)(2,1)}, bf16[2,128,1024]{2,1,0:T(8,128)(2,1)}, u32[]{:S(2)}, u32[]{:S(2)}) collective-permute-start(bf16[2,128,1024]{2,1,0:T(8,128)(2,1)} %get-tuple-element.271.refs_1_), channel_id=1, source_target_pairs={{0,1},{1,2},{2,3},{3,0},{4,5},{5,6},{6,7},{7,4},{8,9},{9,10},{10,1... | collective-permute-start | bytes 1572872 | tf_op jit(solution)/shard_map/ppermute | solution.py:589
  265.2 53.1 %collective-permute-start.28 = (bf16[512,2048]{1,0:T(8,128)(2,1)}, bf16[512,2048]{1,0:T(8,128)(2,1)}, u32[]{:S(2)}, u32[]{:S(2)}) collective-permute-start(bf16[512,2048]{1,0:T(8,128)(2,1)} %get-tuple-element.149), channel_id=1, source_target_pairs={{0,4},{4,0},{8,12},{12,8},{16,20},{20,16},{24,28},{28,24},{1,5},{5... | collective-permute-start | bytes 6291464 | tf_op jit(solution)/shard_map/ppermute | solution.py:585
  265.3 30.7 %collective-permute-start.29 = (bf16[2048,1024]{1,0:T(8,128)(2,1)}, bf16[2048,1024]{1,0:T(8,128)(2,1)}, u32[]{:S(2)}, u32[]{:S(2)}) collective-permute-start(bf16[2048,1024]{1,0:T(8,128)(2,1)} %get-tuple-element.152), channel_id=1, source_target_pairs={{0,4},{4,0},{8,12},{12,8},{16,20},{20,16},{24,28},{28,24},{1,5},{5... | collective-permute-start | bytes 12582920 | tf_op jit(solution)/shard_map/ppermute | solution.py:585
  298.9 45.8 %collective-permute-start.30 = (bf16[2,256,1024]{2,1,0:T(8,128)(2,1)}, bf16[2,256,1024]{2,1,0:T(8,128)(2,1)}, u32[]{:S(2)}, u32[]{:S(2)}) collective-permute-start(bf16[2,256,1024]{2,1,0:T(8,128)(2,1)} %fusion.4.refs_1_), channel_id=1, source_target_pairs={{0,8},{4,12},{8,0},{12,4},{16,24},{20,28},{24,16},{28,20},{1,9},{5... | collective-permute-start | bytes 3145736 | tf_op jit(solution)/shard_map/ppermute | solution.py:585
  303.4 41.4 %collective-permute-start.31 = (bf16[2,256,1024]{2,1,0:T(8,128)(2,1)}, bf16[2,256,1024]{2,1,0:T(8,128)(2,1)}, u32[]{:S(2)}, u32[]{:S(2)}) collective-permute-start(bf16[2,256,1024]{2,1,0:T(8,128)(2,1)} %fusion.5.refs_2_), channel_id=1, source_target_pairs={{0,16},{4,20},{8,24},{12,28},{16,0},{20,4},{24,8},{28,12},{1,17},{... | collective-permute-start | bytes 3145736 | tf_op jit(solution)/shard_map/ppermute | solution.py:585
  350.6 49.0 %collective-permute-start.39 = (bf16[2,64,5120]{2,1,0:T(8,128)(2,1)}, bf16[2,64,5120]{2,1,0:T(8,128)(2,1)}, u32[]{:S(2)}, u32[]{:S(2)}) collective-permute-start(bf16[2,64,5120]{2,1,0:T(8,128)(2,1)} %pad_maximum_fusion.1.refs_2_), channel_id=1, source_target_pairs={{0,8},{4,12},{8,0},{12,4},{16,24},{20,28},{24,16},{28,20},{1,9},{5... | collective-permute-start | bytes 3932168 | tf_op jit(solution)/shard_map/ppermute | solution.py:585
  353.3 46.4 %collective-permute-start.40 = (bf16[2,64,5120]{2,1,0:T(8,128)(2,1)}, bf16[2,64,5120]{2,1,0:T(8,128)(2,1)}, u32[]{:S(2)}, u32[]{:S(2)}) collective-permute-start(bf16[2,64,5120]{2,1,0:T(8,128)(2,1)} %pad_maximum_fusion.2.refs_3_), channel_id=1, source_target_pairs={{0,16},{4,20},{8,24},{12,28},{16,0},{20,4},{24,8},{28,12},{1,17},{... | collective-permute-start | bytes 3932168 | tf_op jit(solution)/shard_map/ppermute | solution.py:585
  403.2 32.3 %collective-permute-start.44 = (bf16[1,64,5120]{2,1,0:T(8,128)(2,1)S(1)}, bf16[1,64,5120]{2,1,0:T(8,128)(2,1)}, u32[]{:S(2)}, u32[]{:S(2)}) collective-permute-start(bf16[1,64,5120]{2,1,0:T(8,128)(2,1)S(1)} %pad_maximum_fusion.6.refs_4_), channel_id=1, source_target_pairs={{0,16},{4,20},{8,24},{12,28},{16,0},{20,4},{24,8},{28,12},{1,17},{... | collective-permute-start | bytes 1966088 | tf_op jit(solution)/shard_map/ppermute | solution.py:585
  404.7 31.0 %collective-permute-start.45 = (bf16[1,64,5120]{2,1,0:T(8,128)(2,1)S(1)}, bf16[1,64,5120]{2,1,0:T(8,128)(2,1)}, u32[]{:S(2)}, u32[]{:S(2)}) collective-permute-start(bf16[1,64,5120]{2,1,0:T(8,128)(2,1)S(1)} %pad_maximum_fusion.7.refs_5_), channel_id=1, source_target_pairs={{0,8},{4,12},{8,0},{12,4},{16,24},{20,28},{24,16},{28,20},{1,9},{5... | collective-permute-start | bytes 1966088 | tf_op jit(solution)/shard_map/ppermute | solution.py:585
  426.9 42.1 %collective-permute-start.43 = (bf16[1,128,1024]{2,1,0:T(8,128)(2,1)}, bf16[1,128,1024]{2,1,0:T(8,128)(2,1)}, u32[]{:S(2)}, u32[]{:S(2)}) collective-permute-start(bf16[1,128,1024]{2,1,0:T(8,128)(2,1)} %get-tuple-element.287.refs_8_), channel_id=1, source_target_pairs={{0,3},{1,0},{2,1},{3,2},{4,7},{5,4},{6,5},{7,6},{8,11},{9,8},{10,9... | collective-permute-start | bytes 786440 | tf_op jit(solution)/shard_map/ppermute | solution.py:589
  429.4 41.2 %collective-permute-start.42 = (bf16[1,128,1024]{2,1,0:T(8,128)(2,1)}, bf16[1,128,1024]{2,1,0:T(8,128)(2,1)}, u32[]{:S(2)}, u32[]{:S(2)}) collective-permute-start(bf16[1,128,1024]{2,1,0:T(8,128)(2,1)} %get-tuple-element.288.refs_7_), channel_id=1, source_target_pairs={{0,2},{1,3},{2,0},{3,1},{4,6},{5,7},{6,4},{7,5},{8,10},{9,11},{10,... | collective-permute-start | bytes 786440 | tf_op jit(solution)/shard_map/ppermute | solution.py:589
  (102 other events, 1529.3 us)
Sparse Core Ops, SparseCore 0:
  73.4 65.3 all-gather.7
  149.7 53.3 all-gather.9
  392.5 61.4 all-gather.5

commit v4 on v3

--- a/solution.py
+++ b/solution.py
@@ -381,6 +381,19 @@
     )(lengths, active, w_outer, hat_one, cot, vectors)
 
 
+def lay(ref, value):
+    blocks, ctx, parts, rows, cols = ref.shape
+    for c in range(ctx):
+        for k in range(parts):
+            start = (c * parts + k) * cols
+            ref[:, c, k] = value[:, start : start + cols].reshape(blocks, rows, cols)
+
+
+def flat(array):
+    blocks, ctx, parts, rows, cols = array.shape
+    return array.transpose(0, 3, 1, 2, 4).reshape(blocks * rows, ctx * parts * cols)
+
+
 def ffn_back(grad_low, start, hidden_t, active, slope, w_outer, w_mid, order, waits=(), cols=512):
     rows, width = grad_low.shape
     count = order.shape[0]
@@ -399,9 +412,9 @@
         )
         inner = (grad_active * s_ref[...].astype(f32)).astype(bf16)
         bias_ref[...] = jnp.sum(inner.astype(f32), axis=0, keepdims=True)
-        dwo_ref[...] = mm_tn(a_ref[...], grad).astype(bf16)
-        dws_ref[...] = mm(ht_ref[0:half, :], inner).astype(bf16)
-        dwk_ref[...] = mm(ht_ref[half:width, :], inner).astype(bf16)
+        lay(dwo_ref, mm_tn(a_ref[...], grad).astype(bf16))
+        lay(dws_ref, mm(ht_ref[0:half, :], inner).astype(bf16))
+        lay(dwk_ref, mm(ht_ref[half:width, :], inner).astype(bf16))
 
         @pl.when(j == 0)
         def _():
@@ -425,9 +438,9 @@
         + [ANY] * len(waits),
         out_specs=[
             pl.BlockSpec((rows, width), whole),
-            pl.BlockSpec((cols, width), lambda j, o: (j, 0)),
-            pl.BlockSpec((half, cols), lambda j, o: (0, j)),
-            pl.BlockSpec((half, cols), lambda j, o: (0, j)),
+            pl.BlockSpec((1, ctx, 1, cols, outer_cols), lambda j, o: (j, 0, 0, 0, 0)),
+            pl.BlockSpec((4, 1, cols // 256, half // 4, 256), lambda j, o: (0, j, 0, 0, 0)),
+            pl.BlockSpec((4, 1, cols // 256, half // 4, 256), lambda j, o: (0, j, 0, 0, 0)),
             pl.BlockSpec((1, cols), lambda j, o: (0, j)),
         ],
     )
@@ -436,9 +449,9 @@
         grid_spec=grid_spec,
         out_shape=[
             jax.ShapeDtypeStruct((rows, width), f32),
-            jax.ShapeDtypeStruct((count * cols, width), bf16),
-            jax.ShapeDtypeStruct((half, count * cols), bf16),
-            jax.ShapeDtypeStruct((half, count * cols), bf16),
+            jax.ShapeDtypeStruct((count, ctx, 1, cols, outer_cols), bf16),
+            jax.ShapeDtypeStruct((4, count, cols // 256, half // 4, 256), bf16),
+            jax.ShapeDtypeStruct((4, count, cols // 256, half // 4, 256), bf16),
             jax.ShapeDtypeStruct((1, count * cols), f32),
         ],
         compiler_params=params(),
@@ -475,8 +488,8 @@
 
         @pl.when(i == steps - 1)
         def _():
-            dws_ref[...] = acc[0:half, :].astype(bf16)
-            dwk_ref[...] = acc[half:width, :].astype(bf16)
+            lay(dws_ref, acc[0:half, :].astype(bf16))
+            lay(dwk_ref, acc[half:width, :].astype(bf16))
 
     block = pl.BlockSpec((rows, width), lambda i, f: (i, 0))
     whole = lambda i, f: (0, 0)
@@ -495,8 +508,8 @@
         out_specs=[
             block,
             block,
-            pl.BlockSpec((half, width), whole),
-            pl.BlockSpec((half, width), whole),
+            pl.BlockSpec((4, ctx, 1, half // 4, cols), lambda i, f: (0, 0, 0, 0, 0)),
+            pl.BlockSpec((4, ctx, 1, half // 4, cols), lambda i, f: (0, 0, 0, 0, 0)),
             pl.BlockSpec((8, width), whole),
         ],
         scratch_shapes=[pltpu.VMEM((width, width), f32)],
@@ -507,8 +520,8 @@
         out_shape=[
             jax.ShapeDtypeStruct((total, width), f32),
             jax.ShapeDtypeStruct((total, width), bf16),
-            jax.ShapeDtypeStruct((half, width), bf16),
-            jax.ShapeDtypeStruct((half, width), bf16),
+            jax.ShapeDtypeStruct((4, ctx, 1, half // 4, cols), bf16),
+            jax.ShapeDtypeStruct((4, ctx, 1, half // 4, cols), bf16),
             jax.ShapeDtypeStruct((8, width), f32),
         ],
         compiler_params=params(),
@@ -532,11 +545,11 @@
 
         value = sum(mm(turned[:, n * slots : (n + 1) * slots], refs[n][...]) for n in range(count))
         if got is not None:
-            value = value + refs[count][...].astype(f32)
-        out_ref[...] = value.astype(bf16)
+            value = value + refs[count][...].reshape(half, cols).astype(f32)
+        lay(out_ref, value.astype(bf16))
 
     column = pl.BlockSpec((slots, cols), lambda j, f: (0, j))
-    out = pl.BlockSpec((half, cols), lambda j, f: (0, j))
+    out = pl.BlockSpec((4, 1, 1, half // 4, cols), lambda j, f: (0, j, 0, 0, 0))
     extra = [] if got is None else [got]
     grid_spec = pltpu.PrefetchScalarGridSpec(
         num_scalar_prefetch=1,
@@ -551,7 +564,7 @@
     return pl.pallas_call(
         kernel,
         grid_spec=grid_spec,
-        out_shape=jax.ShapeDtypeStruct((half, three), bf16),
+        out_shape=jax.ShapeDtypeStruct((4, three // cols, 1, half // 4, cols), bf16),
         compiler_params=params(),
         cost_estimate=cost(total * width * three, 2 * (total * width + total * three + width * three)),
     )(features, x, *grads, *extra, *waits)
@@ -694,33 +707,29 @@
     def __init__(self, parts, r, dp):
         self.parts, self.dp = parts, dp
         self.y, self.x = (r >> 2) & 1, (r >> 1) & 1
-        self.widths = [kept.shape[-1] for _, kept in parts]
 
     def pick(self, array, yi, xi, h):
-        _, rows, width = array.shape
-        array = array.reshape(2, 2, 2, rows // 2, width)
-        start = (0 if yi is None else yi, 0 if xi is None else xi, h, 0, 0)
-        sizes = (2 if yi is None else 1, 2 if xi is None else 1, 1, rows // 2, width)
+        _, ctx, parts, rows, width = array.shape
+        array = array.reshape(2, 2, 2, ctx // 2, parts, rows, width)
+        start = (0 if yi is None else yi, 0 if xi is None else xi, h, 0, 0, 0, 0)
+        sizes = (2 if yi is None else 1, 2 if xi is None else 1, 1, ctx // 2, parts, rows, width)
         out = lax.dynamic_slice(array, tuple(jnp.int32(s) for s in start), sizes)
-        return out.reshape(sizes[0] * sizes[1], rows // 2, width).astype(f32)
+        return out.reshape(sizes[0] * sizes[1], *sizes[3:]).astype(f32)
 
     def summed(self, yi, xi, h):
-        return [
+        sums = [
             self.pick(kept, yi, xi, h) if got is None else self.pick(got, yi, xi, h) + self.pick(kept, yi, xi, h)
             for got, kept in self.parts
         ]
-
-    def pack(self, arrays):
-        return jnp.concatenate([a.astype(bf16) for a in arrays], axis=-1)
-
-    def plus(self, arrays, packed, index=None):
+        return sums[0] if len(sums) == 1 else jnp.concatenate(sums, axis=2)
+
+    def pack(self, array):
+        return array.astype(bf16)
+
+    def plus(self, array, packed, index=None):
         if index is not None:
             packed = lax.dynamic_slice_in_dim(packed, index, 1, axis=0)
-        out, at = [], 0
-        for array, width in zip(arrays, self.widths):
-            out.append(array + lax.slice_in_dim(packed, at, at + width, axis=2).astype(f32))
-            at += width
-        return out
+        return array + packed.astype(f32)
 
     def first_sends(self):
         self.sends = (self.pack(self.summed(None, 1 - self.x, 0)), self.pack(self.summed(1 - self.y, None, 1)))
@@ -754,33 +763,20 @@
         y, x = self.y, self.x
         top = self.plus(self.plus(self.summed(y, x, 0), self.got_x, y), self.top)
         low = self.plus(self.plus(self.summed(y, x, 1), self.got_y, x), self.low)
-        return [jnp.concatenate([a[0], b[0]], axis=0) for a, b in zip(top, low)]
+        return jnp.concatenate([top[0], low[0]], axis=0)
 
 
 class ColumnSum:
     def __init__(self, blocks, c):
-        self.blocks, self.c = blocks, c
-        self.sizes = [b.shape[1] // 4 for b in blocks]
+        self.blocks = blocks
         self.pair, self.odd = c >> 1, c & 1
 
-    def pack(self, arrays):
-        return jnp.concatenate([a.astype(bf16) for a in arrays], axis=1)
-
-    def unpack(self, array, times):
-        pieces, at = [], 0
-        for size in self.sizes:
-            pieces.append(array[:, at : at + times * size].astype(f32))
-            at += times * size
-        return pieces
-
-    def columns(self, arrays, index, times):
-        return [
-            lax.dynamic_slice_in_dim(a, index * times * s, times * s, axis=1) for a, s in zip(arrays, self.sizes)
-        ]
+    def columns(self, array, index, count):
+        return lax.dynamic_slice_in_dim(array, index * count, count, axis=0)
 
     def first_send(self):
         self.other = self.columns(self.blocks, 1 - self.pair, 2)
-        self.send = self.pack(self.other)
+        self.send = self.other.astype(bf16)
         return self.send
 
     def first(self):
@@ -791,7 +787,7 @@
         self.got = after(self.got, *earlier)
 
     def second_send(self):
-        self.send = self.pack([a + b for a, b in zip(self.other, self.unpack(self.got, 2))])
+        self.send = (self.other + self.got.astype(f32)).astype(bf16)
         return self.send
 
     def second(self):
@@ -799,9 +795,8 @@
         return self.got
 
     def third_send(self):
-        mine = self.columns(self.blocks, self.pair, 2)
-        self.mine = [a + b for a, b in zip(mine, self.unpack(self.got, 2))]
-        self.send = self.pack(self.columns(self.mine, 1 - self.odd, 1))
+        self.mine = self.columns(self.blocks, self.pair, 2) + self.got.astype(f32)
+        self.send = self.columns(self.mine, 1 - self.odd, 1).astype(bf16)
         return self.send
 
     def third(self):
@@ -809,13 +804,17 @@
         return self.got
 
     def result(self):
-        return [a + b for a, b in zip(self.columns(self.mine, self.odd, 1), self.unpack(self.got, 1))]
+        return (self.columns(self.mine, self.odd, 1) + self.got.astype(f32))[0]
 
     def whole(self):
         for stage in ("first", "second", "third"):
             getattr(self, stage + "_send")()
             getattr(self, stage)()
         return self.result()
+
+
+def side_by_side(parts):
+    return jnp.concatenate([parts[k] for k in range(parts.shape[0])], axis=1)
 
 
 def pair_columns(query, key, value):
@@ -922,8 +921,7 @@
         return swap(sent, "dp", dp, 1) if paired else sent
 
     def part(got, kept):
-        blocks = (4, kept.shape[0] // 4, kept.shape[1])
-        return (got.reshape(blocks), kept.reshape(blocks))
+        return (got, kept)
 
     grad_hidden, outer_s, inner_s1, inner_k1, bias_1 = ffn_back(
         grad_outer, grad_two, hidden_t, active, slope, w_outer, w_mid, order_s, mixed.pieces
@@ -990,33 +988,29 @@
     slots_n = Exchange(tokens_n[None], c, ctx, False)
     slots_n.send()
     if paired:
-        sum_b.second_there(tokens_n)
-        cols_b = ColumnSum(sum_b.result(), c)
         cols_c.there(tokens_n)
-        hold = (cols_b.first_send(), cols_c.third_send(), *slots_n.pieces)
-        cols_b.first()
-        cols_c.third()
-        qkv_k = attn_weight_grads(x, grad_qkv, features, 1, after(got_qkv, tokens_n), hold)
-        sum_a = RowSum([(None, qkv_k.reshape(4, qkv_k.shape[0] // 4, qkv_k.shape[1]))], r, dp)
-        cols_c.there(qkv_k)
+        qkv_k = attn_weight_grads(x, grad_qkv, features, 1, after(got_qkv, tokens_n), slots_n.pieces)
+        qkv_k, slots_n.parts[3], sum_b.top, sum_b.low = lax.optimization_barrier(
+            (qkv_k, slots_n.parts[3], sum_b.top, sum_b.low)
+        )
+        sum_a = RowSum([(None, qkv_k)], r, dp)
         sends = sum_a.first_sends()
         sum_a.first()
+        sum_b.second_there(*sends, slots_n.parts[1], slots_n.parts[2])
+        cols_b = ColumnSum(sum_b.result(), c)
+        cols_b.first_send()
+        cols_b.first()
+        sum_a.first_there(cols_b.send)
+        sends = sum_a.second_sends()
+        sum_a.second()
         cols_b.there(*sends)
         cols_b.second_send()
         cols_b.second()
-        (sum_outer,) = cols_c.result()
-        slots_n.arrive(cols_b.send)
-        sum_a.first_there(cols_b.send, *slots_n.parts)
-        sends = sum_a.second_sends()
-        sum_a.second()
-        cols_b.there(*sends)
-        cols_b.third_send()
-        cols_b.third()
-        slots_n.arrive(cols_b.send)
         sum_a.second_there(cols_b.send)
         cols_a = ColumnSum(sum_a.result(), c)
         cols_a.first_send()
         cols_a.first()
+        slots_n.arrive(cols_b.send)
     else:
         qkv_k = attn_weight_grads(x, grad_qkv, features, 1)
     slot_grads.append(slots_n.placed())
@@ -1024,13 +1018,21 @@
     grad_tokens = grad_tokens.reshape(seq_total, slot_count, width).astype(f32)
 
     if paired:
-        cols_b.there(cols_a.send)
-        inner_1, inner_2, sum_out = cols_b.result()
         cols_a.second_send()
         cols_a.second()
         cols_a.third_send()
         cols_a.third()
-        (sum_qkv,) = cols_a.result()
+        cols_b.there(cols_a.send)
+        cols_b.third_send()
+        cols_b.third()
+        cols_c.there(cols_a.send)
+        cols_c.third_send()
+        cols_c.third()
+        cols_b.there(cols_a.send)
+        sum_outer = side_by_side(cols_c.result())
+        rest = cols_b.result()
+        inner_1, inner_2, sum_out = side_by_side(rest[0:2]), side_by_side(rest[2:4]), rest[4]
+        sum_qkv = side_by_side(cols_a.result())
         sum_inner = jnp.where(
             core == 0,
             jnp.concatenate([inner_2, inner_1], axis=1),
@@ -1040,14 +1042,19 @@
         bias_units = jnp.where(core == 0, jnp.stack([b_2, b_1], axis=1), jnp.stack([b_1, b_2], axis=1)).reshape(units)
     else:
 
-        def over_dp(*arrays):
-            array = jnp.concatenate(arrays, axis=0)
-            return lax.psum_scatter(array.astype(f32), "dp", scatter_dimension=0, tiled=True)
-
-        inner_s, inner_k = jnp.concatenate([inner_s1, inner_s2], axis=1), jnp.concatenate([inner_k1, inner_k2], axis=1)
-        (sum_outer,) = ColumnSum([over_dp(outer_s, outer_k)], c).whole()
-        sum_inner, sum_out = ColumnSum([over_dp(inner_s, inner_k), over_dp(out_s, out_k)], c).whole()
-        (sum_qkv,) = ColumnSum([over_dp(qkv_s, qkv_k)], c).whole()
+        def summed(*arrays):
+            array = jnp.concatenate(arrays, axis=0).astype(f32)
+            array = lax.psum_scatter(array, "dp", scatter_dimension=0, tiled=True)
+            array = array.reshape(array.shape[0], ctx, -1).transpose(1, 0, 2)
+            return ColumnSum(array, c).whole()
+
+        sum_outer = summed(flat(outer_s), flat(outer_k))
+        sum_inner = summed(
+            jnp.concatenate([flat(inner_s1), flat(inner_s2)], axis=1),
+            jnp.concatenate([flat(inner_k1), flat(inner_k2)], axis=1),
+        )
+        sum_out = summed(flat(out_s), flat(out_k))
+        sum_qkv = summed(flat(qkv_s), flat(qkv_k))
         bias_units = jnp.concatenate([bias_1[0], bias_2[0]])
 
     own_rows = sum_qkv.shape[0]

time: 551 us -> 554 us (level)
  other arithmetic: 52.2 us -> 58.2 us
  waiting for transfers between devices: 82.7 us -> 88.5 us
    optimization_barrier x4 -> x0, local copies, waits for them, and re-layouts: 7.88 us -> none  [the longest x2 4.33 us: second_there(): lax.optimization_barrier((self.top, self.low, *earlier))[:2]]
    add x8 -> x14, other arithmetic: 6.16 us -> 13 us  [the longest x9 7.88 us: summed(): self.pick(got, yi, xi, h) + self.pick(kept, yi, xi, h)]
    ppermute x15, starting transfers between devices: 24.4 us -> 17.9 us  [shift(): lax.ppermute(array, axis, [(i, (i + by) % size) for i in range(size)])]
    unnamed x170 -> x198, local copies, waits for them, and re-layouts: 16.3 us -> 19.8 us
    convert_element_type x21 -> x13, other arithmetic: 20 us -> 21.1 us  [the longest x7 14.7 us: pack(): return array.astype(bf16)]
  transfers between devices with their start and end apart: 62 -> 62, of which waited for: 13 -> 14; matrix products, arithmetic and copies ran while one was open for 16% -> 16% of each run, Pallas kernels for 42% -> 42%
where the time goes in v4:
time: 554 us; the launch traced here: 546 us
  Pallas kernels  251 us (45%)
  waiting for transfers between devices  88.5 us (16%)
  starting transfers between devices  84.5 us (15%)
  other arithmetic  58.2 us (11%)
  local copies, waits for them, and re-layouts  48.5 us (9%)
  between operations  15.6 us (3%)
    pallas_call x2, Pallas kernels, ffn_back(): pl.pallas_call(kernel, grid_spec=grid_spec, out_shape=[jax.ShapeDtypeStru...  55.1 us
    ppermute x32, starting transfers between devices, swap(): return lax.ppermute(array, axis, [(i, i ^ mask) for i in range(size)])  41.2 us
    pallas_call x2, Pallas kernels, attention_backward(): pl.pallas_call(kernel, grid_spec=grid_spec, out_shape=[jax.ShapeDtypeStru...  37.1 us
    ppermute x15, waiting for transfers between devices, shift(): lax.ppermute(array, axis, [(i, (i + by) % size) for i in range(size)])  33.1 us
    ppermute x32, waiting for transfers between devices, swap(): return lax.ppermute(array, axis, [(i, i ^ mask) for i in range(size)])  32.1 us
    pallas_call x1, Pallas kernels, attention_forward(): pl.pallas_call(kernel, grid_spec=grid_spec, out_shape=[jax.ShapeDtypeStru...  24.2 us
    pallas_call x1, Pallas kernels, ffn_one(): pl.pallas_call(kernel, grid=(width // cols,), in_specs=[pl.BlockSpec((row...  23.9 us
    pallas_call x6, Pallas kernels, place(): pl.pallas_call(kernel, grid_spec=pltpu.PrefetchScalarGridSpec(num_scalar_...  20.8 us
  transfers between devices with their start and end apart: 62, of which 14 were waited for; matrix products, arithmetic and copies ran while one was open for 16% of the time, Pallas kernels for 42%

profile of v4, /device:TPU:0, one launch (start us, length us, event | category | flops | bytes accessed | tf_op | source)
XLA Modules:
  0.0 546.4 jit_solution(10148678405643227837)
XLA Ops:
  25.5 6.6 %collective-permute-done.2 = bf16[128,1280]{1,0:T(8,128)(2,1)S(1)} collective-permute-done((bf16[128,1280]{1,0:T(8,128)(2,1)S(1)}, bf16[128,1280]{1,0:T(8,128)(2,1)S(1)}, u32[]{:S(2)}, u32[]{:S(2)}) %collective-permute-start.2) | collective-permute-done | bytes 327712 | tf_op jit(solution)/shard_map/ppermute | solution.py:598
  38.8 12.5 %collective-permute-done.5 = bf16[512,256]{1,0:T(8,128)(2,1)S(1)} collective-permute-done((bf16[512,256]{1,0:T(8,128)(2,1)S(1)}, bf16[512,256]{1,0:T(8,128)(2,1)S(1)}, u32[]{:S(2)}, u32[]{:S(2)}) %collective-permute-start.5) | collective-permute-done | bytes 262176 | tf_op jit(solution)/shard_map/ppermute | solution.py:598
  59.7 9.9 %collective-permute-done.6 = bf16[2,128,1280]{2,1,0:T(8,128)(2,1)S(1)} collective-permute-done((bf16[2,128,1280]{2,1,0:T(8,128)(2,1)}, bf16[2,128,1280]{2,1,0:T(8,128)(2,1)S(1)}, u32[]{:S(2)}, u32[]{:S(2)}) %collective-permute-start.6) | collective-permute-done | bytes 655392 | tf_op jit(solution)/shard_map/ppermute | solution.py:630
  83.2 25.5 %collective-permute-done.9.refs_2_ = bf16[2,128,1024]{2,1,0:T(8,128)(2,1)} collective-permute-done((bf16[2,128,1024]{2,1,0:T(8,128)(2,1)}, bf16[2,128,1024]{2,1,0:T(8,128)(2,1)}, u32[]{:S(2)}, u32[]{:S(2)}) %collective-permute-start.9) | collective-permute-done | bytes 524320 | tf_op jit(solution)/shard_map/ppermute | solution.py:602
  113.0 8.2 %collective-permute-done.11 = bf16[2,512,256]{2,1,0:T(8,128)(2,1)} collective-permute-done((bf16[2,512,256]{2,1,0:T(8,128)(2,1)S(1)}, bf16[2,512,256]{2,1,0:T(8,128)(2,1)}, u32[]{:S(2)}, u32[]{:S(2)}) %collective-permute-start.11) | collective-permute-done | bytes 524320 | tf_op jit(solution)/shard_map/ppermute | solution.py:630
  130.3 6.1 %shard_map.306.w_ref = bf16[1024,3072]{1,0:T(8,128)(2,1)} custom-call(s32[8]{0:T(128)} %stack.168.starts_ref, bf16[128,3072]{1,0:T(8,128)(2,1)} %copy-done.9, bf16[128,3072]{1,0:T(8,128)(2,1)} %copy-done.28, bf16[128,3072]{1,0:T(8,128)(2,1)} %copy-done.27, bf16[64,3072]{1,0:T(8,128)(2,1)} %collective-permute-done.14.refs_3_, ...), custom_call_target="tpu_custom_call" | custom-call | bytes 150994944 | tf_op jit(solution)/shard_map/pallas_call | solution.py:62
  136.3 10.9 %shard_map.307 = bf16[1024,3072]{1,0:T(8,128)(2,1)} custom-call(bf16[1024,1024]{1,0:T(8,128)(2,1)} %bitcast.274, bf16[1024,3072]{1,0:T(8,128)(2,1)} %shard_map.306.w_ref, f32[1,3072]{1,0:T(1,128)} %copy-done.76, bf16[2,128,1024]{2,1,0:T(8,128)(2,1)} %get-tuple-element.138.refs_0_, bf16[2,128,1024]{2,1,0:T(8,128)(2,1)} %get-tuple-element.275.refs_1_, ...), custom_call_target="tpu_custom_call" | custom-call | flops 77309411328 | bytes 176160768 | tf_op jit(solution)/shard_map/pallas_call | solution.py:198
  150.0 24.2 %shard_map.308 = (bf16[2,512,1024]{2,1,0:T(8,128)(2,1)}, f32[2,8,2,512]{3,2,1,0:T(2,128)}) custom-call(s32[2]{0:T(128)} %dynamic_slice.297.len_ref, bf16[2,512,3072]{2,1,0:T(8,128)(2,1)} %bitcast.352), custom_call_target="tpu_custom_call" | custom-call | flops 103079215104 | bytes 101921584 | tf_op jit(solution)/shard_map/pallas_call | solution.py:115
  174.2 10.1 %shard_map.309 = (f32[1024,1024]{1,0:T(8,128)}, f32[1024,1]{1,0:T(8,128)}, bf16[1024,1024]{1,0:T(8,128)(2,1)}, bf16[1024,1024]{1,0:T(8,128)(2,1)}) custom-call(s32[8]{0:T(128)} %pad_add_fusion.1.feat_ref, bf16[1024,1024]{1,0:T(8,128)(2,1)} %bitcast.355, bf16[8,4,128,1280]{3,2,1,0:T(8,128)(2,1)} %bitcast.326, bf16[1024,1024]{1,0:T(8,128)(2,1)} %bitcast.275, ...), custom_call_target="tpu_custom_call" | custom-call | flops 25769803776 | bytes 176160768 | tf_op jit(solution)/shard_map/pallas_call | solution.py:270
  187.5 23.9 %shard_map.310 = (bf16[1024,4096]{1,0:T(8,128)(2,1)}, bf16[1024,4096]{1,0:T(8,128)(2,1)}) custom-call(bf16[1024,1024]{1,0:T(8,128)(2,1)} %get-tuple-element.134.h_ref, bf16[8,4,128,1280]{3,2,1,0:T(8,128)(2,1)} %bitcast.327, f32[1,4096]{1,0:T(1,128)} %bitcast.334), custom_call_target="tpu_custom_call" | custom-call | flops 103079215104 | bytes 327155712 | tf_op jit(solution)/shard_map/pallas_call | solution.py:313
  211.4 20.1 %shard_map.312 = (bf16[1024,1024]{1,0:T(8,128)(2,1)}, f32[1024,1024]{1,0:T(8,128)}, bf16[1024,1024]{1,0:T(8,128)(2,1)}, f32[8,1024]{1,0:T(8,128)}) custom-call(s32[2]{0:T(128)} %dynamic_slice.297.len_ref, bf16[1024,4096]{1,0:T(8,128)(2,1)} %get-tuple-element.135.a_ref, bf16[8,4,512,256]{3,2,1,0:T(8,128)(2,1)} %bitcast.331, ...), custom_call_target="tpu_custom_call" | custom-call | flops 103079215104 | bytes 377487360 | tf_op jit(solution)/shard_map/pallas_call | solution.py:370
  237.9 27.5 %shard_map.313 = (f32[1024,1024]{1,0:T(8,128)}, bf16[4,4,1,512,256]{4,3,2,1,0:T(8,128)(2,1)}, bf16[4,4,2,128,256]{4,3,2,1,0:T(8,128)(2,1)}, bf16[4,4,2,128,256]{4,3,2,1,0:T(8,128)(2,1)}, f32[1,2048]{1,0:T(1,128)}) custom-call(s32[4]{0:T(128)} %copy-done.72, bf16[1024,1024]{1,0:T(8,128)(2,1)} %get-tuple-element.143.g_ref, ...), custom_call_target="tpu_custom_call" | custom-call | flops 206158430208 | bytes 452984832 | tf_op jit(solution)/shard_map/pallas_call | solution.py:447
  267.5 27.6 %shard_map.314 = (f32[1024,1024]{1,0:T(8,128)}, bf16[4,4,1,512,256]{4,3,2,1,0:T(8,128)(2,1)}, bf16[4,4,2,128,256]{4,3,2,1,0:T(8,128)(2,1)}, bf16[4,4,2,128,256]{4,3,2,1,0:T(8,128)(2,1)}, f32[1,2048]{1,0:T(1,128)}) custom-call(s32[4]{0:T(128)} %copy-done.71, bf16[1024,1024]{1,0:T(8,128)(2,1)} %get-tuple-element.143.g_ref, ...), custom_call_target="tpu_custom_call" | custom-call | flops 206158430208 | bytes 452984832 | tf_op jit(solution)/shard_map/pallas_call | solution.py:447
  304.0 14.3 %shard_map.315 = (f32[1024,1024]{1,0:T(8,128)}, bf16[1024,1024]{1,0:T(8,128)(2,1)}, bf16[4,4,1,128,256]{4,3,2,1,0:T(8,128)(2,1)}, bf16[4,4,1,128,256]{4,3,2,1,0:T(8,128)(2,1)}, f32[8,1024]{1,0:T(8,128)}) custom-call(s32[8]{0:T(128)} %pad_add_fusion.1.feat_ref, f32[1024,1024]{1,0:T(8,128)} %get-tuple-element.150.gh_ref, ...), custom_call_target="tpu_custom_call" | custom-call | flops 51539607552 | bytes 251658240 | tf_op jit(solution)/shard_map/pallas_call | solution.py:517
  322.4 18.7 %shard_map.317 = (bf16[512,3072]{1,0:T(8,128)(2,1)}, f32[8,2,128]{2,1,0:T(2,128)}) custom-call(s32[2]{0:T(128)} %dynamic_slice.297.len_ref, bf16[2,512,3072]{2,1,0:T(8,128)(2,1)} %bitcast.353, bf16[1024,1024]{1,0:T(8,128)(2,1)} %get-tuple-element.161.gh_ref, f32[2,8,2,512]{3,2,1,0:T(2,128)} %get-tuple-element.162.lse_ref, ...), custom_call_target="tpu_custom_call" | custom-call | flops 128849018880 | bytes 94371840 | tf_op jit(solution)/shard_map/pallas_call | solution.py:179
  359.9 8.1 %shard_map.318 = bf16[512,1024]{1,0:T(8,128)(2,1)} custom-call(bf16[512,3072]{1,0:T(8,128)(2,1)} %get-tuple-element.165.g_ref.refs_0_, bf16[1024,3072]{1,0:T(8,128)(2,1)} %shard_map.306.w_ref, f32[1024,1024]{1,0:T(8,128)} %get-tuple-element.166.one_ref, bf16[1,2,1,512,256]{4,3,2,1,0:T(8,128)(2,1)} %bitcast.301, bf16[1,2,1,512,256]{4,3,2,1,0:T(8,128)(2,1)} %bitcast.302, ...), custom_call_target="tpu_custom_call" | custom-call | flops 38654705664 | bytes 150994944 | tf_op jit(solution)/shard_map/pallas_call | solution.py:581
  375.6 18.4 %shard_map.319 = (bf16[512,3072]{1,0:T(8,128)(2,1)}, f32[8,2,128]{2,1,0:T(2,128)}) custom-call(s32[2]{0:T(128)} %dynamic_slice.297.len_ref, bf16[2,512,3072]{2,1,0:T(8,128)(2,1)} %bitcast.354, bf16[1024,1024]{1,0:T(8,128)(2,1)} %get-tuple-element.161.gh_ref, f32[2,8,2,512]{3,2,1,0:T(2,128)} %get-tuple-element.162.lse_ref, ...), custom_call_target="tpu_custom_call" | custom-call | flops 128849018880 | bytes 94371840 | tf_op jit(solution)/shard_map/pallas_call | solution.py:179
  410.6 9.0 %shard_map.321 = bf16[4,4,1,128,768]{4,3,2,1,0:T(8,128)(2,1)} custom-call(s32[8]{0:T(128)} %pad_add_fusion.1.feat_ref, bf16[1024,1024]{1,0:T(8,128)(2,1)} %bitcast.276, bf16[512,3072]{1,0:T(8,128)(2,1)} %get-tuple-element.165.g_ref.refs_0_, bf16[512,3072]{1,0:T(8,128)(2,1)} %get-tuple-element.175.refs_1_.g_ref, bf16[4,128,1024]{2,1,0:T(8,128)(2,1)} %shard_map.320.refs_2_, ...), custom_call_target="tpu_custom_call" | custom-call | flops 38654705664 | bytes 176160768 | tf_op jit(solution)/shard_map/pallas_call | solution.py:564
  420.7 8.1 %shard_map.322 = bf16[512,1024]{1,0:T(8,128)(2,1)} custom-call(bf16[512,3072]{1,0:T(8,128)(2,1)} %get-tuple-element.175.refs_1_.g_ref, bf16[1024,3072]{1,0:T(8,128)(2,1)} %shard_map.306.w_ref, f32[1024,1024]{1,0:T(8,128)} %get-tuple-element.166.one_ref, bf16[2,1,512,256]{3,2,1,0:T(8,128)(2,1)} %add_convert_fusion.3.refs_0_), custom_call_target="tpu_custom_call" | custom-call | flops 38654705664 | bytes 150994944 | tf_op jit(solution)/shard_map/pallas_call | solution.py:581
  433.1 9.4 %shard_map.323 = bf16[4,4,1,128,768]{4,3,2,1,0:T(8,128)(2,1)} custom-call(s32[8]{0:T(128)} %pad_add_fusion.1.feat_ref, bf16[1024,1024]{1,0:T(8,128)(2,1)} %bitcast.277, bf16[512,3072]{1,0:T(8,128)(2,1)} %get-tuple-element.165.g_ref.refs_0_, bf16[512,3072]{1,0:T(8,128)(2,1)} %get-tuple-element.175.refs_1_.g_ref, ...), custom_call_target="tpu_custom_call" | custom-call | flops 38654705664 | bytes 176160768 | tf_op jit(solution)/shard_map/pallas_call | solution.py:564
  449.9 7.5 %collective-permute-done.42.refs_2_ = bf16[1,128,1024]{2,1,0:T(8,128)(2,1)S(1)} collective-permute-done((bf16[1,128,1024]{2,1,0:T(8,128)(2,1)}, bf16[1,128,1024]{2,1,0:T(8,128)(2,1)S(1)}, u32[]{:S(2)}, u32[]{:S(2)}) %collective-permute-start.42) | collective-permute-done | bytes 262176 | tf_op jit(solution)/shard_map/ppermute | solution.py:602
  488.4 5.1 collective-permute-start.52
  495.0 5.2 collective-permute-done.52
  513.3 7.2 %collective-permute-start.54 = (bf16[1,1,128,768]{2,3,1,0:T(8,128)(2,1)}, bf16[1,1,128,768]{2,3,1,0:T(8,128)(2,1)}, u32[]{:S(2)}, u32[]{:S(2)}) collective-permute-start(bf16[1,1,128,768]{2,3,1,0:T(8,128)(2,1)} %dynamic-slice_convert_fusion.2), channel_id=1, source_target_pairs={{0,1},{1,0},{2,3},{3,2},{4,5},{5,4},{6,7},{7,6},{8,9},{9,8},{10,11... | collective-permute-start | bytes 589832 | tf_op jit(solution)/shard_map/ppermute | solution.py:598
  (408 shorter events, 206.8 us)
Async XLA Ops:
  7.2 167.0 %all-gather.8.cloned.1.call-start = ((), (), s32[]{:S(2)}) async-start(), calls=%async_computation.1 | async-start | bytes 11796480 | tf_op jit(solution)/shard_map/all_gather | solution.py:886
  73.2 138.2 %all-gather.10.cloned.1.call-start = ((), (), s32[]{:S(2)}) async-start(), calls=%async_computation.2 | async-start | bytes 9437184 | tf_op jit(solution)/shard_map/all_gather | solution.py:904
  73.5 35.3 %collective-permute-start.9 = (bf16[2,128,1024]{2,1,0:T(8,128)(2,1)}, bf16[2,128,1024]{2,1,0:T(8,128)(2,1)}, u32[]{:S(2)}, u32[]{:S(2)}) collective-permute-start(bf16[2,128,1024]{2,1,0:T(8,128)(2,1)} %get-tuple-element.277), channel_id=1, source_target_pairs={{0,2},{1,3},{2,0},{3,1},{4,6},{5,7},{6,4},{7,5},{8,10},{9,11},{10,... | collective-permute-start | bytes 1572872 | tf_op jit(solution)/shard_map/ppermute | solution.py:602
  75.8 34.9 %collective-permute-start.8 = (bf16[2,128,1024]{2,1,0:T(8,128)(2,1)}, bf16[2,128,1024]{2,1,0:T(8,128)(2,1)}, u32[]{:S(2)}, u32[]{:S(2)}) collective-permute-start(bf16[2,128,1024]{2,1,0:T(8,128)(2,1)} %get-tuple-element.121), channel_id=1, source_target_pairs={{0,1},{1,2},{2,3},{3,0},{4,5},{5,6},{6,7},{7,4},{8,9},{9,10},{10,1... | collective-permute-start | bytes 1572872 | tf_op jit(solution)/shard_map/ppermute | solution.py:602
  76.8 33.3 %collective-permute-start.15 = (bf16[64,3072]{1,0:T(8,128)(2,1)}, bf16[64,3072]{1,0:T(8,128)(2,1)}, u32[]{:S(2)}, u32[]{:S(2)}) collective-permute-start(bf16[64,3072]{1,0:T(8,128)(2,1)} %slice.246), channel_id=1, source_target_pairs={{0,8},{4,12},{8,0},{12,4},{16,24},{20,28},{24,16},{28,20},{1,9},{5... | collective-permute-start | bytes 1179656 | tf_op jit(solution)/shard_map/ppermute | solution.py:598
  79.1 31.1 %collective-permute-start.14 = (bf16[64,3072]{1,0:T(8,128)(2,1)}, bf16[64,3072]{1,0:T(8,128)(2,1)}, u32[]{:S(2)}, u32[]{:S(2)}) collective-permute-start(bf16[64,3072]{1,0:T(8,128)(2,1)} %slice.245), channel_id=1, source_target_pairs={{0,16},{4,20},{8,24},{12,28},{16,0},{20,4},{24,8},{28,12},{1,17},{... | collective-permute-start | bytes 1179656 | tf_op jit(solution)/shard_map/ppermute | solution.py:598
  79.6 33.0 %collective-permute-start.10 = (bf16[2,128,1024]{2,1,0:T(8,128)(2,1)}, bf16[2,128,1024]{2,1,0:T(8,128)(2,1)}, u32[]{:S(2)}, u32[]{:S(2)}) collective-permute-start(bf16[2,128,1024]{2,1,0:T(8,128)(2,1)} %get-tuple-element.122), channel_id=1, source_target_pairs={{0,3},{1,0},{2,1},{3,2},{4,7},{5,4},{6,5},{7,6},{8,11},{9,8},{10,9... | collective-permute-start | bytes 1572872 | tf_op jit(solution)/shard_map/ppermute | solution.py:602
  127.9 56.4 %collective-permute-start.23 = (bf16[2,128,1024]{2,1,0:T(8,128)(2,1)}, bf16[2,128,1024]{2,1,0:T(8,128)(2,1)}, u32[]{:S(2)}, u32[]{:S(2)}) collective-permute-start(bf16[2,128,1024]{2,1,0:T(8,128)(2,1)} %get-tuple-element.273.refs_3_), channel_id=1, source_target_pairs={{0,3},{1,0},{2,1},{3,2},{4,7},{5,4},{6,5},{7,6},{8,11},{9,8},{10,9... | collective-permute-start | bytes 1572872 | tf_op jit(solution)/shard_map/ppermute | solution.py:602
  127.9 56.4 %collective-permute-start.22 = (bf16[2,128,1024]{2,1,0:T(8,128)(2,1)}, bf16[2,128,1024]{2,1,0:T(8,128)(2,1)}, u32[]{:S(2)}, u32[]{:S(2)}) collective-permute-start(bf16[2,128,1024]{2,1,0:T(8,128)(2,1)} %get-tuple-element.274.refs_2_), channel_id=1, source_target_pairs={{0,2},{1,3},{2,0},{3,1},{4,6},{5,7},{6,4},{7,5},{8,10},{9,11},{10,... | collective-permute-start | bytes 1572872 | tf_op jit(solution)/shard_map/ppermute | solution.py:602
  128.8 55.6 %collective-permute-start.21 = (bf16[2,128,1024]{2,1,0:T(8,128)(2,1)}, bf16[2,128,1024]{2,1,0:T(8,128)(2,1)}, u32[]{:S(2)}, u32[]{:S(2)}) collective-permute-start(bf16[2,128,1024]{2,1,0:T(8,128)(2,1)} %get-tuple-element.275.refs_1_), channel_id=1, source_target_pairs={{0,1},{1,2},{2,3},{3,0},{4,5},{5,6},{6,7},{7,4},{8,9},{9,10},{10,1... | collective-permute-start | bytes 1572872 | tf_op jit(solution)/shard_map/ppermute | solution.py:602
  149.5 371.0 %all-gather.6.cloned.1.call-start = ((), (), s32[]{:S(2)}) async-start(), calls=%async_computation | async-start | bytes 1622016 | tf_op jit(solution)/shard_map/all_gather | solution.py:1078
  234.4 33.1 %collective-permute-start.26 = (bf16[2,128,1024]{2,1,0:T(8,128)(2,1)}, bf16[2,128,1024]{2,1,0:T(8,128)(2,1)}, u32[]{:S(2)}, u32[]{:S(2)}) collective-permute-start(bf16[2,128,1024]{2,1,0:T(8,128)(2,1)} %get-tuple-element.269.refs_3_), channel_id=1, source_target_pairs={{0,3},{1,0},{2,1},{3,2},{4,7},{5,4},{6,5},{7,6},{8,11},{9,8},{10,9... | collective-permute-start | bytes 1572872 | tf_op jit(solution)/shard_map/ppermute | solution.py:602
  236.4 81.9 %collective-permute-start.25 = (bf16[2,128,1024]{2,1,0:T(8,128)(2,1)}, bf16[2,128,1024]{2,1,0:T(8,128)(2,1)}, u32[]{:S(2)}, u32[]{:S(2)}) collective-permute-start(bf16[2,128,1024]{2,1,0:T(8,128)(2,1)} %get-tuple-element.270.refs_2_), channel_id=1, source_target_pairs={{0,2},{1,3},{2,0},{3,1},{4,6},{5,7},{6,4},{7,5},{8,10},{9,11},{10,... | collective-permute-start | bytes 1572872 | tf_op jit(solution)/shard_map/ppermute | solution.py:602
  236.4 67.5 %collective-permute-start.24 = (bf16[2,128,1024]{2,1,0:T(8,128)(2,1)}, bf16[2,128,1024]{2,1,0:T(8,128)(2,1)}, u32[]{:S(2)}, u32[]{:S(2)}) collective-permute-start(bf16[2,128,1024]{2,1,0:T(8,128)(2,1)} %get-tuple-element.271.refs_1_), channel_id=1, source_target_pairs={{0,1},{1,2},{2,3},{3,0},{4,5},{5,6},{6,7},{7,4},{8,9},{9,10},{10,1... | collective-permute-start | bytes 1572872 | tf_op jit(solution)/shard_map/ppermute | solution.py:602
  265.4 52.9 %collective-permute-start.28 = (bf16[4,4,2,128,256]{4,3,2,1,0:T(8,128)(2,1)}, bf16[4,4,2,128,256]{4,3,2,1,0:T(8,128)(2,1)}, u32[]{:S(2)}, u32[]{:S(2)}) collective-permute-start(bf16[4,4,2,128,256]{4,3,2,1,0:T(8,128)(2,1)} %get-tuple-element.149), channel_id=1, source_target_pairs={{0,4},{4,0},{8,12},{12,8},{16,20},{20,16},{24,28},{28,24},{1,5},{5... | collective-permute-start | bytes 6291464 | tf_op jit(solution)/shard_map/ppermute | solution.py:598
  265.5 31.1 %collective-permute-start.29 = (bf16[4,4,1,512,256]{4,3,2,1,0:T(8,128)(2,1)}, bf16[4,4,1,512,256]{4,3,2,1,0:T(8,128)(2,1)}, u32[]{:S(2)}, u32[]{:S(2)}) collective-permute-start(bf16[4,4,1,512,256]{4,3,2,1,0:T(8,128)(2,1)} %get-tuple-element.152), channel_id=1, source_target_pairs={{0,4},{4,0},{8,12},{12,8},{16,20},{20,16},{24,28},{28,24},{1,5},{5... | collective-permute-start | bytes 12582920 | tf_op jit(solution)/shard_map/ppermute | solution.py:598
  299.7 51.2 %collective-permute-start.30 = (bf16[2,2,1,512,256]{4,3,1,2,0:T(8,128)(2,1)}, bf16[2,2,1,512,256]{4,3,1,2,0:T(8,128)(2,1)}, u32[]{:S(2)}, u32[]{:S(2)}) collective-permute-start(bf16[2,2,1,512,256]{4,3,1,2,0:T(8,128)(2,1)} %get-tuple-element.251), channel_id=1, source_target_pairs={{0,8},{4,12},{8,0},{12,4},{16,24},{20,28},{24,16},{28,20},{1,9},{5... | collective-permute-start | bytes 3145736 | tf_op jit(solution)/shard_map/ppermute | solution.py:598
  318.4 32.3 %collective-permute-start.32 = (bf16[4,4,1,128,256]{4,3,2,1,0:T(8,128)(2,1)}, bf16[4,4,1,128,256]{4,3,2,1,0:T(8,128)(2,1)S(1)}, u32[]{:S(2)}, u32[]{:S(2)}) collective-permute-start(bf16[4,4,1,128,256]{4,3,2,1,0:T(8,128)(2,1)} %get-tuple-element.171), channel_id=1, source_target_pairs={{0,4},{4,0},{8,12},{12,8},{16,20},{20,16},{24,28},{28,24},{1,5},{5... | collective-permute-start | bytes 3145736 | tf_op jit(solution)/shard_map/ppermute | solution.py:598
  318.6 32.3 %collective-permute-start.31 = (bf16[2,2,1,512,256]{4,3,1,2,0:T(8,128)(2,1)S(1)}, bf16[2,2,1,512,256]{4,3,1,2,0:T(8,128)(2,1)S(1)}, u32[]{:S(2)}, u32[]{:S(2)}) collective-permute-start(bf16[2,2,1,512,256]{4,3,1,2,0:T(8,128)(2,1)S(1)} %get-tuple-element.249), channel_id=1, source_target_pairs={{0,16},{4,20},{8,24},{12,28},{16,0},{20,4},{24,8},{28,12},{1,17},{... | collective-permute-start | bytes 3145736 | tf_op jit(solution)/shard_map/ppermute | solution.py:598
  356.5 49.1 %collective-permute-start.39 = (bf16[2,2,5,128,256]{4,3,2,1,0:T(8,128)(2,1)}, bf16[2,2,5,128,256]{4,3,2,1,0:T(8,128)(2,1)}, u32[]{:S(2)}, u32[]{:S(2)}) collective-permute-start(bf16[2,2,5,128,256]{4,3,2,1,0:T(8,128)(2,1)} %pad_maximum_fusion.1.refs_2_), channel_id=1, source_target_pairs={{0,8},{4,12},{8,0},{12,4},{16,24},{20,28},{24,16},{28,20},{1,9},{5... | collective-permute-start | bytes 3932168 | tf_op jit(solution)/shard_map/ppermute | solution.py:598
  359.3 46.4 %collective-permute-start.40 = (bf16[2,2,5,128,256]{4,3,2,1,0:T(8,128)(2,1)}, bf16[2,2,5,128,256]{4,3,2,1,0:T(8,128)(2,1)}, u32[]{:S(2)}, u32[]{:S(2)}) collective-permute-start(bf16[2,2,5,128,256]{4,3,2,1,0:T(8,128)(2,1)} %pad_maximum_fusion.2.refs_3_), channel_id=1, source_target_pairs={{0,16},{4,20},{8,24},{12,28},{16,0},{20,4},{24,8},{28,12},{1,17},{... | collective-permute-start | bytes 3932168 | tf_op jit(solution)/shard_map/ppermute | solution.py:598
  373.7 29.3 %collective-permute-start.34 = (bf16[1,128,1024]{2,1,0:T(8,128)(2,1)}, bf16[1,128,1024]{2,1,0:T(8,128)(2,1)}, u32[]{:S(2)}, u32[]{:S(2)}) collective-permute-start(bf16[1,128,1024]{2,1,0:T(8,128)(2,1)} %get-tuple-element.292.refs_2_), channel_id=1, source_target_pairs={{0,2},{1,3},{2,0},{3,1},{4,6},{5,7},{6,4},{7,5},{8,10},{9,11},{10,... | collective-permute-start | bytes 786440 | tf_op jit(solution)/shard_map/ppermute | solution.py:602
  407.1 35.4 %collective-permute-start.45 = (bf16[1,2,5,128,256]{4,3,2,1,0:T(8,128)(2,1)S(1)}, bf16[1,2,5,128,256]{4,3,2,1,0:T(8,128)(2,1)S(1)}, u32[]{:S(2)}, u32[]{:S(2)}) collective-permute-start(bf16[1,2,5,128,256]{4,3,2,1,0:T(8,128)(2,1)S(1)} %fusion.3.refs_4_), channel_id=1, source_target_pairs={{0,16},{4,20},{8,24},{12,28},{16,0},{20,4},{24,8},{28,12},{1,17},{... | collective-permute-start | bytes 1966088 | tf_op jit(solution)/shard_map/ppermute | solution.py:598
  409.8 32.8 %collective-permute-start.46 = (bf16[1,2,5,128,256]{4,3,2,1,0:T(8,128)(2,1)S(1)}, bf16[1,2,5,128,256]{4,3,2,1,0:T(8,128)(2,1)S(1)}, u32[]{:S(2)}, u32[]{:S(2)}) collective-permute-start(bf16[1,2,5,128,256]{4,3,2,1,0:T(8,128)(2,1)S(1)} %fusion.4.refs_5_), channel_id=1, source_target_pairs={{0,8},{4,12},{8,0},{12,4},{16,24},{20,28},{24,16},{28,20},{1,9},{5... | collective-permute-start | bytes 1966088 | tf_op jit(solution)/shard_map/ppermute | solution.py:598
  (115 other events, 1620.2 us)
Sparse Core Ops, SparseCore 0:
  73.3 65.0 all-gather.7
  149.6 53.3 all-gather.9
  399.4 67.3 all-gather.5
